TPU v7x, 32 devices: a whole 2x2x4 slice. The times are simulated.
32 devices in a mesh: section: 4 (over x, core), dp: 8 (over z, y).
Axes of the slice: x: 2, y: 2, z: 4, core: 2. Of those that a mesh axis runs over, the one named last changes fastest.
Arguments:
- token_ids: int32 [2, 8, 128], P(None, 'dp'), may hold values from 0 to 14591
- segment_ids: int32 [2, 8, 128], P(None, 'dp'), may hold values from 0 to 3, never falling along the last dimension, each value on 1 to 64 neighbouring positions
- masked_rows: int32 [2, 8, 40], P(None, 'dp'), may hold values from 0 to 127, as said below
- embedding: bfloat16 [14592, 768], P('section'), may hold values from -0.59765625 to 0.59765625
- pos_table: bfloat16 [128, 768], replicated, may hold values from -6 to 6
- w_in: bfloat16 [4, 768, 3072], P('section')
- w_out: bfloat16 [4, 3072, 768], P('section'), may hold values from -0.109375 to 0.109375
- b_in: bfloat16 [4, 3072], P('section'), may hold values from -1.796875 to 1.796875
- b_out: bfloat16 [4, 768], P('section'), may hold values from -1.796875 to 1.796875
- norm_gain: bfloat16 [4, 768], P('section'), may hold values from 0.5 to 1.5
- norm_shift: bfloat16 [4, 768], P('section'), may hold values from -1.796875 to 1.796875
- logit_grad: bfloat16 [2, 8, 40, 14592], P(None, 'dp', None, 'section'), may hold values from -0.5 to 0.5
Outputs:
- logits: float32 [2, 8, 40, 14592], P(None, 'dp', None, 'section')
- table_grad: float32 [14592, 768], P(('section', 'dp'))
- pos_grad: float32 [128, 768], P('dp')
- w_in_grad: float32 [4, 768, 3072], P('section', 'dp')
- w_out_grad: float32 [4, 3072, 768], P('section', 'dp')
- b_in_grad: float32 [4, 3072], P('section', 'dp')
- b_out_grad: float32 [4, 768], P('section', 'dp')
- gain_grad: float32 [4, 768], P('section', 'dp')
- shift_grad: float32 [4, 768], P('section', 'dp')
Inputs may be any that keep to these rules, and one draw needn't show every extreme that they name: `masked_rows`: the 40 positions of one row are different from one another. `segment_ids`: document numbers never fall along a row.
All inputs are finite; a program needn't handle non-finite values.
Results may differ from a plain program's by a relative error of at most 0.025.
Values may be sent and summed in bfloat16 or wider, within the bound.
A program may use at most 256 MiB of HBM per device.

v0:
```python
import jax
import jax.numpy as jnp
from jax import lax
from jax.sharding import PartitionSpec as P

HEADS = 12


EPSILON = 1e-12


def for_sending(array):
    return jax.tree.map(lambda a: a.astype(jnp.bfloat16) if a.dtype == jnp.float32 else a, array)


def passed_along(block, axis, distance):
    devices = range(lax.axis_size(axis))
    route = [(i - distance, i) for i in devices if i - distance in devices]
    return lax.ppermute(block, axis, route)


def broadcast(value, axis, source):
    kept = jnp.where(lax.axis_index(axis) == source, value, 0).astype(value.dtype)
    return lax.psum(kept, axis)


def norm_forward(resid, gain_row, shift_row):
    centre = jnp.mean(resid, -1, keepdims=True)
    centred = resid - centre
    inverse = lax.rsqrt(jnp.mean(centred * centred, -1, keepdims=True) + EPSILON)
    normed = centred * inverse
    return (normed * gain_row + shift_row, normed, inverse)


def norm_backward(upstream, normed, inverse, gain_row):
    gain_part = jnp.sum(upstream * normed, 0)
    shift_part = jnp.sum(upstream, 0)
    scaled = upstream * gain_row
    first_mean = jnp.mean(scaled, -1, keepdims=True)
    second_mean = jnp.mean(scaled * normed, -1, keepdims=True)
    return (inverse * (scaled - first_mean - normed * second_mean), gain_part, shift_part)


def to_heads(values):
    return values.reshape(values.shape[0], HEADS, values.shape[1] // HEADS)


def row_scores(query, keyed, segment):
    factor = (query.shape[1] // HEADS) ** (-0.5)
    scores = (
        jnp.einsum(
            "qhd,khd->hqk", to_heads(query), to_heads(keyed), preferred_element_type=jnp.float32
        )
        * factor
    )
    allowed = segment[:, None] == segment[None, :]
    return jnp.where(allowed[None], scores, -1000000000.0)


def attend_row(packed, segment):
    width = packed.shape[1] // 3
    scores = row_scores(packed[:, :width], packed[:, width : 2 * width], segment)
    row_peak = jnp.max(scores, -1, keepdims=True)
    exponent = jnp.exp(scores - row_peak)
    row_total = jnp.sum(exponent, -1, keepdims=True)
    chance = (exponent / row_total).astype(jnp.bfloat16)
    context = jnp.einsum(
        "hqk,khd->qhd", chance, to_heads(packed[:, 2 * width :]), preferred_element_type=jnp.float32
    )
    summary = (row_peak + jnp.log(row_total))[..., 0]
    return (context.reshape(packed.shape[0], width).astype(jnp.bfloat16), summary)


def attend_back(packed, segment, summary, upstream):
    length = packed.shape[0]
    width = packed.shape[1] // 3
    factor = (width // HEADS) ** (-0.5)
    scores = row_scores(packed[:, :width], packed[:, width : 2 * width], segment)
    chance = jnp.exp(scores - summary[..., None])
    grad_heads = to_heads(upstream)
    grad_chance = jnp.einsum(
        "qhd,khd->hqk",
        grad_heads,
        to_heads(packed[:, 2 * width :]),
        preferred_element_type=jnp.float32,
    )
    grad_value = jnp.einsum(
        "hqk,qhd->khd", chance.astype(jnp.bfloat16), grad_heads, preferred_element_type=jnp.float32
    )
    grad_score = chance * (grad_chance - jnp.sum(chance * grad_chance, -1, keepdims=True))
    grad_score = grad_score.astype(jnp.bfloat16)
    grad_query = (
        jnp.einsum(
            "hqk,khd->qhd",
            grad_score,
            to_heads(packed[:, width : 2 * width]),
            preferred_element_type=jnp.float32,
        )
        * factor
    )
    grad_key = (
        jnp.einsum(
            "hqk,qhd->khd",
            grad_score,
            to_heads(packed[:, :width]),
            preferred_element_type=jnp.float32,
        )
        * factor
    )
    joined = jnp.concatenate(
        [
            grad_query.reshape(length, width),
            grad_key.reshape(length, width),
            grad_value.reshape(length, width),
        ],
        1,
    )
    return joined.astype(jnp.bfloat16)


def attention_forward(inputs, segment, params):
    w_first, w_second, bias_first, bias_second, gain_row, shift_row = params
    rows_here, length, width = inputs.shape
    flat = inputs.reshape(rows_here * length, width)
    offset = jnp.concatenate(
        [bias_first[:width], jnp.zeros((width,), jnp.float32), bias_first[2 * width : 3 * width]]
    )
    packed = jnp.dot(flat, w_first[:, : 3 * width], preferred_element_type=jnp.float32) + offset
    packed = packed.astype(jnp.bfloat16).reshape(rows_here, length, 3 * width)
    context, summary = lax.map(lambda item: attend_row(item[0], item[1]), (packed, segment))
    branch = (
        jnp.dot(
            context.reshape(-1, width), w_first[:, 3 * width :], preferred_element_type=jnp.float32
        )
        + bias_second
    )
    result, normed, inverse = norm_forward(flat.astype(jnp.float32) + branch, gain_row, shift_row)
    return (result.reshape(rows_here, length, width), (packed, context, summary, normed, inverse))


def attention_backward(inputs, segment, upstream, params, totals):
    w_first, w_second, bias_first, bias_second, gain_row, shift_row = params
    rows_here, length, width = inputs.shape
    result, saved = attention_forward(inputs, segment, params)
    packed, context, summary, normed, inverse = saved
    flat = inputs.reshape(-1, width)
    grad_resid, gain_part, shift_part = norm_backward(
        upstream.reshape(-1, width), normed, inverse, gain_row
    )
    grad_branch = grad_resid.astype(jnp.bfloat16)
    grad_out_proj = jnp.einsum(
        "nd,ne->de", context.reshape(-1, width), grad_branch, preferred_element_type=jnp.float32
    )
    bias_second_part = jnp.sum(grad_branch.astype(jnp.float32), 0)
    grad_context = jnp.einsum(
        "ne,de->nd", grad_branch, w_first[:, 3 * width :], preferred_element_type=jnp.float32
    )
    grad_context = grad_context.astype(jnp.bfloat16).reshape(rows_here, length, width)
    grad_packed = lax.map(
        lambda item: attend_back(item[0], item[1], item[2], item[3]),
        (packed, segment, summary, grad_context),
    )
    flat_packed = grad_packed.reshape(-1, 3 * width)
    grad_proj = jnp.einsum("nd,nc->dc", flat, flat_packed, preferred_element_type=jnp.float32)
    bias_sums = jnp.sum(flat_packed.astype(jnp.float32), 0)
    grad_input = grad_resid + jnp.einsum(
        "nc,dc->nd", flat_packed, w_first[:, : 3 * width], preferred_element_type=jnp.float32
    )
    first_total, second_total, bias_first_total, bias_second_total, gain_total, shift_total = totals
    first_total = (
        first_total.at[:, : 3 * width].add(grad_proj).at[:, 3 * width :].add(grad_out_proj)
    )
    bias_first_total = (
        bias_first_total.at[:width]
        .add(bias_sums[:width])
        .at[2 * width : 3 * width]
        .add(bias_sums[2 * width :])
    )
    updated = (
        first_total,
        second_total,
        bias_first_total,
        bias_second_total + bias_second_part,
        gain_total + gain_part,
        shift_total + shift_part,
    )
    return (grad_input.reshape(rows_here, length, width).astype(jnp.bfloat16), updated)


def feed_forward(inputs, params):
    w_first, w_second, bias_first, bias_second, gain_row, shift_row = params
    rows_here, length, width = inputs.shape
    flat = inputs.reshape(-1, width)
    hidden = jnp.dot(flat, w_first, preferred_element_type=jnp.float32) + bias_first
    active = jax.nn.gelu(hidden, approximate=False).astype(jnp.bfloat16)
    branch = jnp.dot(active, w_second, preferred_element_type=jnp.float32) + bias_second
    result, normed, inverse = norm_forward(flat.astype(jnp.float32) + branch, gain_row, shift_row)
    return (result.reshape(rows_here, length, width), (hidden, active, normed, inverse))


def feed_backward(inputs, upstream, params, totals):
    w_first, w_second, bias_first, bias_second, gain_row, shift_row = params
    rows_here, length, width = inputs.shape
    result, saved = feed_forward(inputs, params)
    hidden, active, normed, inverse = saved
    flat = inputs.reshape(-1, width)
    grad_resid, gain_part, shift_part = norm_backward(
        upstream.reshape(-1, width), normed, inverse, gain_row
    )
    grad_branch = grad_resid.astype(jnp.bfloat16)
    grad_second = jnp.einsum("nf,nd->fd", active, grad_branch, preferred_element_type=jnp.float32)
    bias_second_part = jnp.sum(grad_branch.astype(jnp.float32), 0)
    grad_active = jnp.einsum("nd,fd->nf", grad_branch, w_second, preferred_element_type=jnp.float32)
    through = jax.vjp(lambda inner: jax.nn.gelu(inner, approximate=False), hidden)[1](grad_active)[
        0
    ]
    grad_hidden = through.astype(jnp.bfloat16)
    grad_first = jnp.einsum("nd,nf->df", flat, grad_hidden, preferred_element_type=jnp.float32)
    bias_first_part = jnp.sum(grad_hidden.astype(jnp.float32), 0)
    grad_input = grad_resid + jnp.einsum(
        "nf,df->nd", grad_hidden, w_first, preferred_element_type=jnp.float32
    )
    terms = (grad_first, grad_second, bias_first_part, bias_second_part, gain_part, shift_part)
    updated = tuple((total + term for total, term in zip(totals, terms)))
    return (grad_input.reshape(rows_here, length, width).astype(jnp.bfloat16), updated)


def local(
    token_ids,
    segment_ids,
    masked_rows,
    embedding,
    pos_table,
    w_in,
    w_out,
    b_in,
    b_out,
    norm_gain,
    norm_shift,
    logit_grad,
):
    sections = lax.axis_size("section")
    section_index = lax.axis_index("section")
    quarter, width = embedding.shape
    batches, rows_here, length = token_ids.shape
    params = (
        w_in[0],
        w_out[0],
        b_in[0].astype(jnp.float32),
        b_out[0].astype(jnp.float32),
        norm_gain[0].astype(jnp.float32),
        norm_shift[0].astype(jnp.float32),
    )
    local_ids = token_ids - section_index * quarter
    inside = (local_ids >= 0) & (local_ids < quarter)
    picked = jnp.take(embedding, jnp.clip(local_ids, 0, quarter - 1), axis=0)
    partial_rows = jnp.where(inside[..., None], picked.astype(jnp.float32), 0.0)
    looked = lax.psum(partial_rows.astype(jnp.bfloat16), "section").astype(jnp.float32)
    entry = (looked + pos_table.astype(jnp.float32)).astype(jnp.bfloat16)

    def spare_forward(inputs, segment):
        return jnp.zeros(inputs.shape, jnp.bfloat16)

    def attend_forward(inputs, segment):
        return attention_forward(inputs, segment, params)[0].astype(jnp.bfloat16)

    def feed_only(inputs, segment):
        return feed_forward(inputs, params)[0].astype(jnp.bfloat16)

    def spare_backward(inputs, segment, upstream, totals):
        return (jnp.zeros(inputs.shape, jnp.bfloat16), totals)

    def attend_backward(inputs, segment, upstream, totals):
        return attention_backward(inputs, segment, upstream, params, totals)

    def feed_back_only(inputs, segment, upstream, totals):
        return feed_backward(inputs, upstream, params, totals)

    ticks = batches + sections - 1
    kept = jnp.zeros_like(entry)
    outputs = jnp.zeros_like(entry)
    incoming = jnp.zeros_like(entry[0])
    for moment in range(ticks):
        micro_index = moment - section_index
        is_live = (micro_index >= 0) & (micro_index < batches)
        micro_slot = jnp.clip(micro_index, 0, batches - 1)
        current = jnp.where(section_index == 0, entry[micro_slot], incoming)
        kept = kept.at[micro_slot].set(jnp.where(is_live, current, kept[micro_slot]))
        branch_index = jnp.where(is_live, 1 + section_index % 2, 0)
        result = lax.switch(
            branch_index,
            [spare_forward, attend_forward, feed_only],
            current,
            segment_ids[micro_slot],
        )
        outputs = outputs.at[micro_slot].set(jnp.where(is_live, result, outputs[micro_slot]))
        if moment + 1 < ticks:
            incoming = jax.tree.map(
                lambda part, own: part.astype(own.dtype),
                passed_along(for_sending(result), "section", 1),
                result,
            )
    final_rows = jnp.take_along_axis(outputs, masked_rows[..., None], axis=2)
    head_rows = broadcast(final_rows, "section", sections - 1)
    logits = jnp.einsum("mrkd,vd->mrkv", head_rows, embedding, preferred_element_type=jnp.float32)
    partial_grad = jnp.einsum(
        "mrkv,vd->mrkd", logit_grad, embedding, preferred_element_type=jnp.float32
    )
    grad_rows = lax.psum(partial_grad.astype(jnp.bfloat16), "section").astype(jnp.float32)
    table_head = jnp.einsum(
        "mrkv,mrkd->vd", logit_grad, head_rows, preferred_element_type=jnp.float32
    )
    places = (masked_rows[..., None] == jnp.arange(length)[None, None, None, :]).astype(jnp.float32)
    top_grad = jnp.einsum("mrkl,mrkd->mrld", places, grad_rows, precision=lax.Precision.HIGHEST)
    gradients = (
        jnp.zeros(w_in.shape[1:], jnp.float32),
        jnp.zeros(w_out.shape[1:], jnp.float32),
        jnp.zeros(b_in.shape[1:], jnp.float32),
        jnp.zeros((width,), jnp.float32),
        jnp.zeros((width,), jnp.float32),
        jnp.zeros((width,), jnp.float32),
    )
    grad_entry = jnp.zeros_like(entry)
    back_in = jnp.zeros_like(entry[0])
    for moment in range(ticks):
        micro_index = moment - (sections - 1 - section_index)
        is_live = (micro_index >= 0) & (micro_index < batches)
        micro_slot = jnp.clip(micro_index, 0, batches - 1)
        upstream = jnp.where(
            section_index == sections - 1, top_grad[micro_slot], back_in.astype(jnp.float32)
        )
        branch_index = jnp.where(is_live, 1 + section_index % 2, 0)
        grad_input, gradients = lax.switch(
            branch_index,
            [spare_backward, attend_backward, feed_back_only],
            kept[micro_slot],
            segment_ids[micro_slot],
            upstream,
            gradients,
        )
        grad_entry = grad_entry.at[micro_slot].set(
            jnp.where(is_live, grad_input, grad_entry[micro_slot])
        )
        if moment + 1 < ticks:
            back_in = jax.tree.map(
                lambda part, own: part.astype(own.dtype),
                passed_along(for_sending(grad_input), "section", -1),
                grad_input,
            )
    input_grad = broadcast(grad_entry, "section", 0)
    input_wide = input_grad.astype(jnp.float32)
    pos_grad = jnp.sum(input_wide, (0, 1))
    targets = jnp.where(inside, local_ids, quarter).reshape(-1)
    table_input = jax.ops.segment_sum(
        input_wide.reshape(-1, width), targets, num_segments=quarter + 1
    )[:quarter]
    w_in_part, w_out_part, b_in_part, b_out_part, gain_part, shift_part = gradients
    reduced = (
        lax.psum_scatter(w_in_part, "dp", scatter_dimension=0, tiled=True),
        lax.psum_scatter(w_out_part, "dp", scatter_dimension=0, tiled=True),
        lax.psum_scatter(b_in_part, "dp", scatter_dimension=0, tiled=True),
        lax.psum_scatter(b_out_part, "dp", scatter_dimension=0, tiled=True),
        lax.psum_scatter(gain_part, "dp", scatter_dimension=0, tiled=True),
        lax.psum_scatter(shift_part, "dp", scatter_dimension=0, tiled=True),
        lax.psum_scatter(pos_grad, "dp", scatter_dimension=0, tiled=True),
        lax.psum_scatter(table_input + table_head, "dp", scatter_dimension=0, tiled=True),
    )
    table_grad = reduced[7]
    return (
        logits,
        table_grad,
        reduced[6],
        reduced[0][None],
        reduced[1][None],
        reduced[2][None],
        reduced[3][None],
        reduced[4][None],
        reduced[5][None],
    )


def solution(mesh):
    placed = (
        P(None, "dp", None),
        P(None, "dp", None),
        P(None, "dp", None),
        P("section", None),
        P(),
        P("section", None, None),
        P("section", None, None),
        P("section", None),
        P("section", None),
        P("section", None),
        P("section", None),
        P(None, "dp", None, "section"),
    )
    return jax.shard_map(
        local,
        mesh=mesh,
        in_specs=placed,
        out_specs=(
            P(None, "dp", None, "section"),
            P(("section", "dp"), None),
            P("dp", None),
            P("section", "dp", None),
            P("section", "dp", None),
            P("section", "dp"),
            P("section", "dp"),
            P("section", "dp"),
            P("section", "dp"),
        ),
        check_vma=False,
    )
```

profile of v0, /device:TPU:1, one launch (start us, length us, event | category | flops | bytes accessed | tf_op | source)
XLA Modules:
  0.0 1079.6 jit_solution(4662740884918499774)
XLA Ops:
  12.5 4.8 gather_fusion
  23.0 29.5 %all-reduce.13.cloned.1.call-done = (bf16[2,1,128,768]{3,2,1,0:T(8,128)(2,1)}, bf16[2,40,768]{2,1,0:T(8,128)(2,1)}) async-done(((bf16[2,1,128,768]{3,2,1,0:T(8,128)(2,1)}, bf16[2,40,768]{2,1,0:T(8,128)(2,1)}), (bf16[2,1,128,768]{3,2,1,0:T(8,128)(2,1)}, bf16[2,40,768]{2,1,0:T(8,128)(2,1)})) %all-reduce.13.cloned.1.call-update) | async-done | bytes 516112 | tf_op jit(solution)/shard_map/psum | solution.py:258
  66.5 10.8 conditional.11
  67.4 8.6 fusion.745
  81.6 5.5 collective-permute-done.1
  87.8 10.3 conditional.12
  88.6 8.6 fusion.752
  98.2 4.8 collective-permute-start.2
  106.4 7.2 conditional.13
  113.6 20.5 %collective-permute-start.3 = (bf16[1,128,768]{2,1,0:T(8,128)(2,1)S(1)}, bf16[1,128,768]{2,1,0:T(8,128)(2,1)S(1)}, u32[]{:S(2)}, u32[]{:S(2)}) collective-permute-start(bf16[1,128,768]{2,1,0:T(8,128)(2,1)S(1)} %get-tuple-element.2116), channel_id=1, source_target_pairs={{0,8},{8,16},{16,24},{1,9},{9,17},{17,25},{2,10},{10,18},{18,26},{... | collective-permute-start | bytes 589832 | tf_op jit(solution)/shard_map/ppermute | solution.py:19
  138.9 18.2 %conditional.15 = (bf16[1,128,768]{2,1,0:T(8,128)(2,1)}, f32[768,3072]{0,1:T(8,128)}, f32[3072,768]{1,0:T(8,128)}, f32[3072]{0:T(1024)}, f32[768]{0:T(1024)}, /*index=5*/f32[768]{0:T(1024)}, f32[768]{0:T(1024)}) conditional(s32[]{:T(128)} %clamp.36, () %tuple.318, (bf16[1,1,128,768]{3,2,1,0:T(8,128)(2,1)S(1)}, ...), branch_computations={%region_54.55_spmd, %region_55.68_spmd, %region_68.77_spmd} | conditional | flops 3659066112 | bytes 83807960 | solution.py:333
  166.1 7.2 conditional.16
  177.6 74.3 %collective-permute-done.5 = bf16[1,128,768]{2,1,0:T(8,128)(2,1)S(1)} collective-permute-done((bf16[1,128,768]{2,1,0:T(8,128)(2,1)}, bf16[1,128,768]{2,1,0:T(8,128)(2,1)S(1)}, u32[]{:S(2)}, u32[]{:S(2)}) %collective-permute-start.5) | collective-permute-done | bytes 196640 | tf_op jit(solution)/shard_map/ppermute | solution.py:19
  252.0 33.6 %conditional.17 = (bf16[1,128,768]{2,1,0:T(8,128)(2,1)}, f32[768,3072]{0,1:T(8,128)}, f32[3072,768]{1,0:T(8,128)}, f32[3072]{0:T(1024)}, f32[768]{0:T(1024)}, /*index=5*/f32[768]{0:T(1024)}, f32[768]{0:T(1024)}) conditional(s32[]{:T(128)} %clamp.38, (f32[768,3072]{0,1:T(8,128)}, f32[3072,768]{1,0:T(8,128)}, ...), branch_computations={%region_102.103_spmd, %region_103.116_spmd, %region_116.125_spmd} | conditional | flops 3663790080 | bytes 120814952 | solution.py:333
  253.6 5.8 multiply_convert_fusion.5
  263.0 8.7 convolution_add_fusion.33
  273.0 8.7 bitcast_add_fusion.1
  290.1 44.3 %collective-permute-done.6 = bf16[1,128,768]{2,1,0:T(8,128)(2,1)S(1)} collective-permute-done((bf16[1,128,768]{2,1,0:T(8,128)(2,1)}, bf16[1,128,768]{2,1,0:T(8,128)(2,1)S(1)}, u32[]{:S(2)}, u32[]{:S(2)}) %collective-permute-start.6) | collective-permute-done | bytes 196640 | tf_op jit(solution)/shard_map/ppermute | solution.py:19
  334.5 33.8 %conditional.18 = (bf16[1,128,768]{2,1,0:T(8,128)(2,1)}, f32[768,3072]{0,1:T(8,128)}, f32[3072,768]{1,0:T(8,128)}, f32[3072]{0:T(1024)}, f32[768]{0:T(1024)}, /*index=5*/f32[768]{0:T(1024)}, f32[768]{0:T(1024)}) conditional(s32[]{:T(128)} %clamp.39, (f32[768,3072]{0,1:T(8,128)}, f32[3072,768]{1,0:T(8,128)}, ...), branch_computations={%region_126.127_spmd, %region_127.140_spmd, %region_140.149_spmd} | conditional | flops 3663790080 | bytes 120814952 | solution.py:333
  336.4 5.8 multiply_convert_fusion.7
  345.7 8.7 convolution_add_fusion.39
  355.7 8.7 bitcast_add_fusion.2
  375.7 6.4 conditional.19
  384.6 96.2 %all-reduce.11.cloned.1.call-done = (bf16[2,40,768]{2,1,0:T(8,128)(2,1)}, bf16[2,1,128,768]{3,2,1,0:T(8,128)(2,1)}) async-done(((bf16[2,40,768]{2,1,0:T(8,128)(2,1)}, bf16[2,1,128,768]{3,2,1,0:T(8,128)(2,1)}), (bf16[2,40,768]{2,1,0:T(8,128)(2,1)}, bf16[2,1,128,768]{3,2,1,0:T(8,128)(2,1)})) %all-reduce.11.cloned.1.call-update) | async-done | bytes 516112 | tf_op jit(solution)/shard_map/psum | solution.py:24
  483.2 9.7 copy.264
  493.9 7.2 scatter_custom_fusion
  501.1 10.1 slice_add_fusion.12
  513.7 30.2 %all-reduce.5 = (f32[3072]{0:T(1024)S(1)}, f32[768]{0:T(1024)S(1)}, f32[768]{0:T(1024)S(1)}, f32[768]{0:T(1024)S(1)}) all-reduce(f32[3072]{0:T(1024)} %get-tuple-element.1644, f32[768]{0:T(1024)} %get-tuple-element.1645, f32[768]{0:T(1024)S(1)} %copy-done.89, f32[768]{0:T(1024)S(1)} %copy-done.72), channel_id=6, replica_groups=mesh['section'=4,'dp'=8] {'dp'}, use_global_device_ids=true, to_apply=%region_180.181.clone | all-reduce | flops 5376 | bytes 43008
  546.2 5.4 fusion.704
  551.7 162.2 %reduce-scatter.11.cloned.1.call-done = f32[384,768]{1,0:T(8,128)} async-done(((f32[3072,768]{1,0:T(8,128)}), f32[384,768]{1,0:T(8,128)}) %reduce-scatter.11.cloned.1.call-update) | async-done | bytes 1179664 | tf_op jit(solution)/shard_map/reduce_scatter | solution.py:360
  713.9 166.6 %reduce-scatter.9.cloned.1.call-done = f32[96,3072]{1,0:T(8,128)} async-done(((f32[768,3072]{1,0:T(8,128)}), f32[96,3072]{1,0:T(8,128)}) %reduce-scatter.9.cloned.1.call-update) | async-done | bytes 1179664 | tf_op jit(solution)/shard_map/reduce_scatter | solution.py:359
  880.5 191.9 %reduce-scatter.5.cloned.1.call-done = f32[456,768]{1,0:T(8,128)} async-done(((f32[3648,768]{1,0:T(8,128)}), f32[456,768]{1,0:T(8,128)}) %reduce-scatter.5.cloned.1.call-update) | async-done | bytes 1400848 | tf_op jit(solution)/shard_map/reduce_scatter | solution.py:366
  (234 shorter events, 108.9 us)
Async XLA Ops:
  7.2 45.3 %all-reduce.13.cloned.1.call-start = ((), (), s32[]{:S(2)}) async-start(), calls=%async_computation.9 | async-start | bytes 1032192 | tf_op jit(solution)/shard_map/psum | solution.py:258
  12.4 9.7 copy-start.101
  12.4 9.7 copy-start.102
  12.5 9.7 copy-start.103
  18.2 36.1 %copy-start.105 = (s32[2,1,128]{2,1,0:T(1,128)S(1)}, s32[2,1,128]{2,1,0:T(1,128)}, u32[]{:S(2)}) copy-start(s32[2,1,128]{2,1,0:T(1,128)} %param.113) | copy-start | bytes 3076
  18.2 462.5 %all-reduce.11.cloned.1.call-start = ((), (), s32[]{:S(2)}) async-start(), calls=%async_computation.8 | async-start | bytes 1032192 | tf_op jit(solution)/shard_map/psum | solution.py:24
  22.2 32.8 %copy-start.66 = (f32[768]{0:T(1024)}, f32[768]{0:T(1024)S(1)}, u32[]{:S(2)}) copy-start(f32[768]{0:T(1024)S(1)} %get-tuple-element.2002) | copy-start | bytes 9220
  22.5 32.6 %copy-start.60 = (f32[1,3072]{1,0:T(1,128)}, f32[1,3072]{1,0:T(1,128)S(1)}, u32[]{:S(2)}) copy-start(f32[1,3072]{1,0:T(1,128)S(1)} %convert_element_type.744) | copy-start | bytes 36868
  55.1 10.7 copy-start.44
  55.1 10.7 collective-permute-start
  77.3 9.8 collective-permute-start.1
  98.2 7.4 collective-permute-start.2
  113.6 23.1 %collective-permute-start.3 = (bf16[1,128,768]{2,1,0:T(8,128)(2,1)S(1)}, bf16[1,128,768]{2,1,0:T(8,128)(2,1)S(1)}, u32[]{:S(2)}, u32[]{:S(2)}) collective-permute-start(bf16[1,128,768]{2,1,0:T(8,128)(2,1)S(1)} %get-tuple-element.2116), channel_id=1, source_target_pairs={{0,8},{8,16},{16,24},{1,9},{9,17},{17,25},{2,10},{10,18},{18,26},{... | collective-permute-start | bytes 589832 | tf_op jit(solution)/shard_map/ppermute | solution.py:19
  157.1 8.1 collective-permute-start.4
  173.4 78.6 %copy-start.62 = (f32[1,3072]{1,0:T(1,128)S(1)}, f32[1,3072]{1,0:T(1,128)}, u32[]{:S(2)}) copy-start(f32[1,3072]{1,0:T(1,128)} %copy-done.60) | copy-start | bytes 36868
  173.4 78.6 %copy-start.108 = (s32[2,1,128]{2,1,0:T(1,128)S(1)}, s32[2,1,128]{2,1,0:T(1,128)}, u32[]{:S(2)}) copy-start(s32[2,1,128]{2,1,0:T(1,128)} %param.113) | copy-start | bytes 3076
  173.4 78.5 %collective-permute-start.5 = (bf16[1,128,768]{2,1,0:T(8,128)(2,1)}, bf16[1,128,768]{2,1,0:T(8,128)(2,1)S(1)}, u32[]{:S(2)}, u32[]{:S(2)}) collective-permute-start(bf16[1,128,768]{2,1,0:T(8,128)(2,1)} %get-tuple-element.1620), channel_id=1, source_target_pairs={{8,0},{16,8},{24,16},{9,1},{17,9},{25,17},{10,2},{18,10},{26,18},{... | collective-permute-start | bytes 589832 | tf_op jit(solution)/shard_map/ppermute | solution.py:19
  261.1 20.6 %slice-start.4 = ((s8[4718592]{0:T(1024)(128)(4,1)}), s8[4194304]{0:T(1024)(128)(4,1)S(1)}, s32[]{:S(2)}) async-start(s8[4718592]{0:T(1024)(128)(4,1)} %bitcast.781), calls=%async_computation.14 | async-start | bytes 8388608 | tf_op jit(solution)/shard_map/cond
  263.0 18.7 %slice-start.5 = ((s8[4718592]{0:T(1024)(128)(4,1)}), s8[524288]{0:T(1024)(128)(4,1)S(1)}, s32[]{:S(2)}) async-start(s8[4718592]{0:T(1024)(128)(4,1)} %bitcast.781), calls=%async_computation.15 | async-start | bytes 1048576 | tf_op jit(solution)/shard_map/cond
  285.6 48.8 %copy-start.2 = (bf16[1,1,128,768]{3,2,1,0:T(8,128)(2,1)S(1)}, bf16[1,1,128,768]{3,2,1,0:T(8,128)(2,1)}, u32[]{:S(2)}) copy-start(bf16[1,1,128,768]{3,2,1,0:T(8,128)(2,1)} %get-tuple-element.1993) | copy-start | bytes 589828
  285.6 48.8 %copy-start.63 = (f32[1,3072]{1,0:T(1,128)S(1)}, f32[1,3072]{1,0:T(1,128)}, u32[]{:S(2)}) copy-start(f32[1,3072]{1,0:T(1,128)} %copy-done.60) | copy-start | bytes 36868
  285.6 48.8 %copy-start.109 = (s32[2,1,128]{2,1,0:T(1,128)S(1)}, s32[2,1,128]{2,1,0:T(1,128)}, u32[]{:S(2)}) copy-start(s32[2,1,128]{2,1,0:T(1,128)} %param.113) | copy-start | bytes 3076
  285.6 48.8 %collective-permute-start.6 = (bf16[1,128,768]{2,1,0:T(8,128)(2,1)}, bf16[1,128,768]{2,1,0:T(8,128)(2,1)S(1)}, u32[]{:S(2)}, u32[]{:S(2)}) collective-permute-start(bf16[1,128,768]{2,1,0:T(8,128)(2,1)} %get-tuple-element.1627), channel_id=1, source_target_pairs={{8,0},{16,8},{24,16},{9,1},{17,9},{25,17},{10,2},{18,10},{26,18},{... | collective-permute-start | bytes 589832 | tf_op jit(solution)/shard_map/ppermute | solution.py:19
  343.8 20.6 %slice-start.6 = ((s8[4718592]{0:T(1024)(128)(4,1)}), s8[4194304]{0:T(1024)(128)(4,1)S(1)}, s32[]{:S(2)}) async-start(s8[4718592]{0:T(1024)(128)(4,1)} %bitcast.783), calls=%async_computation.16 | async-start | bytes 8388608 | tf_op jit(solution)/shard_map/cond
  345.7 18.7 %slice-start.7 = ((s8[4718592]{0:T(1024)(128)(4,1)}), s8[524288]{0:T(1024)(128)(4,1)S(1)}, s32[]{:S(2)}) async-start(s8[4718592]{0:T(1024)(128)(4,1)} %bitcast.783), calls=%async_computation.17 | async-start | bytes 1048576 | tf_op jit(solution)/shard_map/cond
  368.3 7.4 copy-start.1
  368.3 7.4 copy-start.64
  368.3 7.3 collective-permute-start.7
  384.5 167.2 %reduce-scatter.7.cloned.1.call-start = ((), (), s32[]{:S(2)}) async-start(), calls=%async_computation.5 | async-start | bytes 442368 | tf_op jit(solution)/shard_map/reduce_scatter | solution.py:365
  482.6 231.3 %reduce-scatter.11.cloned.1.call-start = ((), (), s32[]{:S(2)}) async-start(), calls=%async_computation.7 | async-start | bytes 10616832 | tf_op jit(solution)/shard_map/reduce_scatter | solution.py:360
  483.2 397.3 %reduce-scatter.9.cloned.1.call-start = ((), (), s32[]{:S(2)}) async-start(), calls=%async_computation.6 | async-start | bytes 10616832 | tf_op jit(solution)/shard_map/reduce_scatter | solution.py:359
  492.9 579.5 %reduce-scatter.5.cloned.1.call-start = ((), (), s32[]{:S(2)}) async-start(), calls=%async_computation.4 | async-start | bytes 12607488 | tf_op jit(solution)/shard_map/reduce_scatter | solution.py:366
  (27 other events, 93.2 us)
Sparse Core Ops, SparseCore 0:
  18.4 34.0 all-reduce.12
  384.6 96.0 all-reduce.10
  484.6 61.1 reduce-scatter.6
  549.8 164.0 reduce-scatter.10
  717.9 162.5 reduce-scatter.8
  884.6 187.7 reduce-scatter.4
where the time goes:
time: 1090 us; the launch traced here: 1080 us
  waiting for transfers between devices  779 us (71%)
  matrix products  94.8 us (9%)
  other arithmetic  48 us (4%)
  local copies, waits for them, and re-layouts  43.8 us (4%)
  starting transfers between devices  39.1 us (4%)
  blocking collectives  30.2 us (3%)
  loops' own time  28.2 us (3%)
  between operations  16.7 us (2%)
    reduce_scatter x1, waiting for transfers between devices, local(): lax.psum_scatter(table_input + table_head, 'dp', scatter_dimension=0, til...  192 us
    reduce_scatter x1, waiting for transfers between devices, local(): lax.psum_scatter(w_in_part, 'dp', scatter_dimension=0, tiled=True)  167 us
    reduce_scatter x1, waiting for transfers between devices, local(): lax.psum_scatter(w_out_part, 'dp', scatter_dimension=0, tiled=True)  162 us
    ppermute x8, waiting for transfers between devices, passed_along(): return lax.ppermute(block, axis, route)  132 us
    psum x1, waiting for transfers between devices, broadcast(): return lax.psum(kept, axis)  96.2 us
    ppermute x8, starting transfers between devices, passed_along(): return lax.ppermute(block, axis, route)  38.8 us
    unnamed x1, blocking collectives  30.2 us
    psum x1, waiting for transfers between devices, local(): lax.psum(partial_rows.astype(jnp.bfloat16), 'section').astype(jnp.float32)  29.5 us
  transfers between devices with their start and end apart: 14, of which 13 were waited for; matrix products, arithmetic and copies ran while one was open for 6% of the time, Pallas kernels for 0%

commit v1 on v0

--- a/solution.py
+++ b/solution.py
@@ -1,6 +1,11 @@
+import functools
+import types
+
 import jax
 import jax.numpy as jnp
 from jax import lax
+from jax.experimental import pallas as pl
+from jax.experimental.pallas import tpu as pltpu
 from jax.sharding import PartitionSpec as P
 
 HEADS = 12
@@ -379,7 +384,793 @@
     )
 
 
+SENDS = 140
+RECVS = 150
+VMEM_LIMIT = 64 * 2**20
+BF = jnp.bfloat16
+F32 = jnp.float32
+MESH = pl.DeviceIdType.MESH
+
+
+def mm(a, b):
+    return jnp.dot(a, b, preferred_element_type=F32)
+
+
+def mm_nt(a, b):
+    return lax.dot_general(a, b, (((1,), (1,)), ((), ())), preferred_element_type=F32)
+
+
+def mm_tn(a, b):
+    return lax.dot_general(a, b, (((0,), (0,)), ((), ())), preferred_element_type=F32)
+
+
+def iota(shape, dim):
+    return lax.broadcasted_iota(jnp.int32, shape, dim)
+
+
+def column(row):
+    return jnp.broadcast_to(row.astype(F32), (128, 128)).T
+
+
+class Plan:
+    def __init__(self, n_dp, length, width, ff, quarter, masks):
+        self.n_dp, self.length, self.width, self.ff = n_dp, length, width, ff
+        self.quarter, self.masks = quarter, masks
+        self.nz = n_dp // 2
+        self.share = quarter // n_dp
+        self.in_rows = width // n_dp
+        self.out_rows = ff // n_dp
+        self.mask_pad = -(-masks // 16) * 16
+        self.share_pad = -(-self.share // 128) * 128
+        self.share_rows = -(-self.share // 16) * 16
+        self.chunks = []
+        at = 0
+        while at < quarter:
+            size = min(1024, quarter - at)
+            self.chunks.append((at, size))
+            at += size
+
+
+class Counter:
+    def __init__(self):
+        self.n = 0
+
+    def take(self, k=1):
+        first = self.n
+        self.n += k
+        return first
+
+
+def scratch_list(p):
+    w, ff, ln = p.width, p.ff, p.length
+    mp = p.mask_pad
+    return dict(
+        emb=((p.quarter, w), BF),
+        wa=((w, ff), BF),
+        w1=((w, ff), BF),
+        w2=((ff, w), BF),
+        par_a=((8, ff), F32),
+        par_f=((8, ff), F32),
+        acc=((2 * ln, w), F32),
+        psend=((ln, w), BF),
+        psum=((ln, w), BF),
+        prow=((2, ln, w), BF),
+        lgp=((2 * mp, p.quarter), BF),
+        lgs=((p.n_dp, 2, mp, p.share_pad), BF),
+        lgr=((2, p.n_dp, mp, p.share_pad), BF),
+        g=((2 * mp, w), F32),
+        grow=((2, p.masks, w), F32),
+        gwide=((ln, w), F32),
+        mrow=((8, ln), jnp.int32),
+        ids_own=((8, ln), jnp.int32),
+        ids_all=((p.n_dp, 8, ln), jnp.int32),
+        x_a=((ln, w), BF),
+        x_f=((ln, w), BF),
+        y_f=((ln, w), BF),
+        pk=((ln, 3 * w), BF),
+        ctx=((ln, w), BF),
+        probs=((w // 128, ln, 256), F32),
+        n_a=((ln, w), F32),
+        n_f=((ln, w), F32),
+        inv_a=((ln, 1), F32),
+        inv_f=((ln, 1), F32),
+        hid=((ln, ff), F32),
+        phi=((ln, ff), F32),
+        act=((ln, ff), BF),
+        xt_a=((p.nz, 2, p.in_rows, ln), BF),
+        ct_a=((p.nz, 2, p.in_rows, ln), BF),
+        xt_f=((p.nz, 2, p.in_rows, ln), BF),
+        at_f=((p.nz, 2, p.out_rows, ln), BF),
+        dyin=((ln, w), BF),
+        dyf=((ln, w), F32),
+        dres=((ln, w), F32),
+        dbr_a=((ln, w), BF),
+        dbr_f=((ln, w), BF),
+        dh=((ln, ff), BF),
+        dpk=((ln, 3 * w), BF),
+        dctx=((ln, w), BF),
+        dx=((ln, w), BF),
+        bsum=((1, ff), F32),
+        sm_a=((8, w), F32),
+        sm_f=((8, w), F32),
+        b_act=((p.nz, p.out_rows, 4 * ln), BF),
+        b_x=((p.nz, p.in_rows, 4 * ln), BF),
+        b_dbr=((4 * ln, w), BF),
+        b_dh=((4 * ln, ff), BF),
+        b_sm=((4, 8, w), F32),
+        sm_tot=((8, w), F32),
+        sm_all=((8, w), F32),
+        r_sm=((p.nz, 8, w), F32),
+        r_in=((p.nz, p.in_rows, ff), BF),
+        r_out=((p.nz, p.out_rows, w), BF),
+        ch_all=((2, p.n_dp, mp, w), BF),
+        de_all=((2, p.n_dp, ln, w), BF),
+    )
+
+
+def fused(p, names, *refs):
+    (tok, seg, picks, lg, pos, b_in, b_out, gain, shift, emb_h, w_in_h, w_out_h) = refs[:12]
+    (o_log, o_tab, o_pos, o_win, o_wout, o_bin, o_bout, o_gain, o_shift) = refs[12:21]
+    r = types.SimpleNamespace(**dict(zip(names, refs[21:])))
+    ss, rs, ls = refs[21 + len(names) :]
+    w, ff, ln, mp, nz, n_dp = p.width, p.ff, p.length, p.mask_pad, p.nz, p.n_dp
+    heads = w // 64
+    pairs = heads // 2
+
+    s = lax.axis_index("section")
+    dp = lax.axis_index("dp")
+    x, c = s // 2, lax.rem(s, 2)
+    z, y = dp // 2, lax.rem(dp, 2)
+    core = s + 1 - 2 * c
+    across = s + 2 - 4 * x
+    ydp = dp + 1 - 2 * y
+    other = 1 - c
+    at_x0, at_x1 = x == 0, x == 1
+    is_att, is_ff = c == 0, c == 1
+    sends, recvs = Counter(), Counter()
+    pending = []
+
+    def send(cond, src, dst, dev, recv):
+        slot = sends.take()
+
+        def make():
+            return pltpu.make_async_remote_copy(
+                src_ref=src,
+                dst_ref=dst,
+                send_sem=ss.at[slot],
+                recv_sem=rs.at[recv],
+                device_id=dev,
+                device_id_type=MESH,
+            )
+
+        if cond is None:
+            make().start()
+        else:
+
+            @pl.when(cond)
+            def _():
+                make().start()
+
+        pending.append((cond, make))
+
+    def arrived(dst, recv):
+        pltpu.make_async_remote_copy(
+            src_ref=dst,
+            dst_ref=dst,
+            send_sem=ss.at[0],
+            recv_sem=rs.at[recv],
+            device_id=(core, dp),
+            device_id_type=MESH,
+        ).wait_recv()
+
+    for i, (at, size) in enumerate(p.chunks):
+        pltpu.make_async_copy(emb_h.at[pl.ds(at, size)], r.emb.at[pl.ds(at, size)], ls.at[i]).start()
+    l_w = len(p.chunks)
+
+    @pl.when(is_att)
+    def _():
+        pltpu.make_async_copy(w_in_h.at[0], r.wa, ls.at[l_w]).start()
+
+    @pl.when(is_ff)
+    def _():
+        pltpu.make_async_copy(w_in_h.at[0], r.w1, ls.at[l_w]).start()
+        pltpu.make_async_copy(w_out_h.at[0], r.w2, ls.at[l_w + 1]).start()
+
+    def fill(par):
+        par[0:1, :] = b_in[...].astype(F32)
+        par[1:2, 0:w] = b_out[...].astype(F32)
+        par[2:3, 0:w] = gain[...].astype(F32)
+        par[3:4, 0:w] = shift[...].astype(F32)
+
+    pl.when(is_att)(lambda: fill(r.par_a))
+    pl.when(is_ff)(lambda: fill(r.par_f))
+
+    barrier = pltpu.get_barrier_semaphore()
+    peers = [(s, lax.rem(dp + k, n_dp)) for k in range(1, n_dp)]
+    peers += [(core, dp), (across, dp), (core, ydp)]
+    for peer in peers:
+        pl.semaphore_signal(barrier, inc=1, device_id=peer, device_id_type=MESH)
+    pl.semaphore_wait(barrier, len(peers))
+
+    k_wa, k_w1, k_w2, k_pa, k_pf = (recvs.take() for _ in range(5))
+
+    def weights(cond_att, cond_ff):
+        send(cond_att, r.par_a, r.par_a, (core, dp), k_pa)
+        send(cond_att, w_in_h.at[0], r.wa, (core, dp), k_wa)
+        if cond_ff is not None:
+            send(cond_ff, r.par_f, r.par_f, (core, dp), k_pf)
+            send(cond_ff, w_in_h.at[0], r.w1, (core, dp), k_w1)
+            send(cond_ff, w_out_h.at[0], r.w2, (core, dp), k_w2)
+
+    weights(is_att & at_x0, None)
+
+    cols = [column(tok[m]) for m in range(2)]
+    first = s * p.quarter
+    for i, (at, size) in enumerate(p.chunks):
+        pltpu.make_async_copy(emb_h.at[pl.ds(at, size)], r.emb.at[pl.ds(at, size)], ls.at[i]).wait()
+        lane = (iota((ln, size), 1) + (first + at)).astype(F32)
+        hot = []
+        for m in range(2):
+            wide = jnp.concatenate([cols[m]] * (-(-size // 128)), 1)[:, :size]
+            hot.append(jnp.where(wide == lane, 1.0, 0.0).astype(BF))
+        part = mm(jnp.concatenate(hot, 0), r.emb[at : at + size, :])
+        if i == 0:
+            r.acc[...] = part
+        else:
+            r.acc[...] += part
+    k_p = recvs.take(2)
+    r.psend[...] = r.acc[pl.ds(pl.multiple_of(ln * other, ln), ln), :].astype(BF)
+    send(None, r.psend, r.prow.at[0], (core, dp), k_p)
+    weights(is_att & at_x1, is_ff)
+
+    r.lgp[...] = jnp.zeros(r.lgp.shape, BF)
+    r.lgp[0 : p.masks] = lg[0, 0]
+    r.lgp[mp : mp + p.masks] = lg[1, 0]
+    arrived(r.prow.at[0], k_p)
+    own_rows = r.acc[pl.ds(pl.multiple_of(ln * c, ln), ln), :]
+    r.acc[0:ln, :] = own_rows + r.prow[0].astype(F32)
+
+    r.psum[...] = r.acc[0:ln, :].astype(BF)
+    send(at_x1, r.psum, r.prow.at[1], (across, dp), k_p + 1)
+
+    for i, (at, size) in enumerate(p.chunks):
+        part = mm(r.lgp[:, at : at + size], r.emb[at : at + size, :])
+        if i == 0:
+            r.g[...] = part
+        else:
+            r.g[...] += part
+    k_g = recvs.take(2)
+    send(None, r.g.at[pl.ds(pl.multiple_of(mp * other, mp), p.masks)], r.grow.at[0], (core, dp), k_g)
+
+    r.lgs[...] = jnp.zeros(r.lgs.shape, BF)
+    for j in range(n_dp):
+        for m in range(2):
+            r.lgs[j, m, :, 0 : p.share] = r.lgp[mp * m : mp * m + mp, p.share * j : p.share * (j + 1)]
+    r.ids_own[...] = jnp.zeros(r.ids_own.shape, jnp.int32)
+    for m in range(2):
+        r.ids_own[m : m + 1, :] = tok[m]
+    r.ids_all[dp] = r.ids_own[...]
+    k_lg, k_id = recvs.take(n_dp), recvs.take(n_dp)
+    r.lgr[:, dp] = r.lgs[dp]
+    for k in range(1, n_dp):
+        to = lax.rem(dp + k, n_dp)
+        send(None, r.lgs.at[to], r.lgr.at[:, dp], (s, to), k_lg + dp)
+        send(None, r.ids_own, r.ids_all.at[dp], (s, to), k_id + dp)
+
+    arrived(r.grow.at[0], k_g)
+    own_g = r.g[pl.ds(pl.multiple_of(mp * c, mp), p.masks), :] + r.grow[0]
+    r.gwide[...] = jnp.zeros(r.gwide.shape, F32)
+    r.gwide[0 : p.masks, :] = own_g
+    send(at_x0, r.gwide.at[0 : p.masks], r.grow.at[1], (across, dp), k_g + 1)
+
+    k_x = recvs.take()
+
+    @pl.when(at_x0)
+    def _():
+        arrived(r.prow.at[1], k_p + 1)
+        whole = r.acc[0:ln, :] + r.prow[1].astype(F32)
+        r.x_a[...] = (whole + pos[...].astype(F32)).astype(BF)
+
+    @pl.when(is_att)
+    def _():
+        pltpu.make_async_copy(w_in_h.at[0], r.wa, ls.at[l_w]).wait()
+        arrived(r.par_f, k_pf)
+
+    @pl.when(is_ff)
+    def _():
+        arrived(r.par_a, k_pa)
+        arrived(r.wa, k_wa)
+
+    @pl.when(at_x1)
+    def _():
+        arrived(r.x_a, k_x)
+
+    low = jnp.where(iota((ln, 128), 1) < 64, 1.0, 0.0).astype(BF)
+    high = jnp.where(iota((ln, 128), 1) < 64, 0.0, 1.0).astype(BF)
+
+    def split(block):
+        return jnp.concatenate([block * low, block * high], 0)
+
+    def stack(block):
+        return jnp.concatenate([block[:, 0:128], block[:, 128:256]], 0)
+
+    def norm_forward(resid, par, n_ref, inv_ref):
+        centred = resid - jnp.mean(resid, -1, keepdims=True)
+        inverse = lax.rsqrt(jnp.mean(centred * centred, -1, keepdims=True) + EPSILON)
+        normed = centred * inverse
+        n_ref[...] = normed
+        inv_ref[...] = inverse
+        return (normed * par[2:3, 0:w] + par[3:4, 0:w]).astype(BF)
+
+    rows_x = r.x_a[...]
+    for j in range(3):
+        part = mm(rows_x, r.wa[:, j * w : (j + 1) * w])
+        if j != 1:
+            part = part + r.par_a[0:1, j * w : (j + 1) * w]
+        r.pk[:, j * w : (j + 1) * w] = part.astype(BF)
+    seg_row = seg[c].astype(F32)
+    seg_col = column(seg[c])
+    seg_row = jnp.broadcast_to(jnp.concatenate([seg_row, seg_row], 1), (ln, 256))
+    seg_col = jnp.concatenate([seg_col, seg_col], 1)
+    for h in range(pairs):
+        at = 128 * h
+        query = r.pk[:, at : at + 128]
+        keyed = split(r.pk[:, w + at : w + at + 128])
+        value = split(r.pk[:, 2 * w + at : 2 * w + at + 128])
+        scores = jnp.where(seg_row == seg_col, mm_nt(query, keyed) * 0.125, -1e9)
+        chance = []
+        for half in (scores[:, 0:128], scores[:, 128:256]):
+            power = jnp.exp(half - jnp.max(half, -1, keepdims=True))
+            chance.append(power / jnp.sum(power, -1, keepdims=True))
+        chance = jnp.concatenate(chance, 1)
+        r.probs[h] = chance
+        r.ctx[:, at : at + 128] = mm(chance.astype(BF), value).astype(BF)
+    resid = rows_x.astype(F32) + mm(r.ctx[...], r.wa[:, 3 * w : 4 * w]) + r.par_a[1:2, 0:w]
+    r.x_f[...] = norm_forward(resid, r.par_a, r.n_a, r.inv_a)
+
+    @pl.when(is_ff)
+    def _():
+        pltpu.make_async_copy(w_in_h.at[0], r.w1, ls.at[l_w]).wait()
+        pltpu.make_async_copy(w_out_h.at[0], r.w2, ls.at[l_w + 1]).wait()
+
+    @pl.when(is_att)
+    def _():
+        arrived(r.w1, k_w1)
+        arrived(r.w2, k_w2)
+
+    rows_x = r.x_f[...]
+    total = rows_x.astype(F32) + r.par_f[1:2, 0:w]
+    for j in range(ff // w):
+        cut = slice(j * w, (j + 1) * w)
+        hidden = mm(rows_x, r.w1[:, cut]) + r.par_f[0:1, cut]
+        below = 0.5 + 0.5 * lax.erf(hidden * (0.5**0.5))
+        active = (hidden * below).astype(BF)
+        r.hid[:, cut] = hidden
+        r.phi[:, cut] = below
+        r.act[:, cut] = active
+        total = total + mm(active, r.w2[cut, :])
+    r.y_f[...] = norm_forward(total, r.par_f, r.n_f, r.inv_f)
+    send(at_x0, r.y_f, r.x_a, (across, dp), k_x)
+
+    def line(buf, base):
+        own = buf(dp)
+        send(None, own, own, (s, ydp), base + dp)
+        send(z < nz - 1, own, own, (s, dp + 2), base + dp)
+        send(z > 0, own, own, (s, dp - 2), base + dp)
+
+    def line_step(buf, base, t):
+        for sign in (-1, 1):
+            from_z = z + sign * t
+            here = (from_z >= 0) & (from_z < nz)
+            from_dp = jnp.clip(from_z, 0, nz - 1) * 2 + y
+            piece = buf(from_dp)
+            pl.when(here)(lambda piece=piece, from_dp=from_dp: arrived(piece, base + from_dp))
+            to_z = z - sign
+            on = here & (to_z >= 0) & (to_z < nz)
+            if t < nz - 1:
+                send(on, piece, piece, (s, dp - 2 * sign), base + from_dp)
+            send(here, piece, piece, (s, ydp), base + from_dp)
+
+    def line_end(buf, base):
+        for zz in range(nz):
+            from_dp = 2 * zz + 1 - y
+            arrived(buf(from_dp), base + from_dp)
+
+    k_ch, k_chx, k_de, k_dex = recvs.take(n_dp), recvs.take(), recvs.take(n_dp), recvs.take()
+
+    def ch(i):
+        return r.ch_all.at[c, i]
+
+    def de(i):
+        return r.de_all.at[c, i]
+
+    @pl.when(at_x1)
+    def _():
+        r.mrow[...] = jnp.full(r.mrow.shape, -1, jnp.int32)
+        r.mrow[0:1, 0 : p.masks] = picks[c]
+        places = jnp.where(iota((ln, ln), 0) == r.mrow[0:1, :], 1.0, 0.0).astype(BF)
+        r.ch_all[c, dp] = mm_tn(places, r.y_f[...])[0:mp].astype(BF)
+        arrived(r.grow.at[1], k_g + 1)
+        r.gwide[0 : p.masks, :] += r.grow[1]
+        coarse = r.gwide[...].astype(BF)
+        fine = (r.gwide[...] - coarse.astype(F32)).astype(BF)
+        r.dyf[...] = mm(places, coarse) + mm(places, fine)
+
+    send(at_x1, ch(dp), ch(dp), (across, dp), k_ch + dp)
+
+    def push(owner, kind, src, dst):
+        home = c == owner
+        slot_y = 2 + jnp.where(home, 0, 1)
+        own_dst, near_dst, far_dst = dst(0), dst(1), dst(slot_y)
+
+        @pl.when(home)
+        def _():
+            pltpu.make_async_copy(src(y), own_dst, rs.at[kind]).start()
+
+        send(jnp.logical_not(home), src(y), near_dst, (core, dp), kind + 1)
+        far_s = jnp.where(home, s, core)
+        send(None, src(1 - y), far_dst, (far_s, ydp), kind + slot_y)
+
+    def gathered(kind, dst):
+        pltpu.make_async_copy(dst(0), dst(0), rs.at[kind]).wait()
+        for slot in range(1, 4):
+            arrived(dst(slot), kind + slot)
+
+    def lanes(slot):
+        return pl.ds(slot * ln if isinstance(slot, int) else pl.multiple_of(slot * ln, ln), ln)
+
+    tiles = ff // w
+    k_dh = [recvs.take(4) for _ in range(tiles)]
+    k_act, k_xt, k_db, k_sm = (recvs.take(4) for _ in range(4))
+    to_x = lambda slot: r.b_x.at[:, :, lanes(slot)]
+    to_act = lambda slot: r.b_act.at[:, :, lanes(slot)]
+    to_ctx = lambda slot: r.b_act.at[:, 0 : p.in_rows, lanes(slot)]
+    to_dbr = lambda slot: r.b_dbr.at[lanes(slot), :]
+    to_sm = lambda slot: r.b_sm.at[slot]
+
+    def to_dh(j):
+        return lambda slot: r.b_dh.at[lanes(slot), j * w : (j + 1) * w]
+
+    def blocks(dst, value, rows):
+        turned = value.T
+        for b in range(n_dp):
+            dst[b // 2, b % 2] = turned[b * rows : (b + 1) * rows]
+
+    def prepare():
+        blocks(r.xt_a, r.x_a[...], p.in_rows)
+        blocks(r.ct_a, r.ctx[...], p.in_rows)
+        blocks(r.xt_f, r.x_f[...], p.in_rows)
+        blocks(r.at_f, r.act[...], p.out_rows)
+
+    prepare()
+    push(0, k_xt, lambda i: r.xt_a.at[:, i], to_x)
+    push(0, k_act, lambda i: r.ct_a.at[:, i], to_ctx)
+    push(1, k_xt, lambda i: r.xt_f.at[:, i], to_x)
+    push(1, k_act, lambda i: r.at_f.at[:, i], to_act)
+
+    @pl.when(at_x0)
+    def _():
+        arrived(ch(dp), k_ch + dp)
+
+    line(ch, k_ch)
+    k_dy = recvs.take()
+
+    @pl.when(at_x0)
+    def _():
+        arrived(r.dyin, k_dy)
+        r.dyf[...] = r.dyin[...].astype(F32)
+
+    def norm_backward(par, n_ref, inv_ref):
+        up, normed = r.dyf[...], n_ref[...]
+        gain_part = jnp.sum(up * normed, 0, keepdims=True)
+        shift_part = jnp.sum(up, 0, keepdims=True)
+        scaled = up * par[2:3, 0:w]
+        first_mean = jnp.mean(scaled, -1, keepdims=True)
+        second_mean = jnp.mean(scaled * normed, -1, keepdims=True)
+        return inv_ref[...] * (scaled - first_mean - normed * second_mean), gain_part, shift_part
+
+    def small(dst, out_part, gain_part, shift_part):
+        dst[...] = jnp.zeros(dst.shape, F32)
+        n_b, n_w = ff // n_dp, w // n_dp
+        for k in range(n_dp):
+            dst[k : k + 1, 0:n_b] = r.bsum[:, k * n_b : (k + 1) * n_b]
+            dst[k : k + 1, n_b : n_b + n_w] = out_part[:, k * n_w : (k + 1) * n_w]
+            dst[k : k + 1, n_b + 128 : n_b + 128 + n_w] = gain_part[:, k * n_w : (k + 1) * n_w]
+            dst[k : k + 1, n_b + 256 : n_b + 256 + n_w] = shift_part[:, k * n_w : (k + 1) * n_w]
+
+    dres, gain_part, shift_part = norm_backward(r.par_f, r.n_f, r.inv_f)
+    r.dres[...] = dres
+    r.dbr_f[...] = dres.astype(BF)
+    push(1, k_db, lambda i: r.dbr_f, to_dbr)
+    branch = r.dbr_f[...]
+    total = r.dres[...]
+    for j in range(tiles):
+        cut = slice(j * w, (j + 1) * w)
+        hidden = r.hid[:, cut]
+        slope = r.phi[:, cut] + hidden * (0.3989422804014327 * jnp.exp(-0.5 * hidden * hidden))
+        dhidden = (mm_nt(branch, r.w2[cut, :]) * slope).astype(BF)
+        r.dh[:, cut] = dhidden
+        push(1, k_dh[j], lambda i, cut=cut: r.dh.at[:, cut], to_dh(j))
+        r.bsum[:, cut] = jnp.sum(dhidden.astype(F32), 0, keepdims=True)
+        total = total + mm_nt(dhidden, r.w1[:, cut])
+    r.dyf[...] = total.astype(BF).astype(F32)
+    small(r.sm_f, jnp.sum(branch.astype(F32), 0, keepdims=True), gain_part, shift_part)
+    push(1, k_sm, lambda i: r.sm_f, to_sm)
+
+    dres, gain_part, shift_part = norm_backward(r.par_a, r.n_a, r.inv_a)
+    r.dres[...] = dres
+    r.dbr_a[...] = dres.astype(BF)
+    push(0, k_db, lambda i: r.dbr_a, to_dbr)
+    branch = r.dbr_a[...]
+    r.dctx[...] = mm_nt(branch, r.wa[:, 3 * w : 4 * w]).astype(BF)
+    for h in range(pairs):
+        at = 128 * h
+        query = r.pk[:, at : at + 128]
+        keyed = split(r.pk[:, w + at : w + at + 128])
+        value = split(r.pk[:, 2 * w + at : 2 * w + at + 128])
+        upper = r.dctx[:, at : at + 128]
+        chance = r.probs[h]
+        dchance = mm_nt(upper, value)
+        mixed = chance * dchance
+        dscores = []
+        for cut in (slice(0, 128), slice(128, 256)):
+            dscores.append(mixed[:, cut] - chance[:, cut] * jnp.sum(mixed[:, cut], -1, keepdims=True))
+        dscores = jnp.concatenate(dscores, 1).astype(BF)
+        r.dpk[:, at : at + 128] = (mm(dscores, keyed) * 0.125).astype(BF)
+        r.dpk[:, w + at : w + at + 128] = (mm_tn(stack(dscores), split(query)) * 0.125).astype(BF)
+        r.dpk[:, 2 * w + at : 2 * w + at + 128] = mm_tn(stack(chance.astype(BF)), split(upper)).astype(BF)
+    total = r.dres[...]
+    r.bsum[...] = jnp.zeros(r.bsum.shape, F32)
+    for j in range(3):
+        cut = slice(j * w, (j + 1) * w)
+        push(0, k_dh[j], lambda i, cut=cut: r.dpk.at[:, cut], to_dh(j))
+        dpart = r.dpk[:, cut]
+        if j != 1:
+            r.bsum[:, cut] = jnp.sum(dpart.astype(F32), 0, keepdims=True)
+        total = total + mm_nt(dpart, r.wa[:, cut])
+    r.dx[...] = total.astype(BF)
+    send(at_x1, r.dx, r.dyin, (across, dp), k_dy)
+
+    @pl.when(at_x0)
+    def _():
+        r.de_all[c, dp] = r.dx[...]
+
+    send(at_x0, r.dx, de(dp), (across, dp), k_de + dp)
+    small(r.sm_a, jnp.sum(branch.astype(F32), 0, keepdims=True), gain_part, shift_part)
+    push(0, k_sm, lambda i: r.sm_a, to_sm)
+
+    k_in = [recvs.take(nz) for _ in range(tiles)]
+    k_out, k_smz = recvs.take(nz), recvs.take(nz)
+    half = nz * p.in_rows
+
+    def spread(cond, src, dst, base):
+        for k in range(1, nz):
+            zz = lax.rem(z + k, nz)
+            send(cond, src(zz), dst, (s, 2 * zz + y), base + z)
+
+    @pl.when(is_ff)
+    def _():
+        gathered(k_act, to_act)
+        gathered(k_db, to_dbr)
+        for zz in range(nz):
+            grad = mm(r.b_act[zz], r.b_dbr[...])
+            r.w2[zz * p.out_rows : (zz + 1) * p.out_rows, :] = grad.astype(BF)
+        r.r_out[z] = r.w2[pl.ds(pl.multiple_of(z * p.out_rows, p.out_rows), p.out_rows), :]
+
+    def out_part(zz):
+        return r.w2.at[pl.ds(pl.multiple_of(zz * p.out_rows, p.out_rows), p.out_rows)]
+
+    spread(is_ff, out_part, r.r_out.at[z], k_out)
+
+    @pl.when(is_ff)
+    def _():
+        gathered(k_xt, to_x)
+
+    @pl.when(is_att)
+    def _():
+        gathered(k_xt, to_x)
+        gathered(k_act, to_ctx)
+        gathered(k_db, to_dbr)
+
+    for j in (3, 0, 1, 2):
+        cut = slice(j * w, (j + 1) * w)
+
+        def keep(grad, cut=cut):
+            r.wa[0:half, cut] = grad.astype(BF)
+            r.r_in[z, :, cut] = r.wa[pl.ds(pl.multiple_of(z * p.in_rows, p.in_rows), p.in_rows), cut]
+
+        @pl.when(is_ff)
+        def _():
+            gathered(k_dh[j], to_dh(j))
+            keep(mm(r.b_x[...].reshape(half, 4 * ln), r.b_dh[:, cut]))
+
+        @pl.when(is_att)
+        def _():
+            if j == 3:
+                keep(mm(r.b_act[:, 0 : p.in_rows].reshape(half, 4 * ln), r.b_dbr[...]))
+            else:
+                gathered(k_dh[j], to_dh(j))
+                keep(mm(r.b_x[...].reshape(half, 4 * ln), r.b_dh[:, cut]))
+
+        def in_part(zz, cut=cut):
+            return r.wa.at[pl.ds(pl.multiple_of(zz * p.in_rows, p.in_rows), p.in_rows), cut]
+
+        spread(None, in_part, r.r_in.at[z, :, cut], k_in[j])
+
+    gathered(k_sm, to_sm)
+    r.sm_tot[...] = r.b_sm[0] + r.b_sm[1] + r.b_sm[2] + r.b_sm[3]
+    r.r_sm[z] = r.sm_tot[...]
+    spread(None, lambda zz: r.sm_tot, r.r_sm.at[z], k_smz)
+
+    @pl.when(at_x1)
+    def _():
+        arrived(de(dp), k_de + dp)
+
+    line(de, k_de)
+    for t in range(1, nz):
+        line_step(ch, k_ch, t)
+        line_step(de, k_de, t)
+    line_end(ch, k_ch)
+    send(None, r.ch_all.at[c], r.ch_all.at[c], (core, dp), k_chx)
+    line_end(de, k_de)
+    send(None, r.de_all.at[c], r.de_all.at[c], (core, dp), k_dex)
+
+    arrived(r.ch_all.at[other], k_chx)
+    chosen = jnp.concatenate([r.ch_all[0, dp], r.ch_all[1, dp]], 0)
+    for at, size in p.chunks:
+        part = mm_nt(chosen, r.emb[at : at + size, :])
+        for m in range(2):
+            o_log[m, 0, :, at : at + size] = part[mp * m : mp * m + p.masks]
+    for k in range(1, n_dp):
+        src = lax.rem(dp + k, n_dp)
+        arrived(r.lgr.at[:, src], k_lg + src)
+        arrived(r.ids_all.at[src], k_id + src)
+    lines = 2 * n_dp * mp
+    grad = mm_tn(r.lgr[...].reshape(lines, p.share_pad), r.ch_all[...].reshape(lines, w))
+    o_tab[...] = grad[0 : p.share]
+
+    arrived(r.de_all.at[other], k_dex)
+    entry = iota((p.share_rows, ln), 0) + (s * p.quarter + dp * p.share)
+
+    def scatter(i, carry):
+        hot = []
+        for m in range(2):
+            hot.append(jnp.where(entry == r.ids_all[i, m : m + 1, :], 1.0, 0.0).astype(BF))
+        rows = jnp.concatenate([r.de_all[0, i], r.de_all[1, i]], 0)
+        o_tab[...] += mm(jnp.concatenate(hot, 1), rows)[0 : p.share]
+        return carry
+
+    lax.fori_loop(0, n_dp, scatter, 0)
+    n_pos = ln // n_dp
+    here = pl.ds(pl.multiple_of(dp * n_pos, n_pos), n_pos)
+    total = jnp.zeros((n_pos, w), F32)
+    for m in range(2):
+        for i in range(n_dp):
+            total = total + r.de_all[m, i, here, :].astype(F32)
+    o_pos[...] = total
+
+    for j in range(tiles):
+        for k in range(1, nz):
+            src = lax.rem(z + k, nz)
+            arrived(r.r_in.at[src, :, j * w : (j + 1) * w], k_in[j] + src)
+    total = r.r_in[0].astype(F32)
+    for zz in range(1, nz):
+        total = total + r.r_in[zz].astype(F32)
+    o_win[0] = total
+
+    @pl.when(is_ff)
+    def _():
+        for k in range(1, nz):
+            src = lax.rem(z + k, nz)
+            arrived(r.r_out.at[src], k_out + src)
+        total = r.r_out[0].astype(F32)
+        for zz in range(1, nz):
+            total = total + r.r_out[zz].astype(F32)
+        o_wout[0] = total
+
+    @pl.when(is_att)
+    def _():
+        o_wout[...] = jnp.zeros(o_wout.shape, F32)
+
+    for k in range(1, nz):
+        src = lax.rem(z + k, nz)
+        arrived(r.r_sm.at[src], k_smz + src)
+    r.sm_all[...] = r.r_sm[0] + r.r_sm[1] + r.r_sm[2] + r.r_sm[3]
+    mine = r.sm_all[pl.ds(dp, 1), :]
+    n_b, n_w = ff // n_dp, w // n_dp
+    o_bin[...] = mine[:, 0:n_b]
+    o_bout[...] = mine[:, n_b : n_b + n_w]
+    o_gain[...] = mine[:, n_b + 128 : n_b + 128 + n_w]
+    o_shift[...] = mine[:, n_b + 256 : n_b + 256 + n_w]
+
+    for cond, make in pending:
+        if cond is None:
+            make().wait_send()
+        else:
+            pl.when(cond)(lambda make=make: make().wait_send())
+    assert sends.n <= SENDS and recvs.n <= RECVS, (sends.n, recvs.n)
+
+
+def whole(
+    n_dp,
+    token_ids,
+    segment_ids,
+    masked_rows,
+    embedding,
+    pos_table,
+    w_in,
+    w_out,
+    b_in,
+    b_out,
+    norm_gain,
+    norm_shift,
+    logit_grad,
+):
+    quarter, width = embedding.shape
+    batches, _, length = token_ids.shape
+    masks = masked_rows.shape[-1]
+    ff = w_in.shape[-1]
+    p = Plan(n_dp, length, width, ff, quarter, masks)
+    scratch = scratch_list(p)
+    shapes = [
+        (batches, 1, masks, quarter),
+        (p.share, width),
+        (length // n_dp, width),
+        (1, p.in_rows, ff),
+        (1, p.out_rows, width),
+        (1, ff // n_dp),
+        (1, p.in_rows),
+        (1, p.in_rows),
+        (1, p.in_rows),
+    ]
+    vmem = pl.BlockSpec(memory_space=pltpu.VMEM)
+    far = pl.BlockSpec(memory_space=pl.ANY)
+    return pl.pallas_call(
+        functools.partial(fused, p, list(scratch)),
+        out_shape=[jax.ShapeDtypeStruct(shape, F32) for shape in shapes],
+        in_specs=[vmem] * 9 + [far] * 3,
+        out_specs=[vmem] * 9,
+        scratch_shapes=[pltpu.VMEM(*one) for one in scratch.values()]
+        + [
+            pltpu.SemaphoreType.DMA((SENDS,)),
+            pltpu.SemaphoreType.DMA((RECVS,)),
+            pltpu.SemaphoreType.DMA((len(p.chunks) + 2,)),
+        ],
+        compiler_params=pltpu.CompilerParams(
+            collective_id=0, has_side_effects=True, vmem_limit_bytes=VMEM_LIMIT
+        ),
+    )(
+        token_ids,
+        segment_ids,
+        masked_rows,
+        logit_grad,
+        pos_table,
+        b_in,
+        b_out,
+        norm_gain,
+        norm_shift,
+        embedding,
+        w_in,
+        w_out,
+    )
+
+
 def solution(mesh):
+    n_section, n_dp = mesh.shape["section"], mesh.shape["dp"]
+
+    def chosen_form(*args):
+        token_ids, embedding, w_in = args[0], args[3], args[5]
+        fits = (
+            n_section == 4
+            and n_dp == 8
+            and token_ids.shape[0] == 2
+            and token_ids.shape[1:] == (1, 128)
+            and w_in.shape[1] % (16 * n_dp) == 0
+            and w_in.shape[2] == 4 * w_in.shape[1]
+            and embedding.shape[0] % (8 * n_dp) == 0
+        )
+        return whole(n_dp, *args) if fits else local(*args)
+
     placed = (
         P(None, "dp", None),
         P(None, "dp", None),
@@ -395,7 +1186,7 @@
         P(None, "dp", None, "section"),
     )
     return jax.shard_map(
-        local,
+        chosen_form,
         mesh=mesh,
         in_specs=placed,
         out_specs=(

time: 1090 us -> 183 us (0.17)
  waiting for transfers between devices: 779 us -> 0 us
  Pallas kernels: 0 us -> 171 us
  matrix products: 94.8 us -> 0 us
  other arithmetic: 48 us -> 0 us
  starting transfers between devices: 39.1 us -> 0 us
  local copies, waits for them, and re-layouts: 43.8 us -> 9.1 us
  blocking collectives: 30.2 us -> 0 us
  loops' own time: 28.2 us -> 0 us
  between operations: 16.7 us -> 0.68 us
    reduce_scatter x4 -> x0, waiting for transfers between devices: 521 us -> none  [the longest x1 192 us: local(): lax.psum_scatter(table_input + table_head, 'dp', scatter_dimension=0, til...]
    pallas_call x0 -> x1, Pallas kernels: none -> 171 us  [whole(): pl.pallas_call(functools.partial(fused, p, list(scratch)), out_shape=[jax...]
    ppermute x8 -> x0, waiting for transfers between devices: 132 us -> none  [passed_along(): return lax.ppermute(block, axis, route)]
    psum x2 -> x0, waiting for transfers between devices: 126 us -> none  [the longest x1 96.2 us: broadcast(): return lax.psum(kept, axis)]
    dot_general x18 -> x0, matrix products: 94.8 us -> none  [the longest x4 18.9 us: feed_forward(): jnp.dot(active, w_second, preferred_element_type=jnp.float32) + bias_second]
    ppermute x8 -> x0, starting transfers between devices: 38.8 us -> none  [passed_along(): return lax.ppermute(block, axis, route)]
    unnamed x1 -> x0, blocking collectives: 30.2 us -> none
    another operation x10 -> x0, loops' own time: 28.2 us -> none  [the longest x5 20.4 us: local(): lax.switch(branch_index, [spare_backward, attend_backward, feed_back_only...]
  transfers between devices with their start and end apart: 14 -> 0, of which waited for: 13 -> 0; matrix products, arithmetic and copies ran while one was open for 6% -> 0% of each run, Pallas kernels for 0% -> 0%
where the time goes in v1:
time: 183 us; the launch traced here: 181 us
  Pallas kernels  171 us (93%)
  local copies, waits for them, and re-layouts  9.1 us (5%)
    pallas_call x1, Pallas kernels, whole(): pl.pallas_call(functools.partial(fused, p, list(scratch)), out_shape=[jax...  171 us
    unnamed x25, local copies, waits for them, and re-layouts  9.1 us

profile of v1, /device:TPU:1, one launch (start us, length us, event | category | flops | bytes accessed | tf_op | source)
XLA Modules:
  0.0 181.1 jit_solution(14598324060838550758)
XLA Ops:
  0.6 171.3 %shard_map.187 = (f32[2,1,40,3648]{3,2,1,0:T(8,128)}, f32[456,768]{1,0:T(8,128)}, f32[16,768]{1,0:T(8,128)}, f32[1,96,3072]{2,1,0:T(8,128)}, f32[1,384,768]{2,1,...) custom-call(s32[2,1,128]{2,1,0:T(1,128)} %refs_0_.1, ...), custom_call_target="tpu_custom_call" | custom-call | tf_op jit(solution)/shard_map/pallas_call | solution.py:1128
  172.0 0.0 copy-start
  172.0 2.5 %copy.30 = f32[2,1,40,3648]{3,2,1,0:T(8,128)} copy(f32[2,1,40,3648]{3,2,1,0:T(8,128)} %get-tuple-element.18) | data formatting | bytes 2334720
  174.5 0.0 copy-done
  174.5 0.0 copy-start.3
  174.5 0.0 copy-start.2
  174.5 1.1 copy.31
  175.6 0.0 copy-done.3
  175.6 0.6 copy.32
  176.2 0.1 copy-done.2
  176.3 0.0 copy-start.1
  176.3 1.0 copy.33
  177.3 0.7 copy-done.1
  178.0 0.0 copy-start.4
  178.0 0.0 copy-start.7
  178.0 0.0 copy-start.6
  178.0 0.0 copy-start.5
  178.0 1.0 copy.34
  179.0 0.0 copy-done.4
  179.0 0.6 copy.35
  179.6 0.0 copy-done.7
  179.6 0.5 copy.36
  180.1 0.0 copy-done.6
  180.1 0.5 copy.37
  180.6 0.0 copy-done.5
  180.6 0.5 copy.38
Async XLA Ops:
  172.0 2.5 %copy-start = (f32[456,768]{1,0:T(8,128)S(1)}, f32[456,768]{1,0:T(8,128)}, u32[]{:S(2)}) copy-start(f32[456,768]{1,0:T(8,128)} %get-tuple-element.19) | copy-start | bytes 4202500
  174.5 1.1 copy-start.3
  174.5 1.8 copy-start.2
  176.3 1.7 copy-start.1
  178.0 1.0 copy-start.4
  178.0 1.6 copy-start.7
  178.0 2.1 %copy-start.6 = (f32[1,96]{1,0:T(1,128)S(1)}, f32[1,96]{1,0:T(1,128)}, u32[]{:S(2)}) copy-start(f32[1,96]{1,0:T(1,128)} %get-tuple-element.25) | copy-start | bytes 1156
  178.0 2.6 %copy-start.5 = (f32[1,96]{1,0:T(1,128)S(1)}, f32[1,96]{1,0:T(1,128)}, u32[]{:S(2)}) copy-start(f32[1,96]{1,0:T(1,128)} %get-tuple-element.26) | copy-start | bytes 1156

commit v2 on v1

--- a/solution.py
+++ b/solution.py
@@ -384,8 +384,8 @@
     )
 
 
-SENDS = 140
-RECVS = 150
+SENDS = 230
+RECVS = 160
 VMEM_LIMIT = 64 * 2**20
 BF = jnp.bfloat16
 F32 = jnp.float32
@@ -456,8 +456,9 @@
         psum=((ln, w), BF),
         prow=((2, ln, w), BF),
         lgp=((2 * mp, p.quarter), BF),
-        lgs=((p.n_dp, 2, mp, p.share_pad), BF),
-        lgr=((2, p.n_dp, mp, p.share_pad), BF),
+        lgs=((p.n_dp, 2 * p.masks, p.share_pad), BF),
+        lgr=((p.n_dp, 2 * p.masks, p.share_pad), BF),
+        ch_pack=((p.n_dp, 2 * p.masks, w), BF),
         g=((2 * mp, w), F32),
         grow=((2, p.masks, w), F32),
         gwide=((ln, w), F32),
@@ -467,6 +468,7 @@
         x_a=((ln, w), BF),
         x_f=((ln, w), BF),
         y_f=((ln, w), BF),
+        y_o=((ln, w), BF),
         pk=((ln, 3 * w), BF),
         ctx=((ln, w), BF),
         probs=((w // 128, ln, 256), F32),
@@ -474,35 +476,35 @@
         n_f=((ln, w), F32),
         inv_a=((ln, 1), F32),
         inv_f=((ln, 1), F32),
-        hid=((ln, ff), F32),
-        phi=((ln, ff), F32),
-        act=((ln, ff), BF),
+        slope=((ln, ff), BF),
         xt_a=((p.nz, 2, p.in_rows, ln), BF),
         ct_a=((p.nz, 2, p.in_rows, ln), BF),
-        xt_f=((p.nz, 2, p.in_rows, ln), BF),
-        at_f=((p.nz, 2, p.out_rows, ln), BF),
         dyin=((ln, w), BF),
         dyf=((ln, w), F32),
         dres=((ln, w), F32),
         dbr_a=((ln, w), BF),
-        dbr_f=((ln, w), BF),
-        dh=((ln, ff), BF),
         dpk=((ln, 3 * w), BF),
         dctx=((ln, w), BF),
         dx=((ln, w), BF),
         bsum=((1, ff), F32),
         sm_a=((8, w), F32),
         sm_f=((8, w), F32),
-        b_act=((p.nz, p.out_rows, 4 * ln), BF),
+        b_ctx=((p.nz, p.in_rows, 4 * ln), BF),
         b_x=((p.nz, p.in_rows, 4 * ln), BF),
         b_dbr=((4 * ln, w), BF),
-        b_dh=((4 * ln, ff), BF),
+        b_dh=((4 * ln, 3 * w), BF),
         b_sm=((4, 8, w), F32),
         sm_tot=((8, w), F32),
         sm_all=((8, w), F32),
         r_sm=((p.nz, 8, w), F32),
-        r_in=((p.nz, p.in_rows, ff), BF),
-        r_out=((p.nz, p.out_rows, w), BF),
+        r_in=((4, p.in_rows, ff), BF),
+        x_all=((2, p.nz, 2, ln, w), BF),
+        db_all=((2, p.nz, 2, ln, w), BF),
+        w_col=((w, p.out_rows), F32),
+        w_send=((p.n_dp, p.in_rows, p.out_rows), BF),
+        r_col=((p.n_dp, p.in_rows, p.out_rows), BF),
+        ch_own=((mp, w), BF),
+        ch_two=((mp, w), BF),
         ch_all=((2, p.n_dp, mp, w), BF),
         de_all=((2, p.n_dp, ln, w), BF),
     )
@@ -587,22 +589,9 @@
 
     barrier = pltpu.get_barrier_semaphore()
     peers = [(s, lax.rem(dp + k, n_dp)) for k in range(1, n_dp)]
-    peers += [(core, dp), (across, dp), (core, ydp)]
+    peers += [(core, dp), (across, dp), (3 - s, dp), (core, ydp)]
     for peer in peers:
         pl.semaphore_signal(barrier, inc=1, device_id=peer, device_id_type=MESH)
-    pl.semaphore_wait(barrier, len(peers))
-
-    k_wa, k_w1, k_w2, k_pa, k_pf = (recvs.take() for _ in range(5))
-
-    def weights(cond_att, cond_ff):
-        send(cond_att, r.par_a, r.par_a, (core, dp), k_pa)
-        send(cond_att, w_in_h.at[0], r.wa, (core, dp), k_wa)
-        if cond_ff is not None:
-            send(cond_ff, r.par_f, r.par_f, (core, dp), k_pf)
-            send(cond_ff, w_in_h.at[0], r.w1, (core, dp), k_w1)
-            send(cond_ff, w_out_h.at[0], r.w2, (core, dp), k_w2)
-
-    weights(is_att & at_x0, None)
 
     cols = [column(tok[m]) for m in range(2)]
     first = s * p.quarter
@@ -618,20 +607,47 @@
             r.acc[...] = part
         else:
             r.acc[...] += part
-    k_p = recvs.take(2)
     r.psend[...] = r.acc[pl.ds(pl.multiple_of(ln * other, ln), ln), :].astype(BF)
+
+    tiles = ff // w
+    k_p, k_g = recvs.take(2), recvs.take(2)
+    k_pa, k_pf, k_wa, k_w1, k_w2 = recvs.take(), recvs.take(), recvs.take(tiles), recvs.take(tiles), recvs.take(tiles)
+    pl.semaphore_wait(barrier, len(peers))
     send(None, r.psend, r.prow.at[0], (core, dp), k_p)
-    weights(is_att & at_x1, is_ff)
+
 
     r.lgp[...] = jnp.zeros(r.lgp.shape, BF)
     r.lgp[0 : p.masks] = lg[0, 0]
     r.lgp[mp : mp + p.masks] = lg[1, 0]
+
+    k_lg, k_id = recvs.take(n_dp), recvs.take(n_dp)
+    for j in range(n_dp):
+        r.lgs[j, :, p.share :] = jnp.zeros((2 * p.masks, p.share_pad - p.share), BF)
+        for m in range(2):
+            r.lgs[j, p.masks * m : p.masks * (m + 1), 0 : p.share] = lg[m, 0, :, p.share * j : p.share * (j + 1)]
+    r.ids_own[...] = jnp.zeros(r.ids_own.shape, jnp.int32)
+    for m in range(2):
+        r.ids_own[m : m + 1, :] = tok[m]
+    r.ids_all[dp] = r.ids_own[...]
+    r.lgr[dp] = r.lgs[dp]
+    for k in range(1, n_dp):
+        to = lax.rem(dp + k, n_dp)
+        send(None, r.lgs.at[to], r.lgr.at[dp], (s, to), k_lg + dp)
+        send(None, r.ids_own, r.ids_all.at[dp], (s, to), k_id + dp)
     arrived(r.prow.at[0], k_p)
     own_rows = r.acc[pl.ds(pl.multiple_of(ln * c, ln), ln), :]
     r.acc[0:ln, :] = own_rows + r.prow[0].astype(F32)
-
     r.psum[...] = r.acc[0:ln, :].astype(BF)
     send(at_x1, r.psum, r.prow.at[1], (across, dp), k_p + 1)
+
+    send(is_att, r.par_a, r.par_a, (core, dp), k_pa)
+    send(is_ff, r.par_f, r.par_f, (core, dp), k_pf)
+    for j in range(tiles):
+        cut = slice(j * w, (j + 1) * w)
+        send(is_att, w_in_h.at[0, :, cut], r.wa.at[:, cut], (core, dp), k_wa + j)
+        send(is_ff, w_in_h.at[0, :, cut], r.w1.at[:, cut], (core, dp), k_w1 + j)
+        send(is_ff, w_out_h.at[0, cut, :], r.w2.at[cut, :], (core, dp), k_w2 + j)
+
 
     for i, (at, size) in enumerate(p.chunks):
         part = mm(r.lgp[:, at : at + size], r.emb[at : at + size, :])
@@ -639,29 +655,14 @@
             r.g[...] = part
         else:
             r.g[...] += part
-    k_g = recvs.take(2)
     send(None, r.g.at[pl.ds(pl.multiple_of(mp * other, mp), p.masks)], r.grow.at[0], (core, dp), k_g)
 
-    r.lgs[...] = jnp.zeros(r.lgs.shape, BF)
-    for j in range(n_dp):
-        for m in range(2):
-            r.lgs[j, m, :, 0 : p.share] = r.lgp[mp * m : mp * m + mp, p.share * j : p.share * (j + 1)]
-    r.ids_own[...] = jnp.zeros(r.ids_own.shape, jnp.int32)
-    for m in range(2):
-        r.ids_own[m : m + 1, :] = tok[m]
-    r.ids_all[dp] = r.ids_own[...]
-    k_lg, k_id = recvs.take(n_dp), recvs.take(n_dp)
-    r.lgr[:, dp] = r.lgs[dp]
-    for k in range(1, n_dp):
-        to = lax.rem(dp + k, n_dp)
-        send(None, r.lgs.at[to], r.lgr.at[:, dp], (s, to), k_lg + dp)
-        send(None, r.ids_own, r.ids_all.at[dp], (s, to), k_id + dp)
-
-    arrived(r.grow.at[0], k_g)
-    own_g = r.g[pl.ds(pl.multiple_of(mp * c, mp), p.masks), :] + r.grow[0]
-    r.gwide[...] = jnp.zeros(r.gwide.shape, F32)
-    r.gwide[0 : p.masks, :] = own_g
-    send(at_x0, r.gwide.at[0 : p.masks], r.grow.at[1], (across, dp), k_g + 1)
+    def masked_gradient():
+        arrived(r.grow.at[0], k_g)
+        r.gwide[...] = jnp.zeros(r.gwide.shape, F32)
+        r.gwide[0 : p.masks, :] = r.g[pl.ds(pl.multiple_of(mp * c, mp), p.masks), :] + r.grow[0]
+
+    pl.when(at_x1)(masked_gradient)
 
     k_x = recvs.take()
 
@@ -678,8 +679,9 @@
 
     @pl.when(is_ff)
     def _():
+        pltpu.make_async_copy(w_in_h.at[0], r.w1, ls.at[l_w]).wait()
+        pltpu.make_async_copy(w_out_h.at[0], r.w2, ls.at[l_w + 1]).wait()
         arrived(r.par_a, k_pa)
-        arrived(r.wa, k_wa)
 
     @pl.when(at_x1)
     def _():
@@ -694,16 +696,19 @@
     def stack(block):
         return jnp.concatenate([block[:, 0:128], block[:, 128:256]], 0)
 
-    def norm_forward(resid, par, n_ref, inv_ref):
+    def norm_forward(resid, par):
         centred = resid - jnp.mean(resid, -1, keepdims=True)
         inverse = lax.rsqrt(jnp.mean(centred * centred, -1, keepdims=True) + EPSILON)
         normed = centred * inverse
-        n_ref[...] = normed
-        inv_ref[...] = inverse
-        return (normed * par[2:3, 0:w] + par[3:4, 0:w]).astype(BF)
+        return (normed * par[2:3, 0:w] + par[3:4, 0:w]).astype(BF), normed, inverse
 
     rows_x = r.x_a[...]
+
+    def wa_tile(j):
+        pl.when(is_ff)(lambda: arrived(r.wa.at[:, j * w : (j + 1) * w], k_wa + j))
+
     for j in range(3):
+        wa_tile(j)
         part = mm(rows_x, r.wa[:, j * w : (j + 1) * w])
         if j != 1:
             part = part + r.par_a[0:1, j * w : (j + 1) * w]
@@ -725,43 +730,29 @@
         chance = jnp.concatenate(chance, 1)
         r.probs[h] = chance
         r.ctx[:, at : at + 128] = mm(chance.astype(BF), value).astype(BF)
+    wa_tile(3)
     resid = rows_x.astype(F32) + mm(r.ctx[...], r.wa[:, 3 * w : 4 * w]) + r.par_a[1:2, 0:w]
-    r.x_f[...] = norm_forward(resid, r.par_a, r.n_a, r.inv_a)
-
-    @pl.when(is_ff)
-    def _():
-        pltpu.make_async_copy(w_in_h.at[0], r.w1, ls.at[l_w]).wait()
-        pltpu.make_async_copy(w_out_h.at[0], r.w2, ls.at[l_w + 1]).wait()
-
-    @pl.when(is_att)
-    def _():
-        arrived(r.w1, k_w1)
-        arrived(r.w2, k_w2)
-
-    rows_x = r.x_f[...]
-    total = rows_x.astype(F32) + r.par_f[1:2, 0:w]
-    for j in range(ff // w):
-        cut = slice(j * w, (j + 1) * w)
-        hidden = mm(rows_x, r.w1[:, cut]) + r.par_f[0:1, cut]
-        below = 0.5 + 0.5 * lax.erf(hidden * (0.5**0.5))
-        active = (hidden * below).astype(BF)
-        r.hid[:, cut] = hidden
-        r.phi[:, cut] = below
-        r.act[:, cut] = active
-        total = total + mm(active, r.w2[cut, :])
-    r.y_f[...] = norm_forward(total, r.par_f, r.n_f, r.inv_f)
-    send(at_x0, r.y_f, r.x_a, (across, dp), k_x)
-
-    def line(buf, base):
+    r.x_f[...], r.n_a[...], r.inv_a[...] = norm_forward(resid, r.par_a)
+
+    def line(buf, base, cond=True, owner=None):
         own = buf(dp)
-        send(None, own, own, (s, ydp), base + dp)
-        send(z < nz - 1, own, own, (s, dp + 2), base + dp)
-        send(z > 0, own, own, (s, dp - 2), base + dp)
-
-    def line_step(buf, base, t):
+        send(cond & (z < nz - 1), own, own, (s, dp + 2), base + dp)
+        send(cond & (z > 0), own, own, (s, dp - 2), base + dp)
+        to_y(buf, base, dp, cond, owner)
+
+    def to_y(buf, base, i, cond, owner):
+        piece = buf(i)
+        if owner is None:
+            send(None if cond is True else cond, piece, piece, (s, ydp), base + i)
+        else:
+            whose = jnp.where(is_att, core, s)
+            send(None if cond is True else cond, piece, piece, (whose, ydp), jnp.where(is_att, owner, base) + i)
+            send(is_att & cond, piece, piece, (core, dp), owner + i)
+
+    def line_step(buf, base, t, cond=True, owner=None, on_x=None):
         for sign in (-1, 1):
             from_z = z + sign * t
-            here = (from_z >= 0) & (from_z < nz)
+            here = (from_z >= 0) & (from_z < nz) & cond
             from_dp = jnp.clip(from_z, 0, nz - 1) * 2 + y
             piece = buf(from_dp)
             pl.when(here)(lambda piece=piece, from_dp=from_dp: arrived(piece, base + from_dp))
@@ -769,47 +760,100 @@
             on = here & (to_z >= 0) & (to_z < nz)
             if t < nz - 1:
                 send(on, piece, piece, (s, dp - 2 * sign), base + from_dp)
-            send(here, piece, piece, (s, ydp), base + from_dp)
-
-    def line_end(buf, base):
-        for zz in range(nz):
-            from_dp = 2 * zz + 1 - y
-            arrived(buf(from_dp), base + from_dp)
-
-    k_ch, k_chx, k_de, k_dex = recvs.take(n_dp), recvs.take(), recvs.take(n_dp), recvs.take()
+            to_y(buf, base, from_dp, here, owner)
+            if on_x is not None:
+                send(here, piece, piece, (across, dp), on_x + from_dp)
+
+    def line_y(buf, base, t, cond=True, on_x=None):
+        for sign in (-1, 1) if t else (1,):
+            from_z = z + sign * t
+            here = (from_z >= 0) & (from_z < nz) & cond
+            from_dp = jnp.clip(from_z, 0, nz - 1) * 2 + 1 - y
+            piece = buf(from_dp)
+            pl.when(here)(lambda piece=piece, from_dp=from_dp: arrived(piece, base + from_dp))
+            if on_x is not None:
+                send(here, piece, piece, (across, dp), on_x + from_dp)
 
     def ch(i):
         return r.ch_all.at[c, i]
 
     def de(i):
         return r.de_all.at[c, i]
+
+    def xs(i):
+        return r.x_all.at[c, i // 2, lax.rem(i, 2)]
+
+    def db(i):
+        return r.db_all.at[c, i // 2, lax.rem(i, 2)]
+
+    k_ch, k_de, k_xs, k_db = (recvs.take(n_dp) for _ in range(4))
+    k_cho, k_chc, k_cha, k_chx, k_dex = (recvs.take() for _ in range(5))
+    k_xsc, k_dbc = recvs.take(n_dp), recvs.take(n_dp)
+
+    r.x_all[c, z, y] = r.x_f[...]
+    line(xs, k_xs, True, k_xsc)
+
+    def feed(rows_x, keep=True):
+        total = rows_x.astype(F32) + r.par_f[1:2, 0:w]
+        for j in range(tiles):
+            cut = slice(j * w, (j + 1) * w)
+
+            @pl.when(is_att)
+            def _():
+                arrived(r.w1.at[:, cut], k_w1 + j)
+                arrived(r.w2.at[cut, :], k_w2 + j)
+
+            hidden = mm(rows_x, r.w1[:, cut]) + r.par_f[0:1, cut]
+            below = 0.5 + 0.5 * lax.erf(hidden * (0.5**0.5))
+            total = total + mm((hidden * below).astype(BF), r.w2[cut, :])
+            if keep:
+                slope = below + hidden * (0.3989422804014327 * jnp.exp(-0.5 * hidden * hidden))
+                r.slope[:, cut] = slope.astype(BF)
+        result, normed, inverse = norm_forward(total, r.par_f)
+        if keep:
+            r.y_f[...], r.n_f[...], r.inv_f[...] = result, normed, inverse
+        else:
+            r.y_o[...] = result
+
+    pl.when(is_ff | at_x1)(lambda: feed(r.x_f[...]))
+    send(at_x0 & is_ff, r.y_f, r.x_a, (across, dp), k_x)
+
+    @pl.when(at_x0 & is_ff)
+    def _():
+        arrived(r.x_all.at[0, z, y], k_xsc + dp)
+        feed(r.x_all[0, z, y], False)
+
+    send(at_x0 & is_ff, r.y_o, r.x_a, (3 - s, dp), k_x)
 
     @pl.when(at_x1)
     def _():
         r.mrow[...] = jnp.full(r.mrow.shape, -1, jnp.int32)
         r.mrow[0:1, 0 : p.masks] = picks[c]
         places = jnp.where(iota((ln, ln), 0) == r.mrow[0:1, :], 1.0, 0.0).astype(BF)
-        r.ch_all[c, dp] = mm_tn(places, r.y_f[...])[0:mp].astype(BF)
+        r.ch_own[...] = mm_tn(places, r.y_f[...])[0:mp].astype(BF)
         arrived(r.grow.at[1], k_g + 1)
         r.gwide[0 : p.masks, :] += r.grow[1]
         coarse = r.gwide[...].astype(BF)
         fine = (r.gwide[...] - coarse.astype(F32)).astype(BF)
         r.dyf[...] = mm(places, coarse) + mm(places, fine)
 
-    send(at_x1, ch(dp), ch(dp), (across, dp), k_ch + dp)
-
-    def push(owner, kind, src, dst):
+    send(at_x1, r.ch_own, r.ch_own, (across, dp), k_cho)
+    send(at_x1, r.ch_own, r.ch_two, (core, dp), k_chc)
+
+    def push(owner, kind, src, dst, cond=None):
         home = c == owner
         slot_y = 2 + jnp.where(home, 0, 1)
         own_dst, near_dst, far_dst = dst(0), dst(1), dst(slot_y)
 
-        @pl.when(home)
+        away = jnp.logical_not(home)
+
+        @pl.when(home if cond is None else home & cond)
         def _():
             pltpu.make_async_copy(src(y), own_dst, rs.at[kind]).start()
 
-        send(jnp.logical_not(home), src(y), near_dst, (core, dp), kind + 1)
+        send(away if cond is None else away & cond, src(y), near_dst, (core, dp), kind + 1)
         far_s = jnp.where(home, s, core)
-        send(None, src(1 - y), far_dst, (far_s, ydp), kind + slot_y)
+        send(cond, src(1 - y), far_dst, (far_s, ydp), kind + slot_y)
 
     def gathered(kind, dst):
         pltpu.make_async_copy(dst(0), dst(0), rs.at[kind]).wait()
@@ -819,40 +863,64 @@
     def lanes(slot):
         return pl.ds(slot * ln if isinstance(slot, int) else pl.multiple_of(slot * ln, ln), ln)
 
-    tiles = ff // w
-    k_dh = [recvs.take(4) for _ in range(tiles)]
-    k_act, k_xt, k_db, k_sm = (recvs.take(4) for _ in range(4))
+    k_dh = [recvs.take(4) for _ in range(3)]
+    k_ctx, k_xt, k_dba, k_sm = (recvs.take(4) for _ in range(4))
     to_x = lambda slot: r.b_x.at[:, :, lanes(slot)]
-    to_act = lambda slot: r.b_act.at[:, :, lanes(slot)]
-    to_ctx = lambda slot: r.b_act.at[:, 0 : p.in_rows, lanes(slot)]
+    to_ctx = lambda slot: r.b_ctx.at[:, :, lanes(slot)]
     to_dbr = lambda slot: r.b_dbr.at[lanes(slot), :]
     to_sm = lambda slot: r.b_sm.at[slot]
 
     def to_dh(j):
         return lambda slot: r.b_dh.at[lanes(slot), j * w : (j + 1) * w]
 
-    def blocks(dst, value, rows):
-        turned = value.T
-        for b in range(n_dp):
-            dst[b // 2, b % 2] = turned[b * rows : (b + 1) * rows]
-
-    def prepare():
-        blocks(r.xt_a, r.x_a[...], p.in_rows)
-        blocks(r.ct_a, r.ctx[...], p.in_rows)
-        blocks(r.xt_f, r.x_f[...], p.in_rows)
-        blocks(r.at_f, r.act[...], p.out_rows)
-
-    prepare()
-    push(0, k_xt, lambda i: r.xt_a.at[:, i], to_x)
-    push(0, k_act, lambda i: r.ct_a.at[:, i], to_ctx)
-    push(1, k_xt, lambda i: r.xt_f.at[:, i], to_x)
-    push(1, k_act, lambda i: r.at_f.at[:, i], to_act)
+    def push_dh(j):
+        push(0, k_dh[j], lambda i: r.dpk.at[:, j * w : (j + 1) * w], to_dh(j))
+
+    def push_rows(cond):
+        push(0, k_xt, lambda i: r.xt_a.at[:, i], to_x, cond)
+        push(0, k_ctx, lambda i: r.ct_a.at[:, i], to_ctx, cond)
+
+    def turn():
+        for dst, src in ((r.xt_a, r.x_a), (r.ct_a, r.ctx)):
+            turned = src[...].T
+            for b in range(n_dp):
+                dst[b // 2, b % 2] = turned[b * p.in_rows : (b + 1) * p.in_rows]
 
     @pl.when(at_x0)
     def _():
-        arrived(ch(dp), k_ch + dp)
-
-    line(ch, k_ch)
+        masked_gradient()
+        turn()
+
+    send(at_x0, r.gwide.at[0 : p.masks], r.grow.at[1], (across, dp), k_g + 1)
+    push_rows(at_x0)
+
+    @pl.when(at_x0 & is_att)
+    def _():
+        feed(r.x_f[...])
+
+    line_step(xs, k_xs, 1, at_x0, k_xsc)
+    line_step(xs, k_xs, 2, at_x0, k_xsc)
+
+    @pl.when(at_x0)
+    def _():
+        arrived(r.ch_own, k_cho)
+        r.ch_all[c, dp] = r.ch_own[...]
+
+    send(at_x0, r.ch_own, r.ch_two, (core, dp), k_chc)
+    for k in range(1, n_dp):
+        send(at_x0, r.ch_own, ch(dp), (s, lax.rem(dp + k, n_dp)), k_ch + dp)
+
+    def logits():
+        arrived(r.ch_two, k_chc)
+        chosen = jnp.concatenate([r.ch_own[...], r.ch_two[...]], 0)
+        for at, size in p.chunks:
+            part = mm_nt(chosen, r.emb[at : at + size, :])
+            o_log[c, 0, :, at : at + size] = part[0 : p.masks]
+            o_log[other, 0, :, at : at + size] = part[mp : mp + p.masks]
+
+    pl.when(at_x0)(logits)
+    line_step(xs, k_xs, 3, at_x0, k_xsc)
+
     k_dy = recvs.take()
 
     @pl.when(at_x0)
@@ -880,27 +948,22 @@
 
     dres, gain_part, shift_part = norm_backward(r.par_f, r.n_f, r.inv_f)
     r.dres[...] = dres
-    r.dbr_f[...] = dres.astype(BF)
-    push(1, k_db, lambda i: r.dbr_f, to_dbr)
-    branch = r.dbr_f[...]
+    r.db_all[c, z, y] = dres.astype(BF)
+    line(db, k_db, True, k_dbc)
+    branch = r.db_all[c, z, y]
     total = r.dres[...]
     for j in range(tiles):
         cut = slice(j * w, (j + 1) * w)
-        hidden = r.hid[:, cut]
-        slope = r.phi[:, cut] + hidden * (0.3989422804014327 * jnp.exp(-0.5 * hidden * hidden))
-        dhidden = (mm_nt(branch, r.w2[cut, :]) * slope).astype(BF)
-        r.dh[:, cut] = dhidden
-        push(1, k_dh[j], lambda i, cut=cut: r.dh.at[:, cut], to_dh(j))
+        dhidden = (mm_nt(branch, r.w2[cut, :]) * r.slope[:, cut].astype(F32)).astype(BF)
         r.bsum[:, cut] = jnp.sum(dhidden.astype(F32), 0, keepdims=True)
         total = total + mm_nt(dhidden, r.w1[:, cut])
     r.dyf[...] = total.astype(BF).astype(F32)
     small(r.sm_f, jnp.sum(branch.astype(F32), 0, keepdims=True), gain_part, shift_part)
-    push(1, k_sm, lambda i: r.sm_f, to_sm)
+    line_step(xs, k_xs, 1, at_x1, k_xsc)
 
     dres, gain_part, shift_part = norm_backward(r.par_a, r.n_a, r.inv_a)
     r.dres[...] = dres
     r.dbr_a[...] = dres.astype(BF)
-    push(0, k_db, lambda i: r.dbr_a, to_dbr)
     branch = r.dbr_a[...]
     r.dctx[...] = mm_nt(branch, r.wa[:, 3 * w : 4 * w]).astype(BF)
     for h in range(pairs):
@@ -920,127 +983,213 @@
         r.dpk[:, w + at : w + at + 128] = (mm_tn(stack(dscores), split(query)) * 0.125).astype(BF)
         r.dpk[:, 2 * w + at : 2 * w + at + 128] = mm_tn(stack(chance.astype(BF)), split(upper)).astype(BF)
     total = r.dres[...]
-    r.bsum[...] = jnp.zeros(r.bsum.shape, F32)
     for j in range(3):
         cut = slice(j * w, (j + 1) * w)
-        push(0, k_dh[j], lambda i, cut=cut: r.dpk.at[:, cut], to_dh(j))
-        dpart = r.dpk[:, cut]
-        if j != 1:
-            r.bsum[:, cut] = jnp.sum(dpart.astype(F32), 0, keepdims=True)
-        total = total + mm_nt(dpart, r.wa[:, cut])
+        total = total + mm_nt(r.dpk[:, cut], r.wa[:, cut])
     r.dx[...] = total.astype(BF)
     send(at_x1, r.dx, r.dyin, (across, dp), k_dy)
 
+    gathers = c == 1 - x
+
     @pl.when(at_x0)
     def _():
         r.de_all[c, dp] = r.dx[...]
 
-    send(at_x0, r.dx, de(dp), (across, dp), k_de + dp)
+    send(at_x0, de(dp), de(dp), (across, dp), k_de + dp)
+    line(de, k_de, at_x0 & is_ff)
+
+    line_step(xs, k_xs, 2, at_x1, k_xsc)
+    line_step(db, k_db, 1, True, k_dbc)
+    pl.when(at_x1)(turn)
+    push_rows(at_x1)
+    push(0, k_dba, lambda i: r.dbr_a, to_dbr)
+    push_dh(0)
+    push(1, k_sm, lambda i: r.sm_f, to_sm)
+
+    @pl.when(at_x0)
+    def _():
+        for k in range(1, n_dp):
+            arrived(ch(lax.rem(dp + k, n_dp)), k_ch + lax.rem(dp + k, n_dp))
+
+    send(at_x0, r.ch_all.at[c], r.ch_all.at[c], (across, dp), k_cha)
+    send(at_x0, r.ch_all.at[c], r.ch_all.at[c], (core, dp), k_chx)
+    r.bsum[...] = jnp.zeros(r.bsum.shape, F32)
+    for j in (0, 2):
+        cut = slice(j * w, (j + 1) * w)
+        r.bsum[:, cut] = jnp.sum(r.dpk[:, cut].astype(F32), 0, keepdims=True)
     small(r.sm_a, jnp.sum(branch.astype(F32), 0, keepdims=True), gain_part, shift_part)
     push(0, k_sm, lambda i: r.sm_a, to_sm)
-
-    k_in = [recvs.take(nz) for _ in range(tiles)]
-    k_out, k_smz = recvs.take(nz), recvs.take(nz)
+    line_step(xs, k_xs, 3, at_x1, k_xsc)
+    line_step(db, k_db, 2, True, k_dbc)
+    push_dh(1)
+    line_step(de, k_de, 1, at_x0 & is_ff, None, k_de)
+    line_step(db, k_db, 3, True, k_dbc)
+    push_dh(2)
+    line_step(de, k_de, 2, at_x0 & is_ff, None, k_de)
+    line_step(de, k_de, 3, at_x0 & is_ff, None, k_de)
+
+    def head_part():
+        arrived(r.ch_all.at[other], k_chx)
+        for k in range(1, n_dp):
+            src = lax.rem(dp + k, n_dp)
+            arrived(r.lgr.at[src], k_lg + src)
+            arrived(r.ids_all.at[src], k_id + src)
+        for i in range(n_dp):
+            for m in range(2):
+                r.ch_pack[i, p.masks * m : p.masks * (m + 1)] = r.ch_all[m, i, 0 : p.masks]
+        lines = 2 * n_dp * p.masks
+        grad = mm_tn(r.lgr[...].reshape(lines, p.share_pad), r.ch_pack[...].reshape(lines, w))
+        o_tab[...] = grad[0 : p.share]
+
+    @pl.when(at_x1 & is_att)
+    def _():
+        arrived(de(dp), k_de + dp)
+
+    line(de, k_de, at_x1 & is_att)
+    pl.when(at_x1)(logits)
+
+    k_in = [recvs.take(4) for _ in range(tiles)]
     half = nz * p.in_rows
-
-    def spread(cond, src, dst, base):
-        for k in range(1, nz):
-            zz = lax.rem(z + k, nz)
-            send(cond, src(zz), dst, (s, 2 * zz + y), base + z)
-
-    @pl.when(is_ff)
-    def _():
-        gathered(k_act, to_act)
-        gathered(k_db, to_dbr)
-        for zz in range(nz):
-            grad = mm(r.b_act[zz], r.b_dbr[...])
-            r.w2[zz * p.out_rows : (zz + 1) * p.out_rows, :] = grad.astype(BF)
-        r.r_out[z] = r.w2[pl.ds(pl.multiple_of(z * p.out_rows, p.out_rows), p.out_rows), :]
-
-    def out_part(zz):
-        return r.w2.at[pl.ds(pl.multiple_of(zz * p.out_rows, p.out_rows), p.out_rows)]
-
-    spread(is_ff, out_part, r.r_out.at[z], k_out)
-
-    @pl.when(is_ff)
-    def _():
-        gathered(k_xt, to_x)
-
-    @pl.when(is_att)
-    def _():
-        gathered(k_xt, to_x)
-        gathered(k_act, to_ctx)
-        gathered(k_db, to_dbr)
-
-    for j in (3, 0, 1, 2):
-        cut = slice(j * w, (j + 1) * w)
-
-        def keep(grad, cut=cut):
-            r.wa[0:half, cut] = grad.astype(BF)
-            r.r_in[z, :, cut] = r.wa[pl.ds(pl.multiple_of(z * p.in_rows, p.in_rows), p.in_rows), cut]
-
-        @pl.when(is_ff)
-        def _():
-            gathered(k_dh[j], to_dh(j))
-            keep(mm(r.b_x[...].reshape(half, 4 * ln), r.b_dh[:, cut]))
+    outer = (z == 0) | (z == nz - 1)
+    mate = z + 1 - 2 * lax.rem(z, 2)
+    far_base = 2 - 2 * (z // 2)
+
+    def shard(zz, cut):
+        return r.wa.at[pl.ds(pl.multiple_of(zz * p.in_rows, p.in_rows), p.in_rows), cut]
+
+    def tile_cut(j):
+        return slice(j * w, (j + 1) * w)
+
+    def attention_tile(j):
+        cut = tile_cut(j)
 
         @pl.when(is_att)
         def _():
             if j == 3:
-                keep(mm(r.b_act[:, 0 : p.in_rows].reshape(half, 4 * ln), r.b_dbr[...]))
+                gathered(k_ctx, to_ctx)
+                gathered(k_dba, to_dbr)
+                grad = mm(r.b_ctx[...].reshape(half, 4 * ln), r.b_dbr[...])
             else:
+                if j == 0:
+                    gathered(k_xt, to_x)
                 gathered(k_dh[j], to_dh(j))
-                keep(mm(r.b_x[...].reshape(half, 4 * ln), r.b_dh[:, cut]))
-
-        def in_part(zz, cut=cut):
-            return r.wa.at[pl.ds(pl.multiple_of(zz * p.in_rows, p.in_rows), p.in_rows), cut]
-
-        spread(None, in_part, r.r_in.at[z, :, cut], k_in[j])
-
+                grad = mm(r.b_x[...].reshape(half, 4 * ln), r.b_dh[:, cut])
+            r.wa[0:half, cut] = grad.astype(BF)
+
+        to_mate = (s, 2 * mate + y)
+        for k in range(2):
+            send(is_att & outer, shard(far_base + k, cut), r.r_in.at[2 + k, :, cut], to_mate, k_in[j] + 2 + k)
+        send(is_att, shard(mate, cut), r.r_in.at[0, :, cut], to_mate, k_in[j])
+
+    def attention_sum(j):
+        cut = tile_cut(j)
+        inner = is_att & jnp.logical_not(outer)
+        for k in range(2):
+
+            @pl.when(inner)
+            def _():
+                arrived(r.r_in.at[2 + k, :, cut], k_in[j] + 2 + k)
+                rows = pl.ds(pl.multiple_of((far_base + k) * p.in_rows, p.in_rows), p.in_rows)
+                r.wa[rows, cut] = (r.wa[rows, cut].astype(F32) + r.r_in[2 + k, :, cut].astype(F32)).astype(BF)
+
+            send(inner, shard(far_base + k, cut), r.r_in.at[1, :, cut], (s, 2 * (far_base + k) + y), k_in[j] + 1)
+
+    attention_tile(3)
+    line_step(de, k_de, 1, at_x1 & is_att, None, k_de)
+    attention_tile(0)
+    attention_sum(3)
+    line_step(de, k_de, 2, at_x1 & is_att, None, k_de)
+
+    k_col = recvs.take(n_dp)
+    mine_in = pl.ds(pl.multiple_of(dp * p.out_rows, p.out_rows), p.out_rows)
+
+    def unit_grads(yy, i):
+        def four(buf):
+            return jnp.concatenate([buf[m, 2 * i + k, yy] for m in range(2) for k in range(2)], 0)
+
+        rows_x, up = four(r.x_all), four(r.db_all)
+        hidden = mm(rows_x, r.w1[:, mine_in]) + r.par_f[0:1, mine_in]
+        below = 0.5 + 0.5 * lax.erf(hidden * (0.5**0.5))
+        slope = below + hidden * (0.3989422804014327 * jnp.exp(-0.5 * hidden * hidden))
+        dhidden = (mm_nt(up, r.w2[mine_in, :]) * slope).astype(BF)
+        o_wout[0] += mm_tn((hidden * below).astype(BF), up)
+        r.w_col[...] += mm_tn(rows_x, dhidden)
+
+    def units_of(yy):
+        for zz in range(nz):
+            i = 2 * zz + yy
+            pl.when((i != dp) | at_x1)(lambda i=i: arrived(r.x_all.at[0, i // 2, lax.rem(i, 2)], k_xsc + i))
+            arrived(r.db_all.at[0, i // 2, lax.rem(i, 2)], k_dbc + i)
+        lax.fori_loop(0, nz // 2, lambda i, carry: (unit_grads(yy, i), carry)[1], 0)
+
+    @pl.when(is_ff)
+    def _():
+        o_wout[...] = jnp.zeros(o_wout.shape, F32)
+        r.w_col[...] = jnp.zeros(r.w_col.shape, F32)
+        units_of(y)
+
+    k_smz = recvs.take(nz)
     gathered(k_sm, to_sm)
     r.sm_tot[...] = r.b_sm[0] + r.b_sm[1] + r.b_sm[2] + r.b_sm[3]
     r.r_sm[z] = r.sm_tot[...]
-    spread(None, lambda zz: r.sm_tot, r.r_sm.at[z], k_smz)
+    for k in range(1, nz):
+        zz = lax.rem(z + k, nz)
+        send(None, r.sm_tot, r.r_sm.at[z], (s, 2 * zz + y), k_smz + z)
+
+    attention_tile(1)
+    attention_sum(0)
+    line_step(de, k_de, 3, at_x1 & is_att, None, k_de)
+    line_y(de, k_de, 0, gathers, k_de)
+    line_y(de, k_de, 1, gathers, k_de)
+    attention_tile(2)
+    attention_sum(1)
+
+    @pl.when(is_ff)
+    def _():
+        for t in range(nz):
+            line_y(xs, k_xs, t)
+        for t in range(nz):
+            line_y(db, k_db, t)
+        units_of(1 - y)
+        for k in range(n_dp):
+            r.w_send[k] = r.w_col[k * p.in_rows : (k + 1) * p.in_rows, :].astype(BF)
+        r.r_col[dp] = r.w_send[dp]
+
+    for k in range(1, n_dp):
+        to = lax.rem(dp + k, n_dp)
+        send(is_ff, r.w_send.at[to], r.r_col.at[dp], (s, to), k_col + dp)
+    line_y(de, k_de, 2, gathers, k_de)
+    line_y(de, k_de, 3, gathers, k_de)
+    attention_sum(2)
 
     @pl.when(at_x1)
     def _():
-        arrived(de(dp), k_de + dp)
-
-    line(de, k_de)
-    for t in range(1, nz):
-        line_step(ch, k_ch, t)
-        line_step(de, k_de, t)
-    line_end(ch, k_ch)
-    send(None, r.ch_all.at[c], r.ch_all.at[c], (core, dp), k_chx)
-    line_end(de, k_de)
+        arrived(r.ch_all.at[c], k_cha)
+
+    send(at_x1, r.ch_all.at[c], r.ch_all.at[c], (core, dp), k_chx)
+
+    head_part()
+
+    for i in range(n_dp):
+        pl.when(jnp.logical_not(gathers) & ((i != dp) | at_x1))(lambda i=i: arrived(de(i), k_de + i))
     send(None, r.de_all.at[c], r.de_all.at[c], (core, dp), k_dex)
 
-    arrived(r.ch_all.at[other], k_chx)
-    chosen = jnp.concatenate([r.ch_all[0, dp], r.ch_all[1, dp]], 0)
-    for at, size in p.chunks:
-        part = mm_nt(chosen, r.emb[at : at + size, :])
-        for m in range(2):
-            o_log[m, 0, :, at : at + size] = part[mp * m : mp * m + p.masks]
-    for k in range(1, n_dp):
-        src = lax.rem(dp + k, n_dp)
-        arrived(r.lgr.at[:, src], k_lg + src)
-        arrived(r.ids_all.at[src], k_id + src)
-    lines = 2 * n_dp * mp
-    grad = mm_tn(r.lgr[...].reshape(lines, p.share_pad), r.ch_all[...].reshape(lines, w))
-    o_tab[...] = grad[0 : p.share]
-
+    entry = iota((p.share_rows, ln), 0) + (s * p.quarter + dp * p.share)
+
+    def scatter(m):
+        def step(i, carry):
+            hot = []
+            for k in range(2):
+                hot.append(jnp.where(entry == r.ids_all[2 * i + k, pl.ds(m, 1), :], 1.0, 0.0).astype(BF))
+            rows = r.de_all[m, pl.ds(2 * i, 2)].reshape(2 * ln, w)
+            o_tab[...] += mm(jnp.concatenate(hot, 1), rows)[0 : p.share]
+            return carry
+
+        lax.fori_loop(0, n_dp // 2, step, 0)
+
+    scatter(c)
     arrived(r.de_all.at[other], k_dex)
-    entry = iota((p.share_rows, ln), 0) + (s * p.quarter + dp * p.share)
-
-    def scatter(i, carry):
-        hot = []
-        for m in range(2):
-            hot.append(jnp.where(entry == r.ids_all[i, m : m + 1, :], 1.0, 0.0).astype(BF))
-        rows = jnp.concatenate([r.de_all[0, i], r.de_all[1, i]], 0)
-        o_tab[...] += mm(jnp.concatenate(hot, 1), rows)[0 : p.share]
-        return carry
-
-    lax.fori_loop(0, n_dp, scatter, 0)
+    scatter(other)
     n_pos = ln // n_dp
     here = pl.ds(pl.multiple_of(dp * n_pos, n_pos), n_pos)
     total = jnp.zeros((n_pos, w), F32)
@@ -1049,28 +1198,24 @@
             total = total + r.de_all[m, i, here, :].astype(F32)
     o_pos[...] = total
 
-    for j in range(tiles):
-        for k in range(1, nz):
-            src = lax.rem(z + k, nz)
-            arrived(r.r_in.at[src, :, j * w : (j + 1) * w], k_in[j] + src)
-    total = r.r_in[0].astype(F32)
-    for zz in range(1, nz):
-        total = total + r.r_in[zz].astype(F32)
-    o_win[0] = total
+    @pl.when(is_att)
+    def _():
+        mine = pl.ds(pl.multiple_of(z * p.in_rows, p.in_rows), p.in_rows)
+        for j in (3, 0, 1, 2):
+            cut = tile_cut(j)
+            arrived(r.r_in.at[0, :, cut], k_in[j])
+            arrived(r.r_in.at[1, :, cut], k_in[j] + 1)
+            near_sum = r.wa[mine, cut].astype(F32) + r.r_in[0, :, cut].astype(F32)
+            o_win[0, :, cut] = near_sum + r.r_in[1, :, cut].astype(F32)
+        o_wout[...] = jnp.zeros(o_wout.shape, F32)
 
     @pl.when(is_ff)
     def _():
-        for k in range(1, nz):
-            src = lax.rem(z + k, nz)
-            arrived(r.r_out.at[src], k_out + src)
-        total = r.r_out[0].astype(F32)
-        for zz in range(1, nz):
-            total = total + r.r_out[zz].astype(F32)
-        o_wout[0] = total
-
-    @pl.when(is_att)
-    def _():
-        o_wout[...] = jnp.zeros(o_wout.shape, F32)
+        for k in range(1, n_dp):
+            src = lax.rem(dp + k, n_dp)
+            arrived(r.r_col.at[src], k_col + src)
+        for k in range(n_dp):
+            o_win[0, :, k * p.out_rows : (k + 1) * p.out_rows] = r.r_col[k].astype(F32)
 
     for k in range(1, nz):
         src = lax.rem(z + k, nz)

time: 183 us -> 123 us (0.67)
  Pallas kernels: 171 us -> 113 us
    pallas_call x1, Pallas kernels: 171 us -> 113 us  [whole(): pl.pallas_call(functools.partial(fused, p, list(scratch)), out_shape=[jax...]
where the time goes in v2:
time: 123 us
  Pallas kernels  113 us (92%)
  local copies, waits for them, and re-layouts  9.1 us (7%)
    pallas_call x1, Pallas kernels, whole(): pl.pallas_call(functools.partial(fused, p, list(scratch)), out_shape=[jax...  113 us
    unnamed x25, local copies, waits for them, and re-layouts  9.1 us

profile of v2, /device:TPU:1, one launch (start us, length us, event | category | flops | bytes accessed | tf_op | source)
XLA Modules:
  0.0 122.9 jit_solution(10186137070395083782)
XLA Ops:
  0.6 113.1 %shard_map.187 = (f32[2,1,40,3648]{3,2,1,0:T(8,128)}, f32[456,768]{1,0:T(8,128)}, f32[16,768]{1,0:T(8,128)}, f32[1,96,3072]{2,1,0:T(8,128)}, f32[1,384,768]{2,1,...) custom-call(s32[2,1,128]{2,1,0:T(1,128)} %refs_0_.1, ...), custom_call_target="tpu_custom_call" | custom-call | tf_op jit(solution)/shard_map/pallas_call | solution.py:1273
  113.8 0.0 copy-start
  113.8 2.5 %copy.30 = f32[2,1,40,3648]{3,2,1,0:T(8,128)} copy(f32[2,1,40,3648]{3,2,1,0:T(8,128)} %get-tuple-element.18) | data formatting | bytes 2334720
  116.3 0.0 copy-done
  116.3 0.0 copy-start.3
  116.3 0.0 copy-start.2
  116.3 1.1 copy.31
  117.4 0.0 copy-done.3
  117.4 0.6 copy.32
  118.0 0.1 copy-done.2
  118.1 0.0 copy-start.1
  118.1 1.0 copy.33
  119.1 0.7 copy-done.1
  119.8 0.0 copy-start.4
  119.8 0.0 copy-start.7
  119.8 0.0 copy-start.6
  119.8 0.0 copy-start.5
  119.8 1.0 copy.34
  120.8 0.0 copy-done.4
  120.8 0.6 copy.35
  121.4 0.0 copy-done.7
  121.4 0.5 copy.36
  121.9 0.0 copy-done.6
  121.9 0.5 copy.37
  122.4 0.0 copy-done.5
  122.4 0.5 copy.38
Async XLA Ops:
  113.8 2.5 %copy-start = (f32[456,768]{1,0:T(8,128)S(1)}, f32[456,768]{1,0:T(8,128)}, u32[]{:S(2)}) copy-start(f32[456,768]{1,0:T(8,128)} %get-tuple-element.19) | copy-start | bytes 4202500
  116.3 1.1 copy-start.3
  116.3 1.8 %copy-start.2 = (f32[1,96,3072]{2,1,0:T(8,128)S(1)}, f32[1,96,3072]{2,1,0:T(8,128)}, u32[]{:S(2)}) copy-start(f32[1,96,3072]{2,1,0:T(8,128)} %get-tuple-element.21) | copy-start | bytes 3538948
  118.1 1.7 %copy-start.1 = (f32[1,384,768]{2,1,0:T(8,128)S(1)}, f32[1,384,768]{2,1,0:T(8,128)}, u32[]{:S(2)}) copy-start(f32[1,384,768]{2,1,0:T(8,128)} %get-tuple-element.22) | copy-start | bytes 3538948
  119.8 1.0 copy-start.4
  119.8 1.6 %copy-start.7 = (f32[1,96]{1,0:T(1,128)S(1)}, f32[1,96]{1,0:T(1,128)}, u32[]{:S(2)}) copy-start(f32[1,96]{1,0:T(1,128)} %get-tuple-element.24) | copy-start | bytes 1156
  119.8 2.1 %copy-start.6 = (f32[1,96]{1,0:T(1,128)S(1)}, f32[1,96]{1,0:T(1,128)}, u32[]{:S(2)}) copy-start(f32[1,96]{1,0:T(1,128)} %get-tuple-element.25) | copy-start | bytes 1156
  119.8 2.6 %copy-start.5 = (f32[1,96]{1,0:T(1,128)S(1)}, f32[1,96]{1,0:T(1,128)}, u32[]{:S(2)}) copy-start(f32[1,96]{1,0:T(1,128)} %get-tuple-element.26) | copy-start | bytes 1156

commit v3 on v2

--- a/solution.py
+++ b/solution.py
@@ -384,7 +384,7 @@
     )
 
 
-SENDS = 230
+SENDS = 260
 RECVS = 160
 VMEM_LIMIT = 64 * 2**20
 BF = jnp.bfloat16
@@ -446,6 +446,8 @@
     mp = p.mask_pad
     return dict(
         emb=((p.quarter, w), BF),
+        lg=((2, 1, p.masks, p.quarter), BF),
+        pos=((ln, w), BF),
         wa=((w, ff), BF),
         w1=((w, ff), BF),
         w2=((ff, w), BF),
@@ -487,6 +489,7 @@
         dctx=((ln, w), BF),
         dx=((ln, w), BF),
         bsum=((1, ff), F32),
+        vecs=((8, w), F32),
         sm_a=((8, w), F32),
         sm_f=((8, w), F32),
         b_ctx=((p.nz, p.in_rows, 4 * ln), BF),
@@ -507,14 +510,21 @@
         ch_two=((mp, w), BF),
         ch_all=((2, p.n_dp, mp, w), BF),
         de_all=((2, p.n_dp, ln, w), BF),
+        u_out=((p.out_rows, w), F32),
+        o_log=((2, 1, p.masks, p.quarter), BF),
+        o_tab=((p.share, w), F32),
+        o_pos=((ln // p.n_dp, w), F32),
+        o_win=((1, p.in_rows, ff), BF),
+        o_wout=((1, p.out_rows, w), BF),
     )
 
 
 def fused(p, names, *refs):
-    (tok, seg, picks, lg, pos, b_in, b_out, gain, shift, emb_h, w_in_h, w_out_h) = refs[:12]
-    (o_log, o_tab, o_pos, o_win, o_wout, o_bin, o_bout, o_gain, o_shift) = refs[12:21]
-    r = types.SimpleNamespace(**dict(zip(names, refs[21:])))
-    ss, rs, ls = refs[21 + len(names) :]
+    (tok, seg, picks, b_in, b_out, gain, shift, lg_h, pos_h, emb_h, w_in_h, w_out_h) = refs[:12]
+    outs = refs[12:18]
+    r = types.SimpleNamespace(**dict(zip(names, refs[18:])))
+    ss, rs, ls, os = refs[18 + len(names) :]
+    (o_log, o_tab, o_pos, o_win, o_wout, o_vec) = (r.o_log, r.o_tab, r.o_pos, r.o_win, r.o_wout, r.sm_all)
     w, ff, ln, mp, nz, n_dp = p.width, p.ff, p.length, p.mask_pad, p.nz, p.n_dp
     heads = w // 64
     pairs = heads // 2
@@ -568,6 +578,9 @@
     for i, (at, size) in enumerate(p.chunks):
         pltpu.make_async_copy(emb_h.at[pl.ds(at, size)], r.emb.at[pl.ds(at, size)], ls.at[i]).start()
     l_w = len(p.chunks)
+    lg, pos = r.lg, r.pos
+    pltpu.make_async_copy(lg_h, lg, ls.at[l_w + 2]).start()
+    pltpu.make_async_copy(pos_h, pos, ls.at[l_w + 3]).start()
 
     @pl.when(is_att)
     def _():
@@ -616,6 +629,8 @@
     send(None, r.psend, r.prow.at[0], (core, dp), k_p)
 
 
+    pltpu.make_async_copy(lg_h, lg, ls.at[l_w + 2]).wait()
+    pltpu.make_async_copy(pos_h, pos, ls.at[l_w + 3]).wait()
     r.lgp[...] = jnp.zeros(r.lgp.shape, BF)
     r.lgp[0 : p.masks] = lg[0, 0]
     r.lgp[mp : mp + p.masks] = lg[1, 0]
@@ -640,14 +655,16 @@
     r.psum[...] = r.acc[0:ln, :].astype(BF)
     send(at_x1, r.psum, r.prow.at[1], (across, dp), k_p + 1)
 
-    send(is_att, r.par_a, r.par_a, (core, dp), k_pa)
-    send(is_ff, r.par_f, r.par_f, (core, dp), k_pf)
-    for j in range(tiles):
-        cut = slice(j * w, (j + 1) * w)
-        send(is_att, w_in_h.at[0, :, cut], r.wa.at[:, cut], (core, dp), k_wa + j)
-        send(is_ff, w_in_h.at[0, :, cut], r.w1.at[:, cut], (core, dp), k_w1 + j)
-        send(is_ff, w_out_h.at[0, cut, :], r.w2.at[cut, :], (core, dp), k_w2 + j)
-
+    def weights(cond):
+        send(is_att & cond, r.par_a, r.par_a, (core, dp), k_pa)
+        send(is_ff & cond, r.par_f, r.par_f, (core, dp), k_pf)
+        for j in range(tiles):
+            cut = slice(j * w, (j + 1) * w)
+            send(is_att & cond, w_in_h.at[0, :, cut], r.wa.at[:, cut], (core, dp), k_wa + j)
+            send(is_ff & cond, w_in_h.at[0, :, cut], r.w1.at[:, cut], (core, dp), k_w1 + j)
+            send(is_ff & cond, w_out_h.at[0, cut, :], r.w2.at[cut, :], (core, dp), k_w2 + j)
+
+    weights(at_x0)
 
     for i, (at, size) in enumerate(p.chunks):
         part = mm(r.lgp[:, at : at + size], r.emb[at : at + size, :])
@@ -663,6 +680,7 @@
         r.gwide[0 : p.masks, :] = r.g[pl.ds(pl.multiple_of(mp * c, mp), p.masks), :] + r.grow[0]
 
     pl.when(at_x1)(masked_gradient)
+    weights(at_x1)
 
     k_x = recvs.take()
 
@@ -749,7 +767,7 @@
             send(None if cond is True else cond, piece, piece, (whose, ydp), jnp.where(is_att, owner, base) + i)
             send(is_att & cond, piece, piece, (core, dp), owner + i)
 
-    def line_step(buf, base, t, cond=True, owner=None, on_x=None):
+    def line_step(buf, base, t, cond=True, owner=None):
         for sign in (-1, 1):
             from_z = z + sign * t
             here = (from_z >= 0) & (from_z < nz) & cond
@@ -761,17 +779,29 @@
             if t < nz - 1:
                 send(on, piece, piece, (s, dp - 2 * sign), base + from_dp)
             to_y(buf, base, from_dp, here, owner)
-            if on_x is not None:
-                send(here, piece, piece, (across, dp), on_x + from_dp)
-
-    def line_y(buf, base, t, cond=True, on_x=None):
+
+    def line_y(buf, base, t):
         for sign in (-1, 1) if t else (1,):
             from_z = z + sign * t
+            from_dp = jnp.clip(from_z, 0, nz - 1) * 2 + 1 - y
+            pl.when((from_z >= 0) & (from_z < nz))(lambda i=from_dp: arrived(buf(i), base + i))
+
+    def pair_line(buf, base, cond, i):
+        piece = buf(i)
+        send(cond & (z < nz - 1), piece, piece, (s, dp + 2), base + i)
+        send(cond & (z > 0), piece, piece, (s, dp - 2), base + i)
+
+    def pair_step(buf, base, t, cond, on_x):
+        for sign in (-1, 1):
+            from_z = z + sign * t
             here = (from_z >= 0) & (from_z < nz) & cond
-            from_dp = jnp.clip(from_z, 0, nz - 1) * 2 + 1 - y
-            piece = buf(from_dp)
-            pl.when(here)(lambda piece=piece, from_dp=from_dp: arrived(piece, base + from_dp))
-            if on_x is not None:
+            for side in (0, 1):
+                from_dp = jnp.clip(from_z, 0, nz - 1) * 2 + (1 - y if side else y)
+                piece = buf(from_dp)
+                pl.when(here)(lambda piece=piece, from_dp=from_dp: arrived(piece, base + from_dp))
+                if t < nz - 1:
+                    on = here & (z - sign >= 0) & (z - sign < nz)
+                    send(on, piece, piece, (s, dp - 2 * sign), base + from_dp)
                 send(here, piece, piece, (across, dp), on_x + from_dp)
 
     def ch(i):
@@ -910,16 +940,19 @@
     for k in range(1, n_dp):
         send(at_x0, r.ch_own, ch(dp), (s, lax.rem(dp + k, n_dp)), k_ch + dp)
 
+    def emit(i, src):
+        pltpu.make_async_copy(src, outs[i], os.at[i]).start()
+
     def logits():
         arrived(r.ch_two, k_chc)
         chosen = jnp.concatenate([r.ch_own[...], r.ch_two[...]], 0)
         for at, size in p.chunks:
             part = mm_nt(chosen, r.emb[at : at + size, :])
-            o_log[c, 0, :, at : at + size] = part[0 : p.masks]
-            o_log[other, 0, :, at : at + size] = part[mp : mp + p.masks]
+            o_log[c, 0, :, at : at + size] = part[0 : p.masks].astype(BF)
+            o_log[other, 0, :, at : at + size] = part[mp : mp + p.masks].astype(BF)
+        emit(0, o_log)
 
     pl.when(at_x0)(logits)
-    line_step(xs, k_xs, 3, at_x0, k_xsc)
 
     k_dy = recvs.take()
 
@@ -958,7 +991,7 @@
         r.bsum[:, cut] = jnp.sum(dhidden.astype(F32), 0, keepdims=True)
         total = total + mm_nt(dhidden, r.w1[:, cut])
     r.dyf[...] = total.astype(BF).astype(F32)
-    small(r.sm_f, jnp.sum(branch.astype(F32), 0, keepdims=True), gain_part, shift_part)
+    r.vecs[0:1], r.vecs[1:2] = gain_part, shift_part
     line_step(xs, k_xs, 1, at_x1, k_xsc)
 
     dres, gain_part, shift_part = norm_backward(r.par_a, r.n_a, r.inv_a)
@@ -995,15 +1028,26 @@
     def _():
         r.de_all[c, dp] = r.dx[...]
 
+    on_0, on_1 = at_x0 & is_ff, at_x1 & is_att
+    send(at_x0, de(dp), de(dp), (s, ydp), k_de + dp)
     send(at_x0, de(dp), de(dp), (across, dp), k_de + dp)
-    line(de, k_de, at_x0 & is_ff)
+    pair_line(de, k_de, on_0, dp)
 
     line_step(xs, k_xs, 2, at_x1, k_xsc)
     line_step(db, k_db, 1, True, k_dbc)
+    line_step(xs, k_xs, 3, at_x0, k_xsc)
+
+    @pl.when(at_x0)
+    def _():
+        arrived(de(ydp), k_de + ydp)
+
+    send(at_x0, de(ydp), de(ydp), (across, dp), k_de + ydp)
+    pair_line(de, k_de, on_0, ydp)
     pl.when(at_x1)(turn)
     push_rows(at_x1)
     push(0, k_dba, lambda i: r.dbr_a, to_dbr)
     push_dh(0)
+    small(r.sm_f, jnp.sum(r.db_all[c, z, y].astype(F32), 0, keepdims=True), r.vecs[0:1], r.vecs[1:2])
     push(1, k_sm, lambda i: r.sm_f, to_sm)
 
     @pl.when(at_x0)
@@ -1022,11 +1066,11 @@
     line_step(xs, k_xs, 3, at_x1, k_xsc)
     line_step(db, k_db, 2, True, k_dbc)
     push_dh(1)
-    line_step(de, k_de, 1, at_x0 & is_ff, None, k_de)
+    pair_step(de, k_de, 1, on_0, k_de)
     line_step(db, k_db, 3, True, k_dbc)
     push_dh(2)
-    line_step(de, k_de, 2, at_x0 & is_ff, None, k_de)
-    line_step(de, k_de, 3, at_x0 & is_ff, None, k_de)
+    pair_step(de, k_de, 2, on_0, k_de)
+    pair_step(de, k_de, 3, on_0, k_de)
 
     def head_part():
         arrived(r.ch_all.at[other], k_chx)
@@ -1041,12 +1085,20 @@
         grad = mm_tn(r.lgr[...].reshape(lines, p.share_pad), r.ch_pack[...].reshape(lines, w))
         o_tab[...] = grad[0 : p.share]
 
-    @pl.when(at_x1 & is_att)
+    @pl.when(on_1)
     def _():
         arrived(de(dp), k_de + dp)
 
-    line(de, k_de, at_x1 & is_att)
+    pair_line(de, k_de, on_1, dp)
+
+    @pl.when(on_1)
+    def _():
+        arrived(de(ydp), k_de + ydp)
+
+    pair_line(de, k_de, on_1, ydp)
     pl.when(at_x1)(logits)
+    pair_step(de, k_de, 1, on_1, k_de)
+    pair_step(de, k_de, 2, on_1, k_de)
 
     k_in = [recvs.take(4) for _ in range(tiles)]
     half = nz * p.in_rows
@@ -1095,10 +1147,9 @@
             send(inner, shard(far_base + k, cut), r.r_in.at[1, :, cut], (s, 2 * (far_base + k) + y), k_in[j] + 1)
 
     attention_tile(3)
-    line_step(de, k_de, 1, at_x1 & is_att, None, k_de)
+    pair_step(de, k_de, 3, on_1, k_de)
     attention_tile(0)
     attention_sum(3)
-    line_step(de, k_de, 2, at_x1 & is_att, None, k_de)
 
     k_col = recvs.take(n_dp)
     mine_in = pl.ds(pl.multiple_of(dp * p.out_rows, p.out_rows), p.out_rows)
@@ -1112,7 +1163,7 @@
         below = 0.5 + 0.5 * lax.erf(hidden * (0.5**0.5))
         slope = below + hidden * (0.3989422804014327 * jnp.exp(-0.5 * hidden * hidden))
         dhidden = (mm_nt(up, r.w2[mine_in, :]) * slope).astype(BF)
-        o_wout[0] += mm_tn((hidden * below).astype(BF), up)
+        r.u_out[...] += mm_tn((hidden * below).astype(BF), up)
         r.w_col[...] += mm_tn(rows_x, dhidden)
 
     def units_of(yy):
@@ -1124,7 +1175,7 @@
 
     @pl.when(is_ff)
     def _():
-        o_wout[...] = jnp.zeros(o_wout.shape, F32)
+        r.u_out[...] = jnp.zeros(r.u_out.shape, F32)
         r.w_col[...] = jnp.zeros(r.w_col.shape, F32)
         units_of(y)
 
@@ -1138,9 +1189,11 @@
 
     attention_tile(1)
     attention_sum(0)
-    line_step(de, k_de, 3, at_x1 & is_att, None, k_de)
-    line_y(de, k_de, 0, gathers, k_de)
-    line_y(de, k_de, 1, gathers, k_de)
+    @pl.when(at_x1)
+    def _():
+        arrived(r.ch_all.at[c], k_cha)
+
+    send(at_x1, r.ch_all.at[c], r.ch_all.at[c], (core, dp), k_chx)
     attention_tile(2)
     attention_sum(1)
 
@@ -1151,6 +1204,8 @@
         for t in range(nz):
             line_y(db, k_db, t)
         units_of(1 - y)
+        o_wout[0] = r.u_out[...].astype(BF)
+        emit(4, o_wout)
         for k in range(n_dp):
             r.w_send[k] = r.w_col[k * p.in_rows : (k + 1) * p.in_rows, :].astype(BF)
         r.r_col[dp] = r.w_send[dp]
@@ -1158,20 +1213,12 @@
     for k in range(1, n_dp):
         to = lax.rem(dp + k, n_dp)
         send(is_ff, r.w_send.at[to], r.r_col.at[dp], (s, to), k_col + dp)
-    line_y(de, k_de, 2, gathers, k_de)
-    line_y(de, k_de, 3, gathers, k_de)
     attention_sum(2)
 
-    @pl.when(at_x1)
-    def _():
-        arrived(r.ch_all.at[c], k_cha)
-
-    send(at_x1, r.ch_all.at[c], r.ch_all.at[c], (core, dp), k_chx)
-
     head_part()
 
     for i in range(n_dp):
-        pl.when(jnp.logical_not(gathers) & ((i != dp) | at_x1))(lambda i=i: arrived(de(i), k_de + i))
+        pl.when(jnp.logical_not(gathers) & (((i != dp) & (i != ydp)) | at_x1))(lambda i=i: arrived(de(i), k_de + i))
     send(None, r.de_all.at[c], r.de_all.at[c], (core, dp), k_dex)
 
     entry = iota((p.share_rows, ln), 0) + (s * p.quarter + dp * p.share)
@@ -1197,6 +1244,8 @@
         for i in range(n_dp):
             total = total + r.de_all[m, i, here, :].astype(F32)
     o_pos[...] = total
+    emit(1, o_tab)
+    emit(2, o_pos)
 
     @pl.when(is_att)
     def _():
@@ -1206,8 +1255,9 @@
             arrived(r.r_in.at[0, :, cut], k_in[j])
             arrived(r.r_in.at[1, :, cut], k_in[j] + 1)
             near_sum = r.wa[mine, cut].astype(F32) + r.r_in[0, :, cut].astype(F32)
-            o_win[0, :, cut] = near_sum + r.r_in[1, :, cut].astype(F32)
-        o_wout[...] = jnp.zeros(o_wout.shape, F32)
+            o_win[0, :, cut] = (near_sum + r.r_in[1, :, cut].astype(F32)).astype(BF)
+        o_wout[...] = jnp.zeros(o_wout.shape, BF)
+        emit(4, o_wout)
 
     @pl.when(is_ff)
     def _():
@@ -1215,18 +1265,17 @@
             src = lax.rem(dp + k, n_dp)
             arrived(r.r_col.at[src], k_col + src)
         for k in range(n_dp):
-            o_win[0, :, k * p.out_rows : (k + 1) * p.out_rows] = r.r_col[k].astype(F32)
+            o_win[0, :, k * p.out_rows : (k + 1) * p.out_rows] = r.r_col[k]
+
+    emit(3, o_win)
 
     for k in range(1, nz):
         src = lax.rem(z + k, nz)
         arrived(r.r_sm.at[src], k_smz + src)
     r.sm_all[...] = r.r_sm[0] + r.r_sm[1] + r.r_sm[2] + r.r_sm[3]
-    mine = r.sm_all[pl.ds(dp, 1), :]
-    n_b, n_w = ff // n_dp, w // n_dp
-    o_bin[...] = mine[:, 0:n_b]
-    o_bout[...] = mine[:, n_b : n_b + n_w]
-    o_gain[...] = mine[:, n_b + 128 : n_b + 128 + n_w]
-    o_shift[...] = mine[:, n_b + 256 : n_b + 256 + n_w]
+    emit(5, o_vec)
+    for i, src in enumerate((o_log, o_tab, o_pos, o_win, o_wout, o_vec)):
+        pltpu.make_async_copy(src, outs[i], os.at[i]).wait()
 
     for cond, make in pending:
         if cond is None:
@@ -1234,6 +1283,48 @@
         else:
             pl.when(cond)(lambda make=make: make().wait_send())
     assert sends.n <= SENDS and recvs.n <= RECVS, (sends.n, recvs.n)
+
+
+def finish(p, *refs):
+    ins, outs, (log_v, log_w, tab_v, win_v, win_w, wout_v, wout_w, vec_v, b_v, v_v, si, so) = refs[:6], refs[6:15], refs[15:]
+    pieces = (log_v, tab_v, None, win_v, wout_v, vec_v)
+
+    def copy_in(i):
+        return pltpu.make_async_copy(ins[i], pieces[i], si.at[i])
+
+    def copy_out(i, src):
+        return pltpu.make_async_copy(src, outs[i], so.at[i])
+
+    for i in (5, 0, 1, 3, 4):
+        copy_in(i).start()
+    straight = pltpu.make_async_copy(ins[2], outs[2], so.at[2])
+    straight.start()
+    n_b, n_w = p.ff // p.n_dp, p.width // p.n_dp
+    copy_in(5).wait()
+    mine = vec_v[pl.ds(lax.axis_index("dp"), 1), :]
+    b_v[...] = mine[:, 0:n_b]
+    for k in range(3):
+        v_v[k] = mine[:, n_b + 128 * k : n_b + 128 * k + n_w]
+    done = [copy_out(5, b_v)] + [copy_out(6 + k, v_v.at[k]) for k in range(3)]
+    copy_in(0).wait()
+    log_w[...] = log_v[...].astype(F32)
+    done.append(copy_out(0, log_w))
+    for one in done:
+        one.start()
+    copy_in(1).wait()
+    done.append(copy_out(1, tab_v))
+    done[-1].start()
+    copy_in(3).wait()
+    win_w[...] = win_v[...].astype(F32)
+    done.append(copy_out(3, win_w))
+    done[-1].start()
+    copy_in(4).wait()
+    wout_w[...] = wout_v[...].astype(F32)
+    done.append(copy_out(4, wout_w))
+    done[-1].start()
+    straight.wait()
+    for one in done:
+        one.wait()
 
 
 def whole(
@@ -1270,16 +1361,20 @@
     ]
     vmem = pl.BlockSpec(memory_space=pltpu.VMEM)
     far = pl.BlockSpec(memory_space=pl.ANY)
-    return pl.pallas_call(
+    part_types = [BF, F32, F32, BF, BF]
+    parts = [jax.ShapeDtypeStruct(shape, kind) for shape, kind in zip(shapes, part_types)]
+    parts.append(jax.ShapeDtypeStruct((8, width), F32))
+    summed = pl.pallas_call(
         functools.partial(fused, p, list(scratch)),
-        out_shape=[jax.ShapeDtypeStruct(shape, F32) for shape in shapes],
-        in_specs=[vmem] * 9 + [far] * 3,
-        out_specs=[vmem] * 9,
+        out_shape=parts,
+        in_specs=[vmem] * 7 + [far] * 5,
+        out_specs=[far] * 6,
         scratch_shapes=[pltpu.VMEM(*one) for one in scratch.values()]
         + [
             pltpu.SemaphoreType.DMA((SENDS,)),
             pltpu.SemaphoreType.DMA((RECVS,)),
-            pltpu.SemaphoreType.DMA((len(p.chunks) + 2,)),
+            pltpu.SemaphoreType.DMA((len(p.chunks) + 4,)),
+            pltpu.SemaphoreType.DMA((6,)),
         ],
         compiler_params=pltpu.CompilerParams(
             collective_id=0, has_side_effects=True, vmem_limit_bytes=VMEM_LIMIT
@@ -1288,16 +1383,37 @@
         token_ids,
         segment_ids,
         masked_rows,
-        logit_grad,
-        pos_table,
         b_in,
         b_out,
         norm_gain,
         norm_shift,
+        logit_grad,
+        pos_table,
         embedding,
         w_in,
         w_out,
     )
+    room = [
+        (shapes[0], BF),
+        (shapes[0], F32),
+        (shapes[1], F32),
+        (shapes[3], BF),
+        (shapes[3], F32),
+        (shapes[4], BF),
+        (shapes[4], F32),
+        ((8, width), F32),
+        (shapes[5], F32),
+        ((3, 1, p.in_rows), F32),
+    ]
+    return pl.pallas_call(
+        functools.partial(finish, p),
+        out_shape=[jax.ShapeDtypeStruct(shape, F32) for shape in shapes],
+        in_specs=[far] * 6,
+        out_specs=[far] * 9,
+        scratch_shapes=[pltpu.VMEM(*one) for one in room]
+        + [pltpu.SemaphoreType.DMA((6,)), pltpu.SemaphoreType.DMA((9,))],
+        compiler_params=pltpu.CompilerParams(vmem_limit_bytes=VMEM_LIMIT),
+    )(*summed)
 
 
 def solution(mesh):

time: 123 us -> 116 us (0.943)
  the two profiles are of different devices: /device:TPU:1 before, /device:TPU:11 now
where the time goes in v3:
time: 116 us
  Pallas kernels  115 us (99%)
    pallas_call x1, Pallas kernels, whole(): pl.pallas_call(functools.partial(fused, p, list(scratch)), out_shape=part...  112 us
    pallas_call x1, Pallas kernels, whole(): pl.pallas_call(functools.partial(finish, p), out_shape=[jax.ShapeDtypeStr...  3.55 us

profile of v3, /device:TPU:11, one launch (start us, length us, event | category | flops | bytes accessed | tf_op | source)
XLA Modules:
  0.0 116.3 jit_solution(17256939457613088317)
XLA Ops:
  0.6 111.9 %shard_map.187 = (bf16[2,1,40,3648]{3,2,1,0:T(8,128)(2,1)}, f32[456,768]{1,0:T(8,128)}, f32[16,768]{1,0:T(8,128)}, bf16[1,96,3072]{2,1,0:T(8,128)(2,1)}, bf16[1,384,768]{2,1,0:T(8,128)(2,1)}, /*index=5*/f32[8,768]{1,0:T(8,128)}) custom-call(s32[2,1,128]{2,1,0:T(1,128)} %refs_0_.1, s32[2,1,128]{2,1,0:T(1,128)} %refs_1_.1, s32[2,1,40]{2,1,0:T(1,128)} %refs_2_.1, ...), custom_call_target="tpu_custom_call" | custom-call | tf_op jit(solution)/shard_map/pallas_call | solution.py:1367
  112.5 3.5 %shard_map.188 = (f32[2,1,40,3648]{3,2,1,0:T(8,128)}, f32[456,768]{1,0:T(8,128)}, f32[16,768]{1,0:T(8,128)}, f32[1,96,3072]{2,1,0:T(8,128)}, f32[1,384,768]{2,1,...) custom-call(bf16[2,1,40,3648]{3,2,1,0:T(8,128)(2,1)} %get-tuple-element.15.refs_0_, ...), custom_call_target="tpu_custom_call" | custom-call | tf_op jit(solution)/shard_map/pallas_call | solution.py:1408

commit v4 on v3

--- a/solution.py
+++ b/solution.py
@@ -1,4 +1,5 @@
 import functools
+import math
 import types
 
 import jax
@@ -384,8 +385,8 @@
     )
 
 
-SENDS = 260
-RECVS = 160
+SENDS = 109
+RECVS = 110
 VMEM_LIMIT = 64 * 2**20
 BF = jnp.bfloat16
 F32 = jnp.float32
@@ -488,6 +489,7 @@
         dpk=((ln, 3 * w), BF),
         dctx=((ln, w), BF),
         dx=((ln, w), BF),
+        dx_pair=((ln, w), BF),
         bsum=((1, ff), F32),
         vecs=((8, w), F32),
         sm_a=((8, w), F32),
@@ -540,30 +542,67 @@
     at_x0, at_x1 = x == 0, x == 1
     is_att, is_ff = c == 0, c == 1
     sends, recvs = Counter(), Counter()
-    pending = []
-
-    def send(cond, src, dst, dev, recv):
-        slot = sends.take()
-
-        def make():
-            return pltpu.make_async_remote_copy(
+    not_first, not_last = z > 0, z < nz - 1
+    known = {}
+
+    def both(*conds):
+        conds = [cond for cond in conds if cond is not None]
+        key = tuple(sorted(id(cond) for cond in conds))
+        if key not in known:
+            known[key] = (functools.reduce(lambda a, b: a & b, conds) if conds else None, conds)
+        return known[key][0]
+
+    def when(cond, body):
+        if cond is None:
+            body()
+        else:
+            pl.when(cond)(body)
+
+    def at_least(k):
+        return known.setdefault(("least", k), z >= k) if k > 0 else None
+
+    def at_most(k):
+        return known.setdefault(("most", k), z <= k) if k < nz - 1 else None
+
+    groups, stage = {}, [0]
+
+    def send(cond, src, dst, dev, recv, bulk=None, tag=None):
+        key = (stage[0], None if cond is None else id(cond), tag)
+        if key not in groups:
+            groups[key] = [cond, sends.take(), 0, bulk]
+        group = groups[key]
+        group[2] += math.prod(src.shape) * src.dtype.itemsize
+
+        def start():
+            pltpu.make_async_remote_copy(
                 src_ref=src,
                 dst_ref=dst,
-                send_sem=ss.at[slot],
+                send_sem=ss.at[group[1]],
                 recv_sem=rs.at[recv],
                 device_id=dev,
                 device_id_type=MESH,
-            )
-
-        if cond is None:
-            make().start()
-        else:
-
-            @pl.when(cond)
-            def _():
-                make().start()
-
-        pending.append((cond, make))
+            ).start()
+
+        when(cond, start)
+
+    def drain(number):
+        for key, (cond, slot, size, bulk) in groups.items():
+            if key[0] == number:
+                rows = size // (w * 2)
+                assert bulk is not None or size == rows * w * 2 and rows % 16 == 0 and rows <= p.quarter, (rows, size)
+                ref = r.emb.at[0:rows] if bulk is None else bulk
+
+                def gone(ref=ref, slot=slot):
+                    pltpu.make_async_remote_copy(
+                        src_ref=ref,
+                        dst_ref=ref,
+                        send_sem=ss.at[slot],
+                        recv_sem=rs.at[0],
+                        device_id=(core, dp),
+                        device_id_type=MESH,
+                    ).wait_send()
+
+                when(cond, gone)
 
     def arrived(dst, recv):
         pltpu.make_async_remote_copy(
@@ -581,15 +620,6 @@
     lg, pos = r.lg, r.pos
     pltpu.make_async_copy(lg_h, lg, ls.at[l_w + 2]).start()
     pltpu.make_async_copy(pos_h, pos, ls.at[l_w + 3]).start()
-
-    @pl.when(is_att)
-    def _():
-        pltpu.make_async_copy(w_in_h.at[0], r.wa, ls.at[l_w]).start()
-
-    @pl.when(is_ff)
-    def _():
-        pltpu.make_async_copy(w_in_h.at[0], r.w1, ls.at[l_w]).start()
-        pltpu.make_async_copy(w_out_h.at[0], r.w2, ls.at[l_w + 1]).start()
 
     def fill(par):
         par[0:1, :] = b_in[...].astype(F32)
@@ -622,6 +652,15 @@
             r.acc[...] += part
     r.psend[...] = r.acc[pl.ds(pl.multiple_of(ln * other, ln), ln), :].astype(BF)
 
+    @pl.when(is_att)
+    def _():
+        pltpu.make_async_copy(w_in_h.at[0], r.wa, ls.at[l_w]).start()
+
+    @pl.when(is_ff)
+    def _():
+        pltpu.make_async_copy(w_in_h.at[0], r.w1, ls.at[l_w]).start()
+        pltpu.make_async_copy(w_out_h.at[0], r.w2, ls.at[l_w + 1]).start()
+
     tiles = ff // w
     k_p, k_g = recvs.take(2), recvs.take(2)
     k_pa, k_pf, k_wa, k_w1, k_w2 = recvs.take(), recvs.take(), recvs.take(tiles), recvs.take(tiles), recvs.take(tiles)
@@ -635,7 +674,7 @@
     r.lgp[0 : p.masks] = lg[0, 0]
     r.lgp[mp : mp + p.masks] = lg[1, 0]
 
-    k_lg, k_id = recvs.take(n_dp), recvs.take(n_dp)
+    k_lg, k_id = recvs.take(), recvs.take()
     for j in range(n_dp):
         r.lgs[j, :, p.share :] = jnp.zeros((2 * p.masks, p.share_pad - p.share), BF)
         for m in range(2):
@@ -647,8 +686,8 @@
     r.lgr[dp] = r.lgs[dp]
     for k in range(1, n_dp):
         to = lax.rem(dp + k, n_dp)
-        send(None, r.lgs.at[to], r.lgr.at[dp], (s, to), k_lg + dp)
-        send(None, r.ids_own, r.ids_all.at[dp], (s, to), k_id + dp)
+        send(None, r.lgs.at[to], r.lgr.at[dp], (s, to), k_lg, r.lgs.at[0 : n_dp - 1], 1)
+        send(None, r.ids_own, r.ids_all.at[dp], (s, to), k_id, r.ids_all.at[0 : n_dp - 1], 2)
     arrived(r.prow.at[0], k_p)
     own_rows = r.acc[pl.ds(pl.multiple_of(ln * c, ln), ln), :]
     r.acc[0:ln, :] = own_rows + r.prow[0].astype(F32)
@@ -656,13 +695,13 @@
     send(at_x1, r.psum, r.prow.at[1], (across, dp), k_p + 1)
 
     def weights(cond):
-        send(is_att & cond, r.par_a, r.par_a, (core, dp), k_pa)
-        send(is_ff & cond, r.par_f, r.par_f, (core, dp), k_pf)
+        send(both(is_att, cond), r.par_a, r.par_a, (core, dp), k_pa)
+        send(both(is_ff, cond), r.par_f, r.par_f, (core, dp), k_pf)
         for j in range(tiles):
             cut = slice(j * w, (j + 1) * w)
-            send(is_att & cond, w_in_h.at[0, :, cut], r.wa.at[:, cut], (core, dp), k_wa + j)
-            send(is_ff & cond, w_in_h.at[0, :, cut], r.w1.at[:, cut], (core, dp), k_w1 + j)
-            send(is_ff & cond, w_out_h.at[0, cut, :], r.w2.at[cut, :], (core, dp), k_w2 + j)
+            send(both(is_att, cond), w_in_h.at[0, :, cut], r.wa.at[:, cut], (core, dp), k_wa + j, tag=3)
+            send(both(is_ff, cond), w_in_h.at[0, :, cut], r.w1.at[:, cut], (core, dp), k_w1 + j, tag=4)
+            send(both(is_ff, cond), w_out_h.at[0, cut, :], r.w2.at[cut, :], (core, dp), k_w2 + j, tag=5)
 
     weights(at_x0)
 
@@ -752,63 +791,60 @@
     resid = rows_x.astype(F32) + mm(r.ctx[...], r.wa[:, 3 * w : 4 * w]) + r.par_a[1:2, 0:w]
     r.x_f[...], r.n_a[...], r.inv_a[...] = norm_forward(resid, r.par_a)
 
-    def line(buf, base, cond=True, owner=None):
+    def line(buf, base, owner):
         own = buf(dp)
-        send(cond & (z < nz - 1), own, own, (s, dp + 2), base + dp)
-        send(cond & (z > 0), own, own, (s, dp - 2), base + dp)
-        to_y(buf, base, dp, cond, owner)
+        send(not_last, own, own, (s, dp + 2), base + dp)
+        send(not_first, own, own, (s, dp - 2), base + dp)
+        send(is_att, own, own, (core, dp), owner + dp)
+        to_y(buf, base, dp, None, owner)
 
     def to_y(buf, base, i, cond, owner):
-        piece = buf(i)
-        if owner is None:
-            send(None if cond is True else cond, piece, piece, (s, ydp), base + i)
-        else:
-            whose = jnp.where(is_att, core, s)
-            send(None if cond is True else cond, piece, piece, (whose, ydp), jnp.where(is_att, owner, base) + i)
-            send(is_att & cond, piece, piece, (core, dp), owner + i)
-
-    def line_step(buf, base, t, cond=True, owner=None):
+        whose = jnp.where(is_att, core, s)
+        send(cond, buf(i), buf(i), (whose, ydp), jnp.where(is_att, owner, base) + i)
+
+    def at_distance(t, sign, cond):
+        here = both(cond, at_least(t) if sign < 0 else at_most(nz - 1 - t))
+        return here, jnp.clip(z + sign * t, 0, nz - 1) * 2 + y
+
+    def onward(here, sign):
+        return both(here, not_last if sign < 0 else not_first)
+
+    def line_step(buf, base, t, cond, owner):
         for sign in (-1, 1):
-            from_z = z + sign * t
-            here = (from_z >= 0) & (from_z < nz) & cond
-            from_dp = jnp.clip(from_z, 0, nz - 1) * 2 + y
+            here, from_dp = at_distance(t, sign, cond)
             piece = buf(from_dp)
-            pl.when(here)(lambda piece=piece, from_dp=from_dp: arrived(piece, base + from_dp))
-            to_z = z - sign
-            on = here & (to_z >= 0) & (to_z < nz)
+            when(here, lambda piece=piece, from_dp=from_dp: arrived(piece, base + from_dp))
             if t < nz - 1:
-                send(on, piece, piece, (s, dp - 2 * sign), base + from_dp)
+                send(onward(here, sign), piece, piece, (s, dp - 2 * sign), base + from_dp)
+            send(both(here, is_att), piece, piece, (core, dp), owner + from_dp)
+
+    def line_cross(buf, base, t, cond, owner):
+        for sign in (-1, 1):
+            here, from_dp = at_distance(t, sign, cond)
             to_y(buf, base, from_dp, here, owner)
-
-    def line_y(buf, base, t):
-        for sign in (-1, 1) if t else (1,):
-            from_z = z + sign * t
-            from_dp = jnp.clip(from_z, 0, nz - 1) * 2 + 1 - y
-            pl.when((from_z >= 0) & (from_z < nz))(lambda i=from_dp: arrived(buf(i), base + i))
 
     def pair_line(buf, base, cond, i):
         piece = buf(i)
-        send(cond & (z < nz - 1), piece, piece, (s, dp + 2), base + i)
-        send(cond & (z > 0), piece, piece, (s, dp - 2), base + i)
+        send(both(cond, not_last), piece, piece, (s, dp + 2), base + i)
+        send(both(cond, not_first), piece, piece, (s, dp - 2), base + i)
 
     def pair_step(buf, base, t, cond, on_x):
         for sign in (-1, 1):
-            from_z = z + sign * t
-            here = (from_z >= 0) & (from_z < nz) & cond
             for side in (0, 1):
-                from_dp = jnp.clip(from_z, 0, nz - 1) * 2 + (1 - y if side else y)
+                here, from_dp = at_distance(t, sign, cond)
+                if side:
+                    from_dp = from_dp + 1 - 2 * y
                 piece = buf(from_dp)
-                pl.when(here)(lambda piece=piece, from_dp=from_dp: arrived(piece, base + from_dp))
+                when(here, lambda piece=piece, from_dp=from_dp: arrived(piece, base + from_dp))
                 if t < nz - 1:
-                    on = here & (z - sign >= 0) & (z - sign < nz)
-                    send(on, piece, piece, (s, dp - 2 * sign), base + from_dp)
+                    send(onward(here, sign), piece, piece, (s, dp - 2 * sign), base + from_dp)
                 send(here, piece, piece, (across, dp), on_x + from_dp)
 
     def ch(i):
         return r.ch_all.at[c, i]
 
     def de(i):
-        return r.de_all.at[c, i]
+        return r.de_all.at[1 - x, i]
 
     def xs(i):
         return r.x_all.at[c, i // 2, lax.rem(i, 2)]
@@ -816,12 +852,15 @@
     def db(i):
         return r.db_all.at[c, i // 2, lax.rem(i, 2)]
 
-    k_ch, k_de, k_xs, k_db = (recvs.take(n_dp) for _ in range(4))
-    k_cho, k_chc, k_cha, k_chx, k_dex = (recvs.take() for _ in range(5))
+    k_ch, k_xs, k_db = (recvs.take(n_dp) for _ in range(3))
+    k_dr = recvs.take(2 * n_dp)
+    k_row = k_dr + (1 - x) * n_dp
+    k_cho, k_chc, k_cha, k_chx, k_dp = (recvs.take() for _ in range(5))
+    k_dex = recvs.take(2)
     k_xsc, k_dbc = recvs.take(n_dp), recvs.take(n_dp)
 
     r.x_all[c, z, y] = r.x_f[...]
-    line(xs, k_xs, True, k_xsc)
+    line(xs, k_xs, k_xsc)
 
     def feed(rows_x, keep=True):
         total = rows_x.astype(F32) + r.par_f[1:2, 0:w]
@@ -846,14 +885,14 @@
             r.y_o[...] = result
 
     pl.when(is_ff | at_x1)(lambda: feed(r.x_f[...]))
-    send(at_x0 & is_ff, r.y_f, r.x_a, (across, dp), k_x)
+    send(both(at_x0, is_ff), r.y_f, r.x_a, (across, dp), k_x)
 
     @pl.when(at_x0 & is_ff)
     def _():
         arrived(r.x_all.at[0, z, y], k_xsc + dp)
         feed(r.x_all[0, z, y], False)
 
-    send(at_x0 & is_ff, r.y_o, r.x_a, (3 - s, dp), k_x)
+    send(both(at_x0, is_ff), r.y_o, r.x_a, (3 - s, dp), k_x)
 
     @pl.when(at_x1)
     def _():
@@ -871,30 +910,28 @@
     send(at_x1, r.ch_own, r.ch_two, (core, dp), k_chc)
 
     def push(owner, kind, src, dst, cond=None):
-        home = c == owner
+        home, away = (is_att, is_ff) if owner == 0 else (is_ff, is_att)
         slot_y = 2 + jnp.where(home, 0, 1)
         own_dst, near_dst, far_dst = dst(0), dst(1), dst(slot_y)
 
-        away = jnp.logical_not(home)
-
-        @pl.when(home if cond is None else home & cond)
+
+        @pl.when(both(home, cond))
         def _():
-            pltpu.make_async_copy(src(y), own_dst, rs.at[kind]).start()
-
-        send(away if cond is None else away & cond, src(y), near_dst, (core, dp), kind + 1)
-        far_s = jnp.where(home, s, core)
-        send(cond, src(1 - y), far_dst, (far_s, ydp), kind + slot_y)
+            own_dst[...] = src(y)[...]
+
+        send(both(away, cond), src(y), near_dst, (core, dp), kind)
+        send(cond, src(1 - y), far_dst, (jnp.where(home, s, core), ydp), kind)
 
     def gathered(kind, dst):
-        pltpu.make_async_copy(dst(0), dst(0), rs.at[kind]).wait()
-        for slot in range(1, 4):
-            arrived(dst(slot), kind + slot)
+        arrived(dst(slice(1, 4)), kind)
 
     def lanes(slot):
+        if isinstance(slot, slice):
+            return pl.ds(slot.start * ln, (slot.stop - slot.start) * ln)
         return pl.ds(slot * ln if isinstance(slot, int) else pl.multiple_of(slot * ln, ln), ln)
 
-    k_dh = [recvs.take(4) for _ in range(3)]
-    k_ctx, k_xt, k_dba, k_sm = (recvs.take(4) for _ in range(4))
+    k_dh = [recvs.take() for _ in range(3)]
+    k_ctx, k_xt, k_dba, k_sm = (recvs.take() for _ in range(4))
     to_x = lambda slot: r.b_x.at[:, :, lanes(slot)]
     to_ctx = lambda slot: r.b_ctx.at[:, :, lanes(slot)]
     to_dbr = lambda slot: r.b_dbr.at[lanes(slot), :]
@@ -916,6 +953,7 @@
             for b in range(n_dp):
                 dst[b // 2, b % 2] = turned[b * p.in_rows : (b + 1) * p.in_rows]
 
+    stage[0] = 1
     @pl.when(at_x0)
     def _():
         masked_gradient()
@@ -928,8 +966,9 @@
     def _():
         feed(r.x_f[...])
 
-    line_step(xs, k_xs, 1, at_x0, k_xsc)
-    line_step(xs, k_xs, 2, at_x0, k_xsc)
+    for t in (1, 2):
+        line_step(xs, k_xs, t, at_x0, k_xsc)
+        line_cross(xs, k_xs, t, at_x0, k_xsc)
 
     @pl.when(at_x0)
     def _():
@@ -937,8 +976,9 @@
         r.ch_all[c, dp] = r.ch_own[...]
 
     send(at_x0, r.ch_own, r.ch_two, (core, dp), k_chc)
-    for k in range(1, n_dp):
-        send(at_x0, r.ch_own, ch(dp), (s, lax.rem(dp + k, n_dp)), k_ch + dp)
+    send(at_x0, r.ch_own, ch(dp), (s, ydp), k_ch + dp)
+    for k in range(1, nz):
+        send(at_x0, r.ch_own, ch(dp), (s, lax.rem(dp + 2 * k, n_dp)), k_ch + dp)
 
     def emit(i, src):
         pltpu.make_async_copy(src, outs[i], os.at[i]).start()
@@ -953,6 +993,8 @@
         emit(0, o_log)
 
     pl.when(at_x0)(logits)
+    line_step(xs, k_xs, 3, at_x0, k_xsc)
+    line_cross(xs, k_xs, 3, at_x0, k_xsc)
 
     k_dy = recvs.take()
 
@@ -982,7 +1024,7 @@
     dres, gain_part, shift_part = norm_backward(r.par_f, r.n_f, r.inv_f)
     r.dres[...] = dres
     r.db_all[c, z, y] = dres.astype(BF)
-    line(db, k_db, True, k_dbc)
+    line(db, k_db, k_dbc)
     branch = r.db_all[c, z, y]
     total = r.dres[...]
     for j in range(tiles):
@@ -993,6 +1035,7 @@
     r.dyf[...] = total.astype(BF).astype(F32)
     r.vecs[0:1], r.vecs[1:2] = gain_part, shift_part
     line_step(xs, k_xs, 1, at_x1, k_xsc)
+    line_cross(xs, k_xs, 1, at_x1, k_xsc)
 
     dres, gain_part, shift_part = norm_backward(r.par_a, r.n_a, r.inv_a)
     r.dres[...] = dres
@@ -1022,62 +1065,68 @@
     r.dx[...] = total.astype(BF)
     send(at_x1, r.dx, r.dyin, (across, dp), k_dy)
 
-    gathers = c == 1 - x
-
-    @pl.when(at_x0)
-    def _():
-        r.de_all[c, dp] = r.dx[...]
-
-    on_0, on_1 = at_x0 & is_ff, at_x1 & is_att
-    send(at_x0, de(dp), de(dp), (s, ydp), k_de + dp)
-    send(at_x0, de(dp), de(dp), (across, dp), k_de + dp)
-    pair_line(de, k_de, on_0, dp)
-
-    line_step(xs, k_xs, 2, at_x1, k_xsc)
-    line_step(db, k_db, 1, True, k_dbc)
-    line_step(xs, k_xs, 3, at_x0, k_xsc)
-
-    @pl.when(at_x0)
-    def _():
-        arrived(de(ydp), k_de + ydp)
-
-    send(at_x0, de(ydp), de(ydp), (across, dp), k_de + ydp)
-    pair_line(de, k_de, on_0, ydp)
+    def row(m, i):
+        return r.de_all.at[m, i]
+
+    on_0, on_1 = both(at_x0, is_ff), both(at_x1, is_ff)
+    away = jnp.where(is_ff, across, 3 - s)
+
+    def hand_on(src, i):
+        send(at_x0, src, row(c, i), (away, dp), k_dr + c * n_dp + i)
+        send(both(at_x0, is_att), src, row(0, i), (core, dp), k_dr + i)
+
+        @pl.when(on_0)
+        def _():
+            r.de_all[1, i] = src[...]
+
+    send(at_x0, r.dx, r.dx_pair, (s, ydp), k_dp)
+    hand_on(r.dx, dp)
+    pair_line(de, k_row, on_0, dp)
+
+    stage[0] = 2
     pl.when(at_x1)(turn)
     push_rows(at_x1)
     push(0, k_dba, lambda i: r.dbr_a, to_dbr)
     push_dh(0)
+    push_dh(1)
+    line_step(xs, k_xs, 2, at_x1, k_xsc)
+    line_step(db, k_db, 1, None, k_dbc)
+
+
+    @pl.when(at_x0)
+    def _():
+        arrived(r.dx_pair, k_dp)
+
+    hand_on(r.dx_pair, ydp)
+    pair_line(de, k_row, on_0, ydp)
+    line_cross(xs, k_xs, 2, at_x1, k_xsc)
+    for k in range(1, nz):
+        i = lax.rem(dp + 2 * k, n_dp)
+        pl.when(at_x0)(lambda i=i: arrived(ch(i), k_ch + i))
+        send(at_x0, ch(i), ch(i), (s, ydp), k_ch + i)
+    line_cross(db, k_db, 1, None, k_dbc)
     small(r.sm_f, jnp.sum(r.db_all[c, z, y].astype(F32), 0, keepdims=True), r.vecs[0:1], r.vecs[1:2])
     push(1, k_sm, lambda i: r.sm_f, to_sm)
-
-    @pl.when(at_x0)
-    def _():
-        for k in range(1, n_dp):
-            arrived(ch(lax.rem(dp + k, n_dp)), k_ch + lax.rem(dp + k, n_dp))
-
-    send(at_x0, r.ch_all.at[c], r.ch_all.at[c], (across, dp), k_cha)
-    send(at_x0, r.ch_all.at[c], r.ch_all.at[c], (core, dp), k_chx)
     r.bsum[...] = jnp.zeros(r.bsum.shape, F32)
     for j in (0, 2):
         cut = slice(j * w, (j + 1) * w)
         r.bsum[:, cut] = jnp.sum(r.dpk[:, cut].astype(F32), 0, keepdims=True)
     small(r.sm_a, jnp.sum(branch.astype(F32), 0, keepdims=True), gain_part, shift_part)
     push(0, k_sm, lambda i: r.sm_a, to_sm)
-    line_step(xs, k_xs, 3, at_x1, k_xsc)
-    line_step(db, k_db, 2, True, k_dbc)
-    push_dh(1)
-    pair_step(de, k_de, 1, on_0, k_de)
-    line_step(db, k_db, 3, True, k_dbc)
     push_dh(2)
-    pair_step(de, k_de, 2, on_0, k_de)
-    pair_step(de, k_de, 3, on_0, k_de)
+    for t in (2, 3):
+        if t == 2:
+            line_step(xs, k_xs, 3, at_x1, k_xsc)
+            line_cross(xs, k_xs, 3, at_x1, k_xsc)
+        line_step(db, k_db, t, None, k_dbc)
+        line_cross(db, k_db, t, None, k_dbc)
+        if t == 2:
+            drain(0)
 
     def head_part():
         arrived(r.ch_all.at[other], k_chx)
-        for k in range(1, n_dp):
-            src = lax.rem(dp + k, n_dp)
-            arrived(r.lgr.at[src], k_lg + src)
-            arrived(r.ids_all.at[src], k_id + src)
+        arrived(r.lgr.at[0 : n_dp - 1], k_lg)
+        arrived(r.ids_all.at[0 : n_dp - 1], k_id)
         for i in range(n_dp):
             for m in range(2):
                 r.ch_pack[i, p.masks * m : p.masks * (m + 1)] = r.ch_all[m, i, 0 : p.masks]
@@ -1085,24 +1134,10 @@
         grad = mm_tn(r.lgr[...].reshape(lines, p.share_pad), r.ch_pack[...].reshape(lines, w))
         o_tab[...] = grad[0 : p.share]
 
-    @pl.when(on_1)
-    def _():
-        arrived(de(dp), k_de + dp)
-
-    pair_line(de, k_de, on_1, dp)
-
-    @pl.when(on_1)
-    def _():
-        arrived(de(ydp), k_de + ydp)
-
-    pair_line(de, k_de, on_1, ydp)
-    pl.when(at_x1)(logits)
-    pair_step(de, k_de, 1, on_1, k_de)
-    pair_step(de, k_de, 2, on_1, k_de)
-
     k_in = [recvs.take(4) for _ in range(tiles)]
     half = nz * p.in_rows
     outer = (z == 0) | (z == nz - 1)
+    outer_att, inner = both(is_att, outer), both(is_att, jnp.logical_not(outer))
     mate = z + 1 - 2 * lax.rem(z, 2)
     far_base = 2 - 2 * (z // 2)
 
@@ -1130,12 +1165,11 @@
 
         to_mate = (s, 2 * mate + y)
         for k in range(2):
-            send(is_att & outer, shard(far_base + k, cut), r.r_in.at[2 + k, :, cut], to_mate, k_in[j] + 2 + k)
+            send(outer_att, shard(far_base + k, cut), r.r_in.at[2 + k, :, cut], to_mate, k_in[j] + 2 + k)
         send(is_att, shard(mate, cut), r.r_in.at[0, :, cut], to_mate, k_in[j])
 
     def attention_sum(j):
         cut = tile_cut(j)
-        inner = is_att & jnp.logical_not(outer)
         for k in range(2):
 
             @pl.when(inner)
@@ -1145,14 +1179,6 @@
                 r.wa[rows, cut] = (r.wa[rows, cut].astype(F32) + r.r_in[2 + k, :, cut].astype(F32)).astype(BF)
 
             send(inner, shard(far_base + k, cut), r.r_in.at[1, :, cut], (s, 2 * (far_base + k) + y), k_in[j] + 1)
-
-    attention_tile(3)
-    pair_step(de, k_de, 3, on_1, k_de)
-    attention_tile(0)
-    attention_sum(3)
-
-    k_col = recvs.take(n_dp)
-    mine_in = pl.ds(pl.multiple_of(dp * p.out_rows, p.out_rows), p.out_rows)
 
     def unit_grads(yy, i):
         def four(buf):
@@ -1166,60 +1192,19 @@
         r.u_out[...] += mm_tn((hidden * below).astype(BF), up)
         r.w_col[...] += mm_tn(rows_x, dhidden)
 
-    def units_of(yy):
-        for zz in range(nz):
-            i = 2 * zz + yy
-            pl.when((i != dp) | at_x1)(lambda i=i: arrived(r.x_all.at[0, i // 2, lax.rem(i, 2)], k_xsc + i))
-            arrived(r.db_all.at[0, i // 2, lax.rem(i, 2)], k_dbc + i)
-        lax.fori_loop(0, nz // 2, lambda i, carry: (unit_grads(yy, i), carry)[1], 0)
-
-    @pl.when(is_ff)
-    def _():
-        r.u_out[...] = jnp.zeros(r.u_out.shape, F32)
-        r.w_col[...] = jnp.zeros(r.w_col.shape, F32)
-        units_of(y)
-
-    k_smz = recvs.take(nz)
-    gathered(k_sm, to_sm)
-    r.sm_tot[...] = r.b_sm[0] + r.b_sm[1] + r.b_sm[2] + r.b_sm[3]
-    r.r_sm[z] = r.sm_tot[...]
-    for k in range(1, nz):
-        zz = lax.rem(z + k, nz)
-        send(None, r.sm_tot, r.r_sm.at[z], (s, 2 * zz + y), k_smz + z)
-
-    attention_tile(1)
-    attention_sum(0)
-    @pl.when(at_x1)
-    def _():
-        arrived(r.ch_all.at[c], k_cha)
-
-    send(at_x1, r.ch_all.at[c], r.ch_all.at[c], (core, dp), k_chx)
-    attention_tile(2)
-    attention_sum(1)
-
-    @pl.when(is_ff)
-    def _():
-        for t in range(nz):
-            line_y(xs, k_xs, t)
-        for t in range(nz):
-            line_y(db, k_db, t)
-        units_of(1 - y)
-        o_wout[0] = r.u_out[...].astype(BF)
-        emit(4, o_wout)
-        for k in range(n_dp):
-            r.w_send[k] = r.w_col[k * p.in_rows : (k + 1) * p.in_rows, :].astype(BF)
-        r.r_col[dp] = r.w_send[dp]
-
-    for k in range(1, n_dp):
-        to = lax.rem(dp + k, n_dp)
-        send(is_ff, r.w_send.at[to], r.r_col.at[dp], (s, to), k_col + dp)
-    attention_sum(2)
-
-    head_part()
-
-    for i in range(n_dp):
-        pl.when(jnp.logical_not(gathers) & (((i != dp) & (i != ydp)) | at_x1))(lambda i=i: arrived(de(i), k_de + i))
-    send(None, r.de_all.at[c], r.de_all.at[c], (core, dp), k_dex)
+    def units_of(yy, i):
+        for k in range(2):
+            d = 4 * i + 2 * k + yy
+            pl.when((d != dp) | at_x1)(lambda d=d: arrived(r.x_all.at[0, d // 2, lax.rem(d, 2)], k_xsc + d))
+            arrived(r.db_all.at[0, d // 2, lax.rem(d, 2)], k_dbc + d)
+        unit_grads(yy, i)
+
+    def units_over_y(t):
+        for buf, base in ((xs, k_xs), (db, k_db)):
+            for k in range(2):
+                d = 4 * t + 2 * k + 1 - y
+                arrived(buf(d), base + d)
+        units_of(1 - y, t)
 
     entry = iota((p.share_rows, ln), 0) + (s * p.quarter + dp * p.share)
 
@@ -1234,9 +1219,109 @@
 
         lax.fori_loop(0, n_dp // 2, step, 0)
 
-    scatter(c)
-    arrived(r.de_all.at[other], k_dex)
-    scatter(other)
+    k_col, k_smz = recvs.take(), recvs.take()
+    mine_in = pl.ds(pl.multiple_of(dp * p.out_rows, p.out_rows), p.out_rows)
+    mate_half = 1 - z // 2
+
+    def gathered_row(cond):
+        send(cond, r.de_all.at[1 - x], r.de_all.at[1 - x], (core, dp), k_dex + (1 - x))
+
+    attention_tile(3)
+    pair_step(de, k_row, 1, on_0, k_row)
+    attention_tile(0)
+    attention_sum(3)
+    pair_step(de, k_row, 2, on_0, k_row)
+    pair_step(de, k_row, 3, on_0, k_row)
+    gathered_row(on_0)
+
+    @pl.when(is_ff)
+    def _():
+        r.u_out[...] = jnp.zeros(r.u_out.shape, F32)
+        r.w_col[...] = jnp.zeros(r.w_col.shape, F32)
+        units_of(y, z // 2)
+        units_of(y, mate_half)
+
+    attention_tile(1)
+    attention_sum(0)
+
+    @pl.when(at_x0)
+    def _():
+        for zz in range(nz):
+            i = 2 * zz + 1 - y
+            arrived(ch(i), k_ch + i)
+
+    send(at_x0, r.ch_all.at[c], r.ch_all.at[c], (across, dp), k_cha)
+    send(at_x0, r.ch_all.at[c], r.ch_all.at[c], (core, dp), k_chx)
+
+    @pl.when(on_1)
+    def _():
+        arrived(row(0, dp), k_dr + dp)
+
+    pair_line(de, k_row, on_1, dp)
+    pl.when(at_x1)(logits)
+
+    @pl.when(on_1)
+    def _():
+        arrived(row(0, ydp), k_dr + ydp)
+
+    pair_line(de, k_row, on_1, ydp)
+    pair_step(de, k_row, 1, on_1, k_row)
+    attention_sum(1)
+
+    gathered(k_sm, to_sm)
+    r.sm_tot[...] = r.b_sm[0] + r.b_sm[1] + r.b_sm[2] + r.b_sm[3]
+    r.r_sm[z] = r.sm_tot[...]
+    for k in range(1, nz):
+        zz = lax.rem(z + k, nz)
+        send(None, r.sm_tot, r.r_sm.at[z], (s, 2 * zz + y), k_smz)
+
+    attention_tile(2)
+    pair_step(de, k_row, 2, on_1, k_row)
+    pair_step(de, k_row, 3, on_1, k_row)
+    gathered_row(on_1)
+    attention_sum(2)
+
+    def passed_row(cond):
+        @pl.when(cond)
+        def _():
+            for i in range(n_dp):
+                arrived(row(x, i), k_dr + x * n_dp + i)
+
+        send(cond, r.de_all.at[x], r.de_all.at[x], (core, dp), k_dex + x)
+
+    passed_row(on_1)
+
+    @pl.when(at_x1)
+    def _():
+        arrived(r.ch_all.at[c], k_cha)
+
+    send(at_x1, r.ch_all.at[c], r.ch_all.at[c], (core, dp), k_chx)
+
+    @pl.when(is_ff)
+    def _():
+        units_over_y(z // 2)
+        units_over_y(mate_half)
+        o_wout[0] = r.u_out[...].astype(BF)
+        emit(4, o_wout)
+        for k in range(n_dp):
+            r.w_send[k] = r.w_col[k * p.in_rows : (k + 1) * p.in_rows, :].astype(BF)
+        r.r_col[dp] = r.w_send[dp]
+
+    for k in (4, 5, 3, 2, 6, 1, 7) if n_dp == 8 else range(1, n_dp):
+        to = lax.rem(dp + k, n_dp)
+        send(is_ff, r.w_send.at[to], r.r_col.at[dp], (s, to), k_col)
+    passed_row(on_0)
+
+    head_part()
+
+    @pl.when(is_att)
+    def _():
+        arrived(r.de_all.at[0], k_dex)
+        arrived(r.de_all.at[1], k_dex + 1)
+
+    scatter(0)
+    scatter(1)
+    drain(1)
     n_pos = ln // n_dp
     here = pl.ds(pl.multiple_of(dp * n_pos, n_pos), n_pos)
     total = jnp.zeros((n_pos, w), F32)
@@ -1261,27 +1346,19 @@
 
     @pl.when(is_ff)
     def _():
-        for k in range(1, n_dp):
-            src = lax.rem(dp + k, n_dp)
-            arrived(r.r_col.at[src], k_col + src)
+        arrived(r.r_col.at[0 : n_dp - 1], k_col)
         for k in range(n_dp):
             o_win[0, :, k * p.out_rows : (k + 1) * p.out_rows] = r.r_col[k]
 
     emit(3, o_win)
 
-    for k in range(1, nz):
-        src = lax.rem(z + k, nz)
-        arrived(r.r_sm.at[src], k_smz + src)
+    arrived(r.r_sm.at[0 : nz - 1], k_smz)
     r.sm_all[...] = r.r_sm[0] + r.r_sm[1] + r.r_sm[2] + r.r_sm[3]
     emit(5, o_vec)
     for i, src in enumerate((o_log, o_tab, o_pos, o_win, o_wout, o_vec)):
         pltpu.make_async_copy(src, outs[i], os.at[i]).wait()
 
-    for cond, make in pending:
-        if cond is None:
-            make().wait_send()
-        else:
-            pl.when(cond)(lambda make=make: make().wait_send())
+    drain(2)
     assert sends.n <= SENDS and recvs.n <= RECVS, (sends.n, recvs.n)
 
 

time: 116 us -> 109 us (0.940)
  the two profiles are of different devices: /device:TPU:11 before, /device:TPU:1 now
where the time goes in v4:
time: 109 us; the launch traced here: 108 us
  Pallas kernels  108 us (99%)
    pallas_call x1, Pallas kernels, whole(): pl.pallas_call(functools.partial(fused, p, list(scratch)), out_shape=part...  104 us
    pallas_call x1, Pallas kernels, whole(): pl.pallas_call(functools.partial(finish, p), out_shape=[jax.ShapeDtypeStr...  3.55 us

profile of v4, /device:TPU:1, one launch (start us, length us, event | category | flops | bytes accessed | tf_op | source)
XLA Modules:
  0.0 108.4 jit_solution(7249204234751634574)
XLA Ops:
  0.6 104.0 %shard_map.187 = (bf16[2,1,40,3648]{3,2,1,0:T(8,128)(2,1)}, f32[456,768]{1,0:T(8,128)}, f32[16,768]{1,0:T(8,128)}, bf16[1,96,3072]{2,1,0:T(8,128)(2,1)}, bf16[1,384,768]{2,1,0:T(8,128)(2,1)}, /*index=5*/f32[8,768]{1,0:T(8,128)}) custom-call(s32[2,1,128]{2,1,0:T(1,128)} %refs_0_.1, s32[2,1,128]{2,1,0:T(1,128)} %refs_1_.1, s32[2,1,40]{2,1,0:T(1,128)} %refs_2_.1, ...), custom_call_target="tpu_custom_call" | custom-call | tf_op jit(solution)/shard_map/pallas_call | solution.py:1444
  104.7 3.5 %shard_map.188 = (f32[2,1,40,3648]{3,2,1,0:T(8,128)}, f32[456,768]{1,0:T(8,128)}, f32[16,768]{1,0:T(8,128)}, f32[1,96,3072]{2,1,0:T(8,128)}, f32[1,384,768]{2,1,...) custom-call(bf16[2,1,40,3648]{3,2,1,0:T(8,128)(2,1)} %get-tuple-element.15.refs_0_, ...), custom_call_target="tpu_custom_call" | custom-call | tf_op jit(solution)/shard_map/pallas_call | solution.py:1485

commit v5 on v4

--- a/solution.py
+++ b/solution.py
@@ -385,8 +385,8 @@
     )
 
 
-SENDS = 109
-RECVS = 110
+SENDS = 91
+RECVS = 84
 VMEM_LIMIT = 64 * 2**20
 BF = jnp.bfloat16
 F32 = jnp.float32
@@ -446,6 +446,13 @@
     w, ff, ln = p.width, p.ff, p.length
     mp = p.mask_pad
     return dict(
+        tok=((2, 1, ln), jnp.int32),
+        seg=((2, 1, ln), jnp.int32),
+        picks=((2, 1, p.masks), jnp.int32),
+        b_in=((1, ff), BF),
+        b_out=((1, w), BF),
+        gain=((1, w), BF),
+        shift=((1, w), BF),
         emb=((p.quarter, w), BF),
         lg=((2, 1, p.masks, p.quarter), BF),
         pos=((ln, w), BF),
@@ -510,6 +517,8 @@
         r_col=((p.n_dp, p.in_rows, p.out_rows), BF),
         ch_own=((mp, w), BF),
         ch_two=((mp, w), BF),
+        ch_pair=((mp, w), BF),
+        ch_far=((mp, w), BF),
         ch_all=((2, p.n_dp, mp, w), BF),
         de_all=((2, p.n_dp, ln, w), BF),
         u_out=((p.out_rows, w), F32),
@@ -522,7 +531,7 @@
 
 
 def fused(p, names, *refs):
-    (tok, seg, picks, b_in, b_out, gain, shift, lg_h, pos_h, emb_h, w_in_h, w_out_h) = refs[:12]
+    far_small, (lg_h, pos_h, emb_h, w_in_h, w_out_h) = refs[:7], refs[7:12]
     outs = refs[12:18]
     r = types.SimpleNamespace(**dict(zip(names, refs[18:])))
     ss, rs, ls, os = refs[18 + len(names) :]
@@ -539,60 +548,73 @@
     across = s + 2 - 4 * x
     ydp = dp + 1 - 2 * y
     other = 1 - c
-    at_x0, at_x1 = x == 0, x == 1
-    is_att, is_ff = c == 0, c == 1
+    at_x0, at_x1 = frozenset(["x0"]), frozenset(["x1"])
+    is_att, is_ff = frozenset(["att"]), frozenset(["ff"])
+    on_0, on_1 = at_x0 | is_ff, at_x1 | is_ff
+    outer_att, inner = is_att | {"outer"}, is_att | {"inner"}
+    always = frozenset()
     sends, recvs = Counter(), Counter()
-    not_first, not_last = z > 0, z < nz - 1
-    known = {}
-
-    def both(*conds):
-        conds = [cond for cond in conds if cond is not None]
-        key = tuple(sorted(id(cond) for cond in conds))
-        if key not in known:
-            known[key] = (functools.reduce(lambda a, b: a & b, conds) if conds else None, conds)
-        return known[key][0]
-
-    def when(cond, body):
-        if cond is None:
-            body()
-        else:
-            pl.when(cond)(body)
+    def holds(name):
+        if name[:2] == "z>":
+            return z >= int(name[2:])
+        if name[:2] == "z<":
+            return z <= int(name[2:])
+        if name in ("outer", "inner"):
+            edge = (z == 0) | (z == nz - 1)
+            return edge if name == "outer" else jnp.logical_not(edge)
+        return {"x0": x == 0, "x1": x == 1, "att": c == 0, "ff": c == 1}[name]
 
     def at_least(k):
-        return known.setdefault(("least", k), z >= k) if k > 0 else None
+        return frozenset(["z>%d" % k]) if k > 0 else always
 
     def at_most(k):
-        return known.setdefault(("most", k), z <= k) if k < nz - 1 else None
+        return frozenset(["z<%d" % k]) if k < nz - 1 else always
+
+    not_first, not_last = at_least(1), at_most(nz - 2)
+    outside = [always]
+
+    def on(cond):
+        def run(body):
+            names = sorted(cond - outside[0])
+            before, outside[0] = outside[0], outside[0] | cond
+            if names:
+                pl.when(functools.reduce(lambda a, b: a & b, [holds(name) for name in names]))(body)
+            else:
+                body()
+            outside[0] = before
+
+        return run
 
     groups, stage = {}, [0]
 
     def send(cond, src, dst, dev, recv, bulk=None, tag=None):
-        key = (stage[0], None if cond is None else id(cond), tag)
+        cond = cond | outside[0]
+        key = (stage[0], cond, tag)
         if key not in groups:
-            groups[key] = [cond, sends.take(), 0, bulk]
+            groups[key] = [sends.take(), 0, bulk]
         group = groups[key]
-        group[2] += math.prod(src.shape) * src.dtype.itemsize
-
-        def start():
+        group[1] += math.prod(src.shape) * src.dtype.itemsize
+
+        @on(cond)
+        def _():
             pltpu.make_async_remote_copy(
                 src_ref=src,
                 dst_ref=dst,
-                send_sem=ss.at[group[1]],
+                send_sem=ss.at[group[0]],
                 recv_sem=rs.at[recv],
                 device_id=dev,
                 device_id_type=MESH,
             ).start()
 
-        when(cond, start)
-
     def drain(number):
-        for key, (cond, slot, size, bulk) in groups.items():
-            if key[0] == number:
+        for (when, cond, _), (slot, size, bulk) in groups.items():
+            if when == number:
                 rows = size // (w * 2)
                 assert bulk is not None or size == rows * w * 2 and rows % 16 == 0 and rows <= p.quarter, (rows, size)
                 ref = r.emb.at[0:rows] if bulk is None else bulk
 
-                def gone(ref=ref, slot=slot):
+                @on(cond)
+                def _():
                     pltpu.make_async_remote_copy(
                         src_ref=ref,
                         dst_ref=ref,
@@ -601,8 +623,6 @@
                         device_id=(core, dp),
                         device_id_type=MESH,
                     ).wait_send()
-
-                when(cond, gone)
 
     def arrived(dst, recv):
         pltpu.make_async_remote_copy(
@@ -614,12 +634,21 @@
             device_id_type=MESH,
         ).wait_recv()
 
+    near_small = (r.tok, r.seg, r.picks, r.b_in, r.b_out, r.gain, r.shift)
+    tok, seg, picks, b_in, b_out, gain, shift = near_small
+
+    def small_copy(i):
+        return pltpu.make_async_copy(far_small[i], near_small[i], ls.at[len(p.chunks) + 4 + i])
+
+    small_copy(0).start()
     for i, (at, size) in enumerate(p.chunks):
         pltpu.make_async_copy(emb_h.at[pl.ds(at, size)], r.emb.at[pl.ds(at, size)], ls.at[i]).start()
     l_w = len(p.chunks)
     lg, pos = r.lg, r.pos
     pltpu.make_async_copy(lg_h, lg, ls.at[l_w + 2]).start()
     pltpu.make_async_copy(pos_h, pos, ls.at[l_w + 3]).start()
+    for i in range(1, 7):
+        small_copy(i).start()
 
     def fill(par):
         par[0:1, :] = b_in[...].astype(F32)
@@ -627,15 +656,13 @@
         par[2:3, 0:w] = gain[...].astype(F32)
         par[3:4, 0:w] = shift[...].astype(F32)
 
-    pl.when(is_att)(lambda: fill(r.par_a))
-    pl.when(is_ff)(lambda: fill(r.par_f))
-
     barrier = pltpu.get_barrier_semaphore()
     peers = [(s, lax.rem(dp + k, n_dp)) for k in range(1, n_dp)]
     peers += [(core, dp), (across, dp), (3 - s, dp), (core, ydp)]
     for peer in peers:
         pl.semaphore_signal(barrier, inc=1, device_id=peer, device_id_type=MESH)
 
+    small_copy(0).wait()
     cols = [column(tok[m]) for m in range(2)]
     first = s * p.quarter
     for i, (at, size) in enumerate(p.chunks):
@@ -652,20 +679,25 @@
             r.acc[...] += part
     r.psend[...] = r.acc[pl.ds(pl.multiple_of(ln * other, ln), ln), :].astype(BF)
 
-    @pl.when(is_att)
+    @on(is_att)
     def _():
         pltpu.make_async_copy(w_in_h.at[0], r.wa, ls.at[l_w]).start()
 
-    @pl.when(is_ff)
+    @on(is_ff)
     def _():
         pltpu.make_async_copy(w_in_h.at[0], r.w1, ls.at[l_w]).start()
         pltpu.make_async_copy(w_out_h.at[0], r.w2, ls.at[l_w + 1]).start()
+
+    for i in range(1, 7):
+        small_copy(i).wait()
+    on(is_att)(lambda: fill(r.par_a))
+    on(is_ff)(lambda: fill(r.par_f))
 
     tiles = ff // w
     k_p, k_g = recvs.take(2), recvs.take(2)
     k_pa, k_pf, k_wa, k_w1, k_w2 = recvs.take(), recvs.take(), recvs.take(tiles), recvs.take(tiles), recvs.take(tiles)
     pl.semaphore_wait(barrier, len(peers))
-    send(None, r.psend, r.prow.at[0], (core, dp), k_p)
+    send(always, r.psend, r.prow.at[0], (core, dp), k_p)
 
 
     pltpu.make_async_copy(lg_h, lg, ls.at[l_w + 2]).wait()
@@ -686,8 +718,8 @@
     r.lgr[dp] = r.lgs[dp]
     for k in range(1, n_dp):
         to = lax.rem(dp + k, n_dp)
-        send(None, r.lgs.at[to], r.lgr.at[dp], (s, to), k_lg, r.lgs.at[0 : n_dp - 1], 1)
-        send(None, r.ids_own, r.ids_all.at[dp], (s, to), k_id, r.ids_all.at[0 : n_dp - 1], 2)
+        send(always, r.lgs.at[to], r.lgr.at[dp], (s, to), k_lg, r.lgs.at[0 : n_dp - 1], 1)
+        send(always, r.ids_own, r.ids_all.at[dp], (s, to), k_id, r.ids_all.at[0 : n_dp - 1], 2)
     arrived(r.prow.at[0], k_p)
     own_rows = r.acc[pl.ds(pl.multiple_of(ln * c, ln), ln), :]
     r.acc[0:ln, :] = own_rows + r.prow[0].astype(F32)
@@ -695,13 +727,13 @@
     send(at_x1, r.psum, r.prow.at[1], (across, dp), k_p + 1)
 
     def weights(cond):
-        send(both(is_att, cond), r.par_a, r.par_a, (core, dp), k_pa)
-        send(both(is_ff, cond), r.par_f, r.par_f, (core, dp), k_pf)
+        send(is_att | cond, r.par_a, r.par_a, (core, dp), k_pa)
+        send(is_ff | cond, r.par_f, r.par_f, (core, dp), k_pf)
         for j in range(tiles):
             cut = slice(j * w, (j + 1) * w)
-            send(both(is_att, cond), w_in_h.at[0, :, cut], r.wa.at[:, cut], (core, dp), k_wa + j, tag=3)
-            send(both(is_ff, cond), w_in_h.at[0, :, cut], r.w1.at[:, cut], (core, dp), k_w1 + j, tag=4)
-            send(both(is_ff, cond), w_out_h.at[0, cut, :], r.w2.at[cut, :], (core, dp), k_w2 + j, tag=5)
+            send(is_att | cond, w_in_h.at[0, :, cut], r.wa.at[:, cut], (core, dp), k_wa + j, tag=3)
+            send(is_ff | cond, w_in_h.at[0, :, cut], r.w1.at[:, cut], (core, dp), k_w1 + j, tag=4)
+            send(is_ff | cond, w_out_h.at[0, cut, :], r.w2.at[cut, :], (core, dp), k_w2 + j, tag=5)
 
     weights(at_x0)
 
@@ -711,36 +743,36 @@
             r.g[...] = part
         else:
             r.g[...] += part
-    send(None, r.g.at[pl.ds(pl.multiple_of(mp * other, mp), p.masks)], r.grow.at[0], (core, dp), k_g)
+    send(always, r.g.at[pl.ds(pl.multiple_of(mp * other, mp), p.masks)], r.grow.at[0], (core, dp), k_g)
 
     def masked_gradient():
         arrived(r.grow.at[0], k_g)
         r.gwide[...] = jnp.zeros(r.gwide.shape, F32)
         r.gwide[0 : p.masks, :] = r.g[pl.ds(pl.multiple_of(mp * c, mp), p.masks), :] + r.grow[0]
 
-    pl.when(at_x1)(masked_gradient)
+    on(at_x1)(masked_gradient)
     weights(at_x1)
 
     k_x = recvs.take()
 
-    @pl.when(at_x0)
+    @on(at_x0)
     def _():
         arrived(r.prow.at[1], k_p + 1)
         whole = r.acc[0:ln, :] + r.prow[1].astype(F32)
         r.x_a[...] = (whole + pos[...].astype(F32)).astype(BF)
 
-    @pl.when(is_att)
+    @on(is_att)
     def _():
         pltpu.make_async_copy(w_in_h.at[0], r.wa, ls.at[l_w]).wait()
         arrived(r.par_f, k_pf)
 
-    @pl.when(is_ff)
+    @on(is_ff)
     def _():
         pltpu.make_async_copy(w_in_h.at[0], r.w1, ls.at[l_w]).wait()
         pltpu.make_async_copy(w_out_h.at[0], r.w2, ls.at[l_w + 1]).wait()
         arrived(r.par_a, k_pa)
 
-    @pl.when(at_x1)
+    @on(at_x1)
     def _():
         arrived(r.x_a, k_x)
 
@@ -762,7 +794,7 @@
     rows_x = r.x_a[...]
 
     def wa_tile(j):
-        pl.when(is_ff)(lambda: arrived(r.wa.at[:, j * w : (j + 1) * w], k_wa + j))
+        on(is_ff)(lambda: arrived(r.wa.at[:, j * w : (j + 1) * w], k_wa + j))
 
     for j in range(3):
         wa_tile(j)
@@ -791,54 +823,82 @@
     resid = rows_x.astype(F32) + mm(r.ctx[...], r.wa[:, 3 * w : 4 * w]) + r.par_a[1:2, 0:w]
     r.x_f[...], r.n_a[...], r.inv_a[...] = norm_forward(resid, r.par_a)
 
-    def line(buf, base, owner):
-        own = buf(dp)
-        send(not_last, own, own, (s, dp + 2), base + dp)
-        send(not_first, own, own, (s, dp - 2), base + dp)
-        send(is_att, own, own, (core, dp), owner + dp)
-        to_y(buf, base, dp, None, owner)
-
-    def to_y(buf, base, i, cond, owner):
-        whose = jnp.where(is_att, core, s)
-        send(cond, buf(i), buf(i), (whose, ydp), jnp.where(is_att, owner, base) + i)
+    class Gather:
+        def __init__(self, buf):
+            self.buf = buf
+            self.near, self.far, self.own, self.core0 = recvs.take(nz), recvs.take(2), recvs.take(), recvs.take(4)
+
+        def at(self, zz, yy):
+            return self.buf.at[c, zz, yy]
+
+        def pair(self, m, half_z, yy):
+            return self.buf.at[m, pl.ds(2 * half_z, 2), yy]
+
+        def start(self):
+            own = self.at(z, y)
+            send(not_last, own, own, (s, dp + 2), self.near + z)
+            send(not_first, own, own, (s, dp - 2), self.near + z)
+            send(is_att, own, own, (core, dp), self.own)
+            self.to_y(z, always)
+
+        def to_y(self, zz, cond):
+            recv = jnp.where(c == 0, self.core0 + 2, self.far) + zz // 2
+            send(cond, self.at(zz, y), self.at(zz, y), (jnp.where(c == 0, core, s), ydp), recv)
+
+        def step(self, t, cond=always):
+            for sign in (-1, 1):
+                here, zz = at_distance(t, sign, cond)
+                piece = self.at(zz, y)
+                on(here)(lambda piece=piece, zz=zz: arrived(piece, self.near + zz))
+                if t < nz - 1:
+                    send(onward(here, sign), piece, piece, (s, dp - 2 * sign), self.near + zz)
+                send(here | is_att, piece, piece, (core, dp), self.core0 + zz // 2)
+
+        def cross(self, t, cond=always):
+            for sign in (-1, 1):
+                here, zz = at_distance(t, sign, cond)
+                self.to_y(zz, here)
+
+        def from_core0(self, half_z, own_side):
+            if own_side:
+                mine = (z // 2) == half_z
+
+                @pl.when(mine)
+                def _():
+                    arrived(self.buf.at[0, z + 1 - 2 * lax.rem(z, 2), y], self.core0 + half_z)
+
+                @pl.when(jnp.logical_not(mine))
+                def _():
+                    arrived(self.pair(0, half_z, y), self.core0 + half_z)
+
+            else:
+                arrived(self.pair(0, half_z, 1 - y), self.core0 + 2 + half_z)
+
+        def from_y(self, half_z):
+            arrived(self.pair(1, half_z, 1 - y), self.far + half_z)
 
     def at_distance(t, sign, cond):
-        here = both(cond, at_least(t) if sign < 0 else at_most(nz - 1 - t))
-        return here, jnp.clip(z + sign * t, 0, nz - 1) * 2 + y
+        here = cond | (at_least(t) if sign < 0 else at_most(nz - 1 - t))
+        return here, jnp.clip(z + sign * t, 0, nz - 1)
 
     def onward(here, sign):
-        return both(here, not_last if sign < 0 else not_first)
-
-    def line_step(buf, base, t, cond, owner):
-        for sign in (-1, 1):
-            here, from_dp = at_distance(t, sign, cond)
-            piece = buf(from_dp)
-            when(here, lambda piece=piece, from_dp=from_dp: arrived(piece, base + from_dp))
-            if t < nz - 1:
-                send(onward(here, sign), piece, piece, (s, dp - 2 * sign), base + from_dp)
-            send(both(here, is_att), piece, piece, (core, dp), owner + from_dp)
-
-    def line_cross(buf, base, t, cond, owner):
-        for sign in (-1, 1):
-            here, from_dp = at_distance(t, sign, cond)
-            to_y(buf, base, from_dp, here, owner)
+        return here | (not_last if sign < 0 else not_first)
 
     def pair_line(buf, base, cond, i):
         piece = buf(i)
-        send(both(cond, not_last), piece, piece, (s, dp + 2), base + i)
-        send(both(cond, not_first), piece, piece, (s, dp - 2), base + i)
+        send(cond | not_last, piece, piece, (s, dp + 2), base + i)
+        send(cond | not_first, piece, piece, (s, dp - 2), base + i)
 
     def pair_step(buf, base, t, cond, on_x):
         for sign in (-1, 1):
             for side in (0, 1):
-                here, from_dp = at_distance(t, sign, cond)
-                if side:
-                    from_dp = from_dp + 1 - 2 * y
+                here, zz = at_distance(t, sign, cond)
+                from_dp = 2 * zz + (1 - y if side else y)
                 piece = buf(from_dp)
-                when(here, lambda piece=piece, from_dp=from_dp: arrived(piece, base + from_dp))
+                on(here)(lambda piece=piece, from_dp=from_dp: arrived(piece, base + from_dp))
                 if t < nz - 1:
                     send(onward(here, sign), piece, piece, (s, dp - 2 * sign), base + from_dp)
-                send(here, piece, piece, (across, dp), on_x + from_dp)
+                send(here, piece, piece, (across, dp), on_x)
 
     def ch(i):
         return r.ch_all.at[c, i]
@@ -846,28 +906,20 @@
     def de(i):
         return r.de_all.at[1 - x, i]
 
-    def xs(i):
-        return r.x_all.at[c, i // 2, lax.rem(i, 2)]
-
-    def db(i):
-        return r.db_all.at[c, i // 2, lax.rem(i, 2)]
-
-    k_ch, k_xs, k_db = (recvs.take(n_dp) for _ in range(3))
-    k_dr = recvs.take(2 * n_dp)
-    k_row = k_dr + (1 - x) * n_dp
-    k_cho, k_chc, k_cha, k_chx, k_dp = (recvs.take() for _ in range(5))
+    k_row, k_pass = recvs.take(n_dp), recvs.take()
+    k_ch, k_cho, k_chc, k_chp, k_chq, k_cha, k_chx, k_dp = (recvs.take() for _ in range(8))
     k_dex = recvs.take(2)
-    k_xsc, k_dbc = recvs.take(n_dp), recvs.take(n_dp)
+    xs, db = Gather(r.x_all), Gather(r.db_all)
 
     r.x_all[c, z, y] = r.x_f[...]
-    line(xs, k_xs, k_xsc)
+    xs.start()
 
     def feed(rows_x, keep=True):
         total = rows_x.astype(F32) + r.par_f[1:2, 0:w]
         for j in range(tiles):
             cut = slice(j * w, (j + 1) * w)
 
-            @pl.when(is_att)
+            @on(is_att)
             def _():
                 arrived(r.w1.at[:, cut], k_w1 + j)
                 arrived(r.w2.at[cut, :], k_w2 + j)
@@ -884,17 +936,18 @@
         else:
             r.y_o[...] = result
 
-    pl.when(is_ff | at_x1)(lambda: feed(r.x_f[...]))
-    send(both(at_x0, is_ff), r.y_f, r.x_a, (across, dp), k_x)
-
-    @pl.when(at_x0 & is_ff)
-    def _():
-        arrived(r.x_all.at[0, z, y], k_xsc + dp)
+    on(on_0)(lambda: feed(r.x_f[...]))
+    on(at_x1)(lambda: feed(r.x_f[...]))
+    send(at_x0 | is_ff, r.y_f, r.x_a, (across, dp), k_x)
+
+    @on(at_x0 | is_ff)
+    def _():
+        arrived(r.x_all.at[0, z, y], xs.own)
         feed(r.x_all[0, z, y], False)
 
-    send(both(at_x0, is_ff), r.y_o, r.x_a, (3 - s, dp), k_x)
-
-    @pl.when(at_x1)
+    send(at_x0 | is_ff, r.y_o, r.x_a, (3 - s, dp), k_x)
+
+    @on(at_x1)
     def _():
         r.mrow[...] = jnp.full(r.mrow.shape, -1, jnp.int32)
         r.mrow[0:1, 0 : p.masks] = picks[c]
@@ -908,19 +961,21 @@
 
     send(at_x1, r.ch_own, r.ch_own, (across, dp), k_cho)
     send(at_x1, r.ch_own, r.ch_two, (core, dp), k_chc)
-
-    def push(owner, kind, src, dst, cond=None):
+    send(at_x1, r.ch_own, r.ch_pair, (s, ydp), k_chp)
+
+    def push(owner, kind, src, dst, cond=always):
         home, away = (is_att, is_ff) if owner == 0 else (is_ff, is_att)
-        slot_y = 2 + jnp.where(home, 0, 1)
+        at_home = holds("att" if owner == 0 else "ff")
+        slot_y = 2 + jnp.where(at_home, 0, 1)
         own_dst, near_dst, far_dst = dst(0), dst(1), dst(slot_y)
 
 
-        @pl.when(both(home, cond))
+        @on(home | cond)
         def _():
             own_dst[...] = src(y)[...]
 
-        send(both(away, cond), src(y), near_dst, (core, dp), kind)
-        send(cond, src(1 - y), far_dst, (jnp.where(home, s, core), ydp), kind)
+        send(away | cond, src(y), near_dst, (core, dp), kind)
+        send(cond, src(1 - y), far_dst, (jnp.where(at_home, s, core), ydp), kind)
 
     def gathered(kind, dst):
         arrived(dst(slice(1, 4)), kind)
@@ -943,42 +998,15 @@
     def push_dh(j):
         push(0, k_dh[j], lambda i: r.dpk.at[:, j * w : (j + 1) * w], to_dh(j))
 
-    def push_rows(cond):
-        push(0, k_xt, lambda i: r.xt_a.at[:, i], to_x, cond)
-        push(0, k_ctx, lambda i: r.ct_a.at[:, i], to_ctx, cond)
+    def push_rows():
+        push(0, k_xt, lambda i: r.xt_a.at[:, i], to_x)
+        push(0, k_ctx, lambda i: r.ct_a.at[:, i], to_ctx)
 
     def turn():
         for dst, src in ((r.xt_a, r.x_a), (r.ct_a, r.ctx)):
             turned = src[...].T
             for b in range(n_dp):
                 dst[b // 2, b % 2] = turned[b * p.in_rows : (b + 1) * p.in_rows]
-
-    stage[0] = 1
-    @pl.when(at_x0)
-    def _():
-        masked_gradient()
-        turn()
-
-    send(at_x0, r.gwide.at[0 : p.masks], r.grow.at[1], (across, dp), k_g + 1)
-    push_rows(at_x0)
-
-    @pl.when(at_x0 & is_att)
-    def _():
-        feed(r.x_f[...])
-
-    for t in (1, 2):
-        line_step(xs, k_xs, t, at_x0, k_xsc)
-        line_cross(xs, k_xs, t, at_x0, k_xsc)
-
-    @pl.when(at_x0)
-    def _():
-        arrived(r.ch_own, k_cho)
-        r.ch_all[c, dp] = r.ch_own[...]
-
-    send(at_x0, r.ch_own, r.ch_two, (core, dp), k_chc)
-    send(at_x0, r.ch_own, ch(dp), (s, ydp), k_ch + dp)
-    for k in range(1, nz):
-        send(at_x0, r.ch_own, ch(dp), (s, lax.rem(dp + 2 * k, n_dp)), k_ch + dp)
 
     def emit(i, src):
         pltpu.make_async_copy(src, outs[i], os.at[i]).start()
@@ -992,13 +1020,30 @@
             o_log[other, 0, :, at : at + size] = part[mp : mp + p.masks].astype(BF)
         emit(0, o_log)
 
-    pl.when(at_x0)(logits)
-    line_step(xs, k_xs, 3, at_x0, k_xsc)
-    line_cross(xs, k_xs, 3, at_x0, k_xsc)
+    @on(at_x0)
+    def _():
+        masked_gradient()
+        send(at_x0, r.gwide.at[0 : p.masks], r.grow.at[1], (across, dp), k_g + 1)
+        turn()
+        push_rows()
+        on(is_att)(lambda: feed(r.x_f[...]))
+        for t in (1, 2):
+            xs.step(t)
+            xs.cross(t)
+        arrived(r.ch_own, k_cho)
+        r.ch_all[c, dp] = r.ch_own[...]
+        send(at_x0, r.ch_own, r.ch_two, (core, dp), k_chc)
+        for k in range(1, nz):
+            send(at_x0, r.ch_own, ch(dp), (s, lax.rem(dp + 2 * k, n_dp)), k_ch)
+        logits()
+        xs.step(3)
+        xs.cross(3)
+
+    stage[0] = 1
 
     k_dy = recvs.take()
 
-    @pl.when(at_x0)
+    @on(at_x0)
     def _():
         arrived(r.dyin, k_dy)
         r.dyf[...] = r.dyin[...].astype(F32)
@@ -1024,7 +1069,7 @@
     dres, gain_part, shift_part = norm_backward(r.par_f, r.n_f, r.inv_f)
     r.dres[...] = dres
     r.db_all[c, z, y] = dres.astype(BF)
-    line(db, k_db, k_dbc)
+    db.start()
     branch = r.db_all[c, z, y]
     total = r.dres[...]
     for j in range(tiles):
@@ -1034,8 +1079,11 @@
         total = total + mm_nt(dhidden, r.w1[:, cut])
     r.dyf[...] = total.astype(BF).astype(F32)
     r.vecs[0:1], r.vecs[1:2] = gain_part, shift_part
-    line_step(xs, k_xs, 1, at_x1, k_xsc)
-    line_cross(xs, k_xs, 1, at_x1, k_xsc)
+
+    @on(at_x1)
+    def _():
+        xs.step(1)
+        xs.cross(1)
 
     dres, gain_part, shift_part = norm_backward(r.par_a, r.n_a, r.inv_a)
     r.dres[...] = dres
@@ -1068,43 +1116,34 @@
     def row(m, i):
         return r.de_all.at[m, i]
 
-    on_0, on_1 = both(at_x0, is_ff), both(at_x1, is_ff)
-    away = jnp.where(is_ff, across, 3 - s)
+    away = jnp.where(c == 1, across, 3 - s)
 
     def hand_on(src, i):
-        send(at_x0, src, row(c, i), (away, dp), k_dr + c * n_dp + i)
-        send(both(at_x0, is_att), src, row(0, i), (core, dp), k_dr + i)
-
-        @pl.when(on_0)
+        send(at_x0, src, row(c, i), (away, dp), jnp.where(c == 1, k_pass, k_row + i))
+        send(at_x0 | is_att, src, row(0, i), (core, dp), k_pass)
+
+        @on(on_0)
         def _():
             r.de_all[1, i] = src[...]
-
-    send(at_x0, r.dx, r.dx_pair, (s, ydp), k_dp)
-    hand_on(r.dx, dp)
-    pair_line(de, k_row, on_0, dp)
-
-    stage[0] = 2
-    pl.when(at_x1)(turn)
-    push_rows(at_x1)
+            pair_line(de, k_row, on_0, i)
+
+    @on(at_x0)
+    def _():
+        send(at_x0, r.dx, r.dx_pair, (s, ydp), k_dp)
+        hand_on(r.dx, dp)
+
+    @on(is_att)
+    def _():
+        o_wout[...] = jnp.zeros(o_wout.shape, BF)
+        emit(4, o_wout)
+
+    @on(at_x1)
+    def _():
+        turn()
+        push_rows()
+
     push(0, k_dba, lambda i: r.dbr_a, to_dbr)
     push_dh(0)
-    push_dh(1)
-    line_step(xs, k_xs, 2, at_x1, k_xsc)
-    line_step(db, k_db, 1, None, k_dbc)
-
-
-    @pl.when(at_x0)
-    def _():
-        arrived(r.dx_pair, k_dp)
-
-    hand_on(r.dx_pair, ydp)
-    pair_line(de, k_row, on_0, ydp)
-    line_cross(xs, k_xs, 2, at_x1, k_xsc)
-    for k in range(1, nz):
-        i = lax.rem(dp + 2 * k, n_dp)
-        pl.when(at_x0)(lambda i=i: arrived(ch(i), k_ch + i))
-        send(at_x0, ch(i), ch(i), (s, ydp), k_ch + i)
-    line_cross(db, k_db, 1, None, k_dbc)
     small(r.sm_f, jnp.sum(r.db_all[c, z, y].astype(F32), 0, keepdims=True), r.vecs[0:1], r.vecs[1:2])
     push(1, k_sm, lambda i: r.sm_f, to_sm)
     r.bsum[...] = jnp.zeros(r.bsum.shape, F32)
@@ -1113,15 +1152,41 @@
         r.bsum[:, cut] = jnp.sum(r.dpk[:, cut].astype(F32), 0, keepdims=True)
     small(r.sm_a, jnp.sum(branch.astype(F32), 0, keepdims=True), gain_part, shift_part)
     push(0, k_sm, lambda i: r.sm_a, to_sm)
+    push_dh(1)
+
+    @on(at_x1)
+    def _():
+        arrived(r.ch_pair, k_chp)
+        send(at_x1, r.ch_pair, r.ch_far, (across, dp), k_chq)
+        xs.step(2)
+
+    db.step(1)
+
+    @on(at_x0)
+    def _():
+        arrived(r.dx_pair, k_dp)
+        hand_on(r.dx_pair, ydp)
+
+    on(at_x1)(lambda: xs.cross(2))
+    db.cross(1)
     push_dh(2)
-    for t in (2, 3):
-        if t == 2:
-            line_step(xs, k_xs, 3, at_x1, k_xsc)
-            line_cross(xs, k_xs, 3, at_x1, k_xsc)
-        line_step(db, k_db, t, None, k_dbc)
-        line_cross(db, k_db, t, None, k_dbc)
-        if t == 2:
-            drain(0)
+
+    @on(at_x1)
+    def _():
+        xs.step(3)
+        xs.cross(3)
+
+    db.step(2)
+    db.cross(2)
+
+    @on(at_x0)
+    def _():
+        arrived(r.ch_far, k_chq)
+        r.ch_all[c, ydp] = r.ch_far[...]
+        for k in range(1, nz):
+            send(at_x0, r.ch_far, ch(ydp), (s, lax.rem(dp + 2 * k, n_dp)), k_ch)
+
+    drain(0)
 
     def head_part():
         arrived(r.ch_all.at[other], k_chx)
@@ -1134,10 +1199,8 @@
         grad = mm_tn(r.lgr[...].reshape(lines, p.share_pad), r.ch_pack[...].reshape(lines, w))
         o_tab[...] = grad[0 : p.share]
 
-    k_in = [recvs.take(4) for _ in range(tiles)]
+    k_in = [recvs.take(3) for _ in range(tiles)]
     half = nz * p.in_rows
-    outer = (z == 0) | (z == nz - 1)
-    outer_att, inner = both(is_att, outer), both(is_att, jnp.logical_not(outer))
     mate = z + 1 - 2 * lax.rem(z, 2)
     far_base = 2 - 2 * (z // 2)
 
@@ -1150,7 +1213,7 @@
     def attention_tile(j):
         cut = tile_cut(j)
 
-        @pl.when(is_att)
+        @on(is_att)
         def _():
             if j == 3:
                 gathered(k_ctx, to_ctx)
@@ -1165,20 +1228,19 @@
 
         to_mate = (s, 2 * mate + y)
         for k in range(2):
-            send(outer_att, shard(far_base + k, cut), r.r_in.at[2 + k, :, cut], to_mate, k_in[j] + 2 + k)
+            send(outer_att, shard(far_base + k, cut), r.r_in.at[2 + k, :, cut], to_mate, k_in[j] + 2)
         send(is_att, shard(mate, cut), r.r_in.at[0, :, cut], to_mate, k_in[j])
 
     def attention_sum(j):
         cut = tile_cut(j)
-        for k in range(2):
-
-            @pl.when(inner)
-            def _():
-                arrived(r.r_in.at[2 + k, :, cut], k_in[j] + 2 + k)
+
+        @on(inner)
+        def _():
+            arrived(r.r_in.at[2:4, :, cut], k_in[j] + 2)
+            for k in range(2):
                 rows = pl.ds(pl.multiple_of((far_base + k) * p.in_rows, p.in_rows), p.in_rows)
                 r.wa[rows, cut] = (r.wa[rows, cut].astype(F32) + r.r_in[2 + k, :, cut].astype(F32)).astype(BF)
-
-            send(inner, shard(far_base + k, cut), r.r_in.at[1, :, cut], (s, 2 * (far_base + k) + y), k_in[j] + 1)
+                send(inner, shard(far_base + k, cut), r.r_in.at[1, :, cut], (s, 2 * (far_base + k) + y), k_in[j] + 1)
 
     def unit_grads(yy, i):
         def four(buf):
@@ -1192,19 +1254,16 @@
         r.u_out[...] += mm_tn((hidden * below).astype(BF), up)
         r.w_col[...] += mm_tn(rows_x, dhidden)
 
-    def units_of(yy, i):
-        for k in range(2):
-            d = 4 * i + 2 * k + yy
-            pl.when((d != dp) | at_x1)(lambda d=d: arrived(r.x_all.at[0, d // 2, lax.rem(d, 2)], k_xsc + d))
-            arrived(r.db_all.at[0, d // 2, lax.rem(d, 2)], k_dbc + d)
-        unit_grads(yy, i)
+    def units_here(t):
+        for one in (xs, db):
+            one.from_core0(t, True)
+        unit_grads(y, t)
 
     def units_over_y(t):
-        for buf, base in ((xs, k_xs), (db, k_db)):
-            for k in range(2):
-                d = 4 * t + 2 * k + 1 - y
-                arrived(buf(d), base + d)
-        units_of(1 - y, t)
+        for one in (xs, db):
+            one.from_core0(t, False)
+            one.from_y(t)
+        unit_grads(1 - y, t)
 
     entry = iota((p.share_rows, ln), 0) + (s * p.quarter + dp * p.share)
 
@@ -1227,79 +1286,72 @@
         send(cond, r.de_all.at[1 - x], r.de_all.at[1 - x], (core, dp), k_dex + (1 - x))
 
     attention_tile(3)
-    pair_step(de, k_row, 1, on_0, k_row)
+    pair_step(de, k_row, 1, on_0, k_pass)
     attention_tile(0)
+    db.step(3)
+    db.cross(3)
     attention_sum(3)
-    pair_step(de, k_row, 2, on_0, k_row)
-    pair_step(de, k_row, 3, on_0, k_row)
-    gathered_row(on_0)
-
-    @pl.when(is_ff)
+    pair_step(de, k_row, 2, on_0, k_pass)
+
+    @on(at_x0)
+    def _():
+        arrived(r.ch_all.at[c, 0 : n_dp - 2], k_ch)
+        send(at_x0, r.ch_all.at[c], r.ch_all.at[c], (across, dp), k_cha)
+        send(at_x0, r.ch_all.at[c], r.ch_all.at[c], (core, dp), k_chx)
+
+
+    @on(is_ff)
     def _():
         r.u_out[...] = jnp.zeros(r.u_out.shape, F32)
         r.w_col[...] = jnp.zeros(r.w_col.shape, F32)
-        units_of(y, z // 2)
-        units_of(y, mate_half)
+        on(at_x1)(lambda: arrived(r.x_all.at[0, z, y], xs.own))
+        arrived(r.db_all.at[0, z, y], db.own)
+        units_here(z // 2)
+        units_here(mate_half)
 
     attention_tile(1)
     attention_sum(0)
 
-    @pl.when(at_x0)
-    def _():
-        for zz in range(nz):
-            i = 2 * zz + 1 - y
-            arrived(ch(i), k_ch + i)
-
-    send(at_x0, r.ch_all.at[c], r.ch_all.at[c], (across, dp), k_cha)
-    send(at_x0, r.ch_all.at[c], r.ch_all.at[c], (core, dp), k_chx)
-
-    @pl.when(on_1)
-    def _():
-        arrived(row(0, dp), k_dr + dp)
-
-    pair_line(de, k_row, on_1, dp)
-    pl.when(at_x1)(logits)
-
-    @pl.when(on_1)
-    def _():
-        arrived(row(0, ydp), k_dr + ydp)
-
-    pair_line(de, k_row, on_1, ydp)
-    pair_step(de, k_row, 1, on_1, k_row)
+    def row_0(i):
+        @on(on_1)
+        def _():
+            arrived(row(0, i), k_row + i)
+            pair_line(de, k_row, on_1, i)
+
+    row_0(dp)
+    on(at_x1)(logits)
+    row_0(ydp)
+    pair_step(de, k_row, 1, on_1, k_pass)
     attention_sum(1)
+
+    attention_tile(2)
+    pair_step(de, k_row, 2, on_1, k_pass)
 
     gathered(k_sm, to_sm)
     r.sm_tot[...] = r.b_sm[0] + r.b_sm[1] + r.b_sm[2] + r.b_sm[3]
     r.r_sm[z] = r.sm_tot[...]
     for k in range(1, nz):
         zz = lax.rem(z + k, nz)
-        send(None, r.sm_tot, r.r_sm.at[z], (s, 2 * zz + y), k_smz)
-
-    attention_tile(2)
-    pair_step(de, k_row, 2, on_1, k_row)
-    pair_step(de, k_row, 3, on_1, k_row)
-    gathered_row(on_1)
+        send(always, r.sm_tot, r.r_sm.at[z], (s, 2 * zz + y), k_smz)
+
     attention_sum(2)
 
+    @on(is_ff)
+    def _():
+        units_over_y(z // 2)
+
+    pair_step(de, k_row, 3, is_ff, k_pass)
+    gathered_row(is_ff)
+
     def passed_row(cond):
-        @pl.when(cond)
+        @on(cond)
         def _():
-            for i in range(n_dp):
-                arrived(row(x, i), k_dr + x * n_dp + i)
+            arrived(r.de_all.at[x], k_pass)
 
         send(cond, r.de_all.at[x], r.de_all.at[x], (core, dp), k_dex + x)
 
-    passed_row(on_1)
-
-    @pl.when(at_x1)
-    def _():
-        arrived(r.ch_all.at[c], k_cha)
-
-    send(at_x1, r.ch_all.at[c], r.ch_all.at[c], (core, dp), k_chx)
-
-    @pl.when(is_ff)
-    def _():
-        units_over_y(z // 2)
+    @on(is_ff)
+    def _():
         units_over_y(mate_half)
         o_wout[0] = r.u_out[...].astype(BF)
         emit(4, o_wout)
@@ -1310,18 +1362,20 @@
     for k in (4, 5, 3, 2, 6, 1, 7) if n_dp == 8 else range(1, n_dp):
         to = lax.rem(dp + k, n_dp)
         send(is_ff, r.w_send.at[to], r.r_col.at[dp], (s, to), k_col)
-    passed_row(on_0)
+    passed_row(is_ff)
+
+    @on(at_x1)
+    def _():
+        arrived(r.ch_all.at[c], k_cha)
+        send(at_x1, r.ch_all.at[c], r.ch_all.at[c], (core, dp), k_chx)
+
 
     head_part()
 
-    @pl.when(is_att)
-    def _():
-        arrived(r.de_all.at[0], k_dex)
-        arrived(r.de_all.at[1], k_dex + 1)
-
-    scatter(0)
-    scatter(1)
-    drain(1)
+    on(is_att)(lambda: arrived(r.de_all.at[1 - x], k_dex + 1 - x))
+    scatter(1 - x)
+    on(is_att)(lambda: arrived(r.de_all.at[x], k_dex + x))
+    scatter(x)
     n_pos = ln // n_dp
     here = pl.ds(pl.multiple_of(dp * n_pos, n_pos), n_pos)
     total = jnp.zeros((n_pos, w), F32)
@@ -1332,7 +1386,7 @@
     emit(1, o_tab)
     emit(2, o_pos)
 
-    @pl.when(is_att)
+    @on(is_att)
     def _():
         mine = pl.ds(pl.multiple_of(z * p.in_rows, p.in_rows), p.in_rows)
         for j in (3, 0, 1, 2):
@@ -1341,16 +1395,14 @@
             arrived(r.r_in.at[1, :, cut], k_in[j] + 1)
             near_sum = r.wa[mine, cut].astype(F32) + r.r_in[0, :, cut].astype(F32)
             o_win[0, :, cut] = (near_sum + r.r_in[1, :, cut].astype(F32)).astype(BF)
-        o_wout[...] = jnp.zeros(o_wout.shape, BF)
-        emit(4, o_wout)
-
-    @pl.when(is_ff)
+            pltpu.make_async_copy(o_win.at[:, :, cut], outs[3].at[:, :, cut], os.at[3]).start()
+
+    @on(is_ff)
     def _():
         arrived(r.r_col.at[0 : n_dp - 1], k_col)
         for k in range(n_dp):
-            o_win[0, :, k * p.out_rows : (k + 1) * p.out_rows] = r.r_col[k]
-
-    emit(3, o_win)
+            cut = slice(k * p.out_rows, (k + 1) * p.out_rows)
+            pltpu.make_async_copy(r.r_col.at[k], outs[3].at[0, :, cut], os.at[3]).start()
 
     arrived(r.r_sm.at[0 : nz - 1], k_smz)
     r.sm_all[...] = r.r_sm[0] + r.r_sm[1] + r.r_sm[2] + r.r_sm[3]
@@ -1358,7 +1410,7 @@
     for i, src in enumerate((o_log, o_tab, o_pos, o_win, o_wout, o_vec)):
         pltpu.make_async_copy(src, outs[i], os.at[i]).wait()
 
-    drain(2)
+    drain(1)
     assert sends.n <= SENDS and recvs.n <= RECVS, (sends.n, recvs.n)
 
 
@@ -1436,7 +1488,6 @@
         (1, p.in_rows),
         (1, p.in_rows),
     ]
-    vmem = pl.BlockSpec(memory_space=pltpu.VMEM)
     far = pl.BlockSpec(memory_space=pl.ANY)
     part_types = [BF, F32, F32, BF, BF]
     parts = [jax.ShapeDtypeStruct(shape, kind) for shape, kind in zip(shapes, part_types)]
@@ -1444,13 +1495,13 @@
     summed = pl.pallas_call(
         functools.partial(fused, p, list(scratch)),
         out_shape=parts,
-        in_specs=[vmem] * 7 + [far] * 5,
+        in_specs=[far] * 12,
         out_specs=[far] * 6,
         scratch_shapes=[pltpu.VMEM(*one) for one in scratch.values()]
         + [
             pltpu.SemaphoreType.DMA((SENDS,)),
             pltpu.SemaphoreType.DMA((RECVS,)),
-            pltpu.SemaphoreType.DMA((len(p.chunks) + 4,)),
+            pltpu.SemaphoreType.DMA((len(p.chunks) + 11,)),
             pltpu.SemaphoreType.DMA((6,)),
         ],
         compiler_params=pltpu.CompilerParams(

time: 109 us -> 104 us (0.954); the launches traced: 108 us -> 102 us
  Pallas kernels: 108 us -> 101 us
    pallas_call x1, Pallas kernels: 104 us -> 97.8 us  [whole(): pl.pallas_call(functools.partial(fused, p, list(scratch)), out_shape=part...]
where the time goes in v5:
time: 104 us; the launch traced here: 102 us
  Pallas kernels  101 us (97%)
    pallas_call x1, Pallas kernels, whole(): pl.pallas_call(functools.partial(fused, p, list(scratch)), out_shape=part...  97.8 us
    pallas_call x1, Pallas kernels, whole(): pl.pallas_call(functools.partial(finish, p), out_shape=[jax.ShapeDtypeStr...  3.55 us

profile of v5, /device:TPU:1, one launch (start us, length us, event | category | flops | bytes accessed | tf_op | source)
XLA Modules:
  0.0 102.2 jit_solution(10636967442537341779)
XLA Ops:
  0.6 97.8 %shard_map.187 = (bf16[2,1,40,3648]{3,2,1,0:T(8,128)(2,1)}, f32[456,768]{1,0:T(8,128)}, f32[16,768]{1,0:T(8,128)}, bf16[1,96,3072]{2,1,0:T(8,128)(2,1)}, bf16[1,384,768]{2,1,0:T(8,128)(2,1)}, /*index=5*/f32[8,768]{1,0:T(8,128)}) custom-call(s32[2,1,128]{2,1,0:T(1,128)} %refs_0_.1, s32[2,1,128]{2,1,0:T(1,128)} %refs_1_.1, s32[2,1,40]{2,1,0:T(1,128)} %refs_2_.1, ...), custom_call_target="tpu_custom_call" | custom-call | tf_op jit(solution)/shard_map/pallas_call | solution.py:1495
  98.4 3.5 %shard_map.188 = (f32[2,1,40,3648]{3,2,1,0:T(8,128)}, f32[456,768]{1,0:T(8,128)}, f32[16,768]{1,0:T(8,128)}, f32[1,96,3072]{2,1,0:T(8,128)}, f32[1,384,768]{2,1,...) custom-call(bf16[2,1,40,3648]{3,2,1,0:T(8,128)(2,1)} %get-tuple-element.15.refs_0_, ...), custom_call_target="tpu_custom_call" | custom-call | tf_op jit(solution)/shard_map/pallas_call | solution.py:1536

commit v6 on v5

--- a/solution.py
+++ b/solution.py
@@ -385,8 +385,8 @@
     )
 
 
-SENDS = 91
-RECVS = 84
+SENDS = 95
+RECVS = 88
 VMEM_LIMIT = 64 * 2**20
 BF = jnp.bfloat16
 F32 = jnp.float32
@@ -459,16 +459,17 @@
         wa=((w, ff), BF),
         w1=((w, ff), BF),
         w2=((ff, w), BF),
+        w1t=((ff, w), BF),
+        w2t=((w, ff), BF),
         par_a=((8, ff), F32),
         par_f=((8, ff), F32),
-        acc=((2 * ln, w), F32),
         psend=((ln, w), BF),
         psum=((ln, w), BF),
         prow=((2, ln, w), BF),
         lgp=((2 * mp, p.quarter), BF),
         lgs=((p.n_dp, 2 * p.masks, p.share_pad), BF),
         lgr=((p.n_dp, 2 * p.masks, p.share_pad), BF),
-        ch_pack=((p.n_dp, 2 * p.masks, w), BF),
+
         g=((2 * mp, w), F32),
         grow=((2, p.masks, w), F32),
         gwide=((ln, w), F32),
@@ -476,9 +477,7 @@
         ids_own=((8, ln), jnp.int32),
         ids_all=((p.n_dp, 8, ln), jnp.int32),
         x_a=((ln, w), BF),
-        x_f=((ln, w), BF),
         y_f=((ln, w), BF),
-        y_o=((ln, w), BF),
         pk=((ln, 3 * w), BF),
         ctx=((ln, w), BF),
         probs=((w // 128, ln, 256), F32),
@@ -503,17 +502,14 @@
         sm_f=((8, w), F32),
         b_ctx=((p.nz, p.in_rows, 4 * ln), BF),
         b_x=((p.nz, p.in_rows, 4 * ln), BF),
-        b_dbr=((4 * ln, w), BF),
-        b_dh=((4 * ln, 3 * w), BF),
         b_sm=((4, 8, w), F32),
         sm_tot=((8, w), F32),
         sm_all=((8, w), F32),
         r_sm=((p.nz, 8, w), F32),
-        r_in=((4, p.in_rows, ff), BF),
+        r_in=((5, p.in_rows, ff), BF),
         x_all=((2, p.nz, 2, ln, w), BF),
         db_all=((2, p.nz, 2, ln, w), BF),
         w_col=((w, p.out_rows), F32),
-        w_send=((p.n_dp, p.in_rows, p.out_rows), BF),
         r_col=((p.n_dp, p.in_rows, p.out_rows), BF),
         ch_own=((mp, w), BF),
         ch_two=((mp, w), BF),
@@ -522,11 +518,8 @@
         ch_all=((2, p.n_dp, mp, w), BF),
         de_all=((2, p.n_dp, ln, w), BF),
         u_out=((p.out_rows, w), F32),
-        o_log=((2, 1, p.masks, p.quarter), BF),
         o_tab=((p.share, w), F32),
         o_pos=((ln // p.n_dp, w), F32),
-        o_win=((1, p.in_rows, ff), BF),
-        o_wout=((1, p.out_rows, w), BF),
     )
 
 
@@ -535,7 +528,9 @@
     outs = refs[12:18]
     r = types.SimpleNamespace(**dict(zip(names, refs[18:])))
     ss, rs, ls, os = refs[18 + len(names) :]
-    (o_log, o_tab, o_pos, o_win, o_wout, o_vec) = (r.o_log, r.o_tab, r.o_pos, r.o_win, r.o_wout, r.sm_all)
+    acc, o_log = r.u_out.at[0 : 2 * p.length], r.lg
+    o_win = r.r_in.at[0:1]
+    (o_tab, o_pos, o_wout, o_vec) = (r.o_tab, r.o_pos, r.w1t.at[1024 : 1024 + p.out_rows], r.sm_all)
     w, ff, ln, mp, nz, n_dp = p.width, p.ff, p.length, p.mask_pad, p.nz, p.n_dp
     heads = w // 64
     pairs = heads // 2
@@ -674,10 +669,10 @@
             hot.append(jnp.where(wide == lane, 1.0, 0.0).astype(BF))
         part = mm(jnp.concatenate(hot, 0), r.emb[at : at + size, :])
         if i == 0:
-            r.acc[...] = part
+            acc[...] = part
         else:
-            r.acc[...] += part
-    r.psend[...] = r.acc[pl.ds(pl.multiple_of(ln * other, ln), ln), :].astype(BF)
+            acc[...] += part
+    r.psend[...] = acc[pl.ds(pl.multiple_of(ln * other, ln), ln), :].astype(BF)
 
     @on(is_att)
     def _():
@@ -721,21 +716,27 @@
         send(always, r.lgs.at[to], r.lgr.at[dp], (s, to), k_lg, r.lgs.at[0 : n_dp - 1], 1)
         send(always, r.ids_own, r.ids_all.at[dp], (s, to), k_id, r.ids_all.at[0 : n_dp - 1], 2)
     arrived(r.prow.at[0], k_p)
-    own_rows = r.acc[pl.ds(pl.multiple_of(ln * c, ln), ln), :]
-    r.acc[0:ln, :] = own_rows + r.prow[0].astype(F32)
-    r.psum[...] = r.acc[0:ln, :].astype(BF)
+    own_rows = acc[pl.ds(pl.multiple_of(ln * c, ln), ln), :]
+    acc[0:ln, :] = own_rows + r.prow[0].astype(F32)
+    r.psum[...] = acc[0:ln, :].astype(BF)
     send(at_x1, r.psum, r.prow.at[1], (across, dp), k_p + 1)
 
     def weights(cond):
         send(is_att | cond, r.par_a, r.par_a, (core, dp), k_pa)
         send(is_ff | cond, r.par_f, r.par_f, (core, dp), k_pf)
-        for j in range(tiles):
-            cut = slice(j * w, (j + 1) * w)
-            send(is_att | cond, w_in_h.at[0, :, cut], r.wa.at[:, cut], (core, dp), k_wa + j, tag=3)
-            send(is_ff | cond, w_in_h.at[0, :, cut], r.w1.at[:, cut], (core, dp), k_w1 + j, tag=4)
-            send(is_ff | cond, w_out_h.at[0, cut, :], r.w2.at[cut, :], (core, dp), k_w2 + j, tag=5)
+        cuts = [slice(j * w, (j + 1) * w) for j in range(tiles)]
+        first = [(is_att, w_in_h.at[0, :, cut], r.wa.at[:, cut], k_wa + j, 3) for j, cut in enumerate(cuts)]
+        left = [(is_ff, w_in_h.at[0, :, cut], r.w1.at[:, cut], k_w1 + j, 4) for j, cut in enumerate(cuts)]
+        right = [(is_ff, w_out_h.at[0, cut, :], r.w2.at[cut, :], k_w2 + j, 5) for j, cut in enumerate(cuts)]
+        if cond == at_x1:
+            order = first + right + left
+        else:
+            order = first + [one for pair in zip(left, right) for one in pair]
+        for whose, src, dst, recv, tag in order:
+            send(whose | cond, src, dst, (core, dp), recv, tag=tag)
 
     weights(at_x0)
+    weights(at_x1)
 
     for i, (at, size) in enumerate(p.chunks):
         part = mm(r.lgp[:, at : at + size], r.emb[at : at + size, :])
@@ -751,14 +752,13 @@
         r.gwide[0 : p.masks, :] = r.g[pl.ds(pl.multiple_of(mp * c, mp), p.masks), :] + r.grow[0]
 
     on(at_x1)(masked_gradient)
-    weights(at_x1)
 
     k_x = recvs.take()
 
     @on(at_x0)
     def _():
         arrived(r.prow.at[1], k_p + 1)
-        whole = r.acc[0:ln, :] + r.prow[1].astype(F32)
+        whole = acc[0:ln, :] + r.prow[1].astype(F32)
         r.x_a[...] = (whole + pos[...].astype(F32)).astype(BF)
 
     @on(is_att)
@@ -772,8 +772,46 @@
         pltpu.make_async_copy(w_out_h.at[0], r.w2, ls.at[l_w + 1]).wait()
         arrived(r.par_a, k_pa)
 
+    def turn_second():
+        def step(i, carry):
+            at = pl.ds(pl.multiple_of(i * 128, 128), 128)
+            r.w2t[:, at] = r.w2[at, :].T
+            return carry
+
+        lax.fori_loop(0, ff // 128, step, 0)
+
+    def turn_first():
+        def step(i, carry):
+            at = pl.ds(pl.multiple_of(i * 128, 128), 128)
+            r.w1t[at, :] = r.w1[:, at].T
+            return carry
+
+        lax.fori_loop(0, ff // 128, step, 0)
+
+    def turn_attention(j):
+        cut = slice(j * w, (j + 1) * w)
+        r.wa[:, cut] = r.wa[:, cut].T
+
+    def second_here():
+        @on(is_att)
+        def _():
+            for j in range(tiles):
+                cut = slice(j * w, (j + 1) * w)
+                arrived(r.w2.at[cut, :], k_w2 + j)
+
+    def first_here():
+        @on(is_att)
+        def _():
+            for j in range(tiles):
+                cut = slice(j * w, (j + 1) * w)
+                arrived(r.w1.at[:, cut], k_w1 + j)
+
     @on(at_x1)
     def _():
+        second_here()
+        turn_second()
+        first_here()
+        turn_first()
         arrived(r.x_a, k_x)
 
     low = jnp.where(iota((ln, 128), 1) < 64, 1.0, 0.0).astype(BF)
@@ -821,7 +859,7 @@
         r.ctx[:, at : at + 128] = mm(chance.astype(BF), value).astype(BF)
     wa_tile(3)
     resid = rows_x.astype(F32) + mm(r.ctx[...], r.wa[:, 3 * w : 4 * w]) + r.par_a[1:2, 0:w]
-    r.x_f[...], r.n_a[...], r.inv_a[...] = norm_forward(resid, r.par_a)
+    r.x_all[c, z, y], r.n_a[...], r.inv_a[...] = norm_forward(resid, r.par_a)
 
     class Gather:
         def __init__(self, buf):
@@ -911,20 +949,23 @@
     k_dex = recvs.take(2)
     xs, db = Gather(r.x_all), Gather(r.db_all)
 
-    r.x_all[c, z, y] = r.x_f[...]
     xs.start()
 
-    def feed(rows_x, keep=True):
+    def feed(rows_x, keep=True, turning=False):
         total = rows_x.astype(F32) + r.par_f[1:2, 0:w]
+
+        def hidden_tile(j):
+            cut = slice(j * w, (j + 1) * w)
+            return mm(rows_x, r.w1[:, cut]) + r.par_f[0:1, cut]
+
+        later = hidden_tile(0)
         for j in range(tiles):
             cut = slice(j * w, (j + 1) * w)
-
-            @on(is_att)
-            def _():
-                arrived(r.w1.at[:, cut], k_w1 + j)
-                arrived(r.w2.at[cut, :], k_w2 + j)
-
-            hidden = mm(rows_x, r.w1[:, cut]) + r.par_f[0:1, cut]
+            hidden = later
+            if j + 1 < tiles:
+                later = hidden_tile(j + 1)
+            if turning:
+                turn_attention(j)
             below = 0.5 + 0.5 * lax.erf(hidden * (0.5**0.5))
             total = total + mm((hidden * below).astype(BF), r.w2[cut, :])
             if keep:
@@ -934,10 +975,10 @@
         if keep:
             r.y_f[...], r.n_f[...], r.inv_f[...] = result, normed, inverse
         else:
-            r.y_o[...] = result
-
-    on(on_0)(lambda: feed(r.x_f[...]))
-    on(at_x1)(lambda: feed(r.x_f[...]))
+            r.psum[...] = result
+
+    on(on_0)(lambda: feed(r.x_all[c, z, y]))
+    on(at_x1)(lambda: feed(r.x_all[c, z, y], turning=True))
     send(at_x0 | is_ff, r.y_f, r.x_a, (across, dp), k_x)
 
     @on(at_x0 | is_ff)
@@ -945,7 +986,7 @@
         arrived(r.x_all.at[0, z, y], xs.own)
         feed(r.x_all[0, z, y], False)
 
-    send(at_x0 | is_ff, r.y_o, r.x_a, (3 - s, dp), k_x)
+    send(at_x0 | is_ff, r.psum, r.x_a, (3 - s, dp), k_x)
 
     @on(at_x1)
     def _():
@@ -989,14 +1030,21 @@
     k_ctx, k_xt, k_dba, k_sm = (recvs.take() for _ in range(4))
     to_x = lambda slot: r.b_x.at[:, :, lanes(slot)]
     to_ctx = lambda slot: r.b_ctx.at[:, :, lanes(slot)]
-    to_dbr = lambda slot: r.b_dbr.at[lanes(slot), :]
+    spare = [r.x_all.at[1, 0:2], r.x_all.at[1, 2:4], r.db_all.at[1, 0:2], r.db_all.at[1, 2:4]]
+
+    def in_spare(i):
+        def at(slot):
+            if isinstance(slot, slice):
+                return r.de_all.at[0, slot]
+            return spare[i].at[slot // 2, lax.rem(slot, 2)]
+
+        return at
+
+    to_dbr = in_spare(3)
     to_sm = lambda slot: r.b_sm.at[slot]
 
-    def to_dh(j):
-        return lambda slot: r.b_dh.at[lanes(slot), j * w : (j + 1) * w]
-
     def push_dh(j):
-        push(0, k_dh[j], lambda i: r.dpk.at[:, j * w : (j + 1) * w], to_dh(j))
+        push(0, k_dh[j], lambda i: r.dpk.at[:, j * w : (j + 1) * w], in_spare(j))
 
     def push_rows():
         push(0, k_xt, lambda i: r.xt_a.at[:, i], to_x)
@@ -1009,7 +1057,7 @@
                 dst[b // 2, b % 2] = turned[b * p.in_rows : (b + 1) * p.in_rows]
 
     def emit(i, src):
-        pltpu.make_async_copy(src, outs[i], os.at[i]).start()
+        pltpu.make_async_copy(src, outs[i].at[0] if i == 4 else outs[i], os.at[i]).start()
 
     def logits():
         arrived(r.ch_two, k_chc)
@@ -1026,18 +1074,23 @@
         send(at_x0, r.gwide.at[0 : p.masks], r.grow.at[1], (across, dp), k_g + 1)
         turn()
         push_rows()
-        on(is_att)(lambda: feed(r.x_f[...]))
-        for t in (1, 2):
-            xs.step(t)
-            xs.cross(t)
+        first_here()
+        second_here()
+        on(is_att)(lambda: feed(r.x_all[c, z, y]))
+        xs.step(1)
+        xs.cross(1)
+        turn_second()
+        turn_first()
+        for j in range(tiles):
+            turn_attention(j)
+        xs.step(2)
+        xs.cross(2)
         arrived(r.ch_own, k_cho)
         r.ch_all[c, dp] = r.ch_own[...]
         send(at_x0, r.ch_own, r.ch_two, (core, dp), k_chc)
         for k in range(1, nz):
             send(at_x0, r.ch_own, ch(dp), (s, lax.rem(dp + 2 * k, n_dp)), k_ch)
         logits()
-        xs.step(3)
-        xs.cross(3)
 
     stage[0] = 1
 
@@ -1071,16 +1124,17 @@
     r.db_all[c, z, y] = dres.astype(BF)
     db.start()
     branch = r.db_all[c, z, y]
+
     total = r.dres[...]
     for j in range(tiles):
         cut = slice(j * w, (j + 1) * w)
-        dhidden = (mm_nt(branch, r.w2[cut, :]) * r.slope[:, cut].astype(F32)).astype(BF)
+        dhidden = (mm(branch, r.w2t[:, cut]) * r.slope[:, cut].astype(F32)).astype(BF)
         r.bsum[:, cut] = jnp.sum(dhidden.astype(F32), 0, keepdims=True)
-        total = total + mm_nt(dhidden, r.w1[:, cut])
+        total = total + mm(dhidden, r.w1t[cut, :])
     r.dyf[...] = total.astype(BF).astype(F32)
     r.vecs[0:1], r.vecs[1:2] = gain_part, shift_part
 
-    @on(at_x1)
+    @on(on_1)
     def _():
         xs.step(1)
         xs.cross(1)
@@ -1089,7 +1143,7 @@
     r.dres[...] = dres
     r.dbr_a[...] = dres.astype(BF)
     branch = r.dbr_a[...]
-    r.dctx[...] = mm_nt(branch, r.wa[:, 3 * w : 4 * w]).astype(BF)
+    r.dctx[...] = mm(branch, r.wa[:, 3 * w : 4 * w]).astype(BF)
     for h in range(pairs):
         at = 128 * h
         query = r.pk[:, at : at + 128]
@@ -1109,7 +1163,7 @@
     total = r.dres[...]
     for j in range(3):
         cut = slice(j * w, (j + 1) * w)
-        total = total + mm_nt(r.dpk[:, cut], r.wa[:, cut])
+        total = total + mm(r.dpk[:, cut], r.wa[:, cut])
     r.dx[...] = total.astype(BF)
     send(at_x1, r.dx, r.dyin, (across, dp), k_dy)
 
@@ -1134,7 +1188,7 @@
 
     @on(is_att)
     def _():
-        o_wout[...] = jnp.zeros(o_wout.shape, BF)
+        o_wout[...] = jnp.zeros((p.out_rows, w), BF)
         emit(4, o_wout)
 
     @on(at_x1)
@@ -1153,9 +1207,12 @@
     small(r.sm_a, jnp.sum(branch.astype(F32), 0, keepdims=True), gain_part, shift_part)
     push(0, k_sm, lambda i: r.sm_a, to_sm)
     push_dh(1)
+    push_dh(2)
 
     @on(at_x1)
     def _():
+        xs.step(1, is_att)
+        xs.cross(1, is_att)
         arrived(r.ch_pair, k_chp)
         send(at_x1, r.ch_pair, r.ch_far, (across, dp), k_chq)
         xs.step(2)
@@ -1168,8 +1225,13 @@
         hand_on(r.dx_pair, ydp)
 
     on(at_x1)(lambda: xs.cross(2))
+
+    @on(at_x0)
+    def _():
+        xs.step(3)
+        xs.cross(3)
+
     db.cross(1)
-    push_dh(2)
 
     @on(at_x1)
     def _():
@@ -1192,14 +1254,15 @@
         arrived(r.ch_all.at[other], k_chx)
         arrived(r.lgr.at[0 : n_dp - 1], k_lg)
         arrived(r.ids_all.at[0 : n_dp - 1], k_id)
+        lines = 2 * p.masks
         for i in range(n_dp):
             for m in range(2):
-                r.ch_pack[i, p.masks * m : p.masks * (m + 1)] = r.ch_all[m, i, 0 : p.masks]
-        lines = 2 * n_dp * p.masks
-        grad = mm_tn(r.lgr[...].reshape(lines, p.share_pad), r.ch_pack[...].reshape(lines, w))
+                at = lines * i + p.masks * m
+                r.w1t[at : at + p.masks, :] = r.ch_all[m, i, 0 : p.masks]
+        grad = mm_tn(r.lgr[...].reshape(n_dp * lines, p.share_pad), r.w1t[0 : n_dp * lines, :])
         o_tab[...] = grad[0 : p.share]
 
-    k_in = [recvs.take(3) for _ in range(tiles)]
+    k_in = [recvs.take(4) for _ in range(tiles)]
     half = nz * p.in_rows
     mate = z + 1 - 2 * lax.rem(z, 2)
     far_base = 2 - 2 * (z // 2)
@@ -1218,18 +1281,24 @@
             if j == 3:
                 gathered(k_ctx, to_ctx)
                 gathered(k_dba, to_dbr)
-                grad = mm(r.b_ctx[...].reshape(half, 4 * ln), r.b_dbr[...])
+                grad = mm(r.b_ctx[...].reshape(half, 4 * ln), spare[3][...].reshape(4 * ln, w))
             else:
                 if j == 0:
                     gathered(k_xt, to_x)
-                gathered(k_dh[j], to_dh(j))
-                grad = mm(r.b_x[...].reshape(half, 4 * ln), r.b_dh[:, cut])
+                gathered(k_dh[j], in_spare(j))
+                grad = mm(r.b_x[...].reshape(half, 4 * ln), spare[j][...].reshape(4 * ln, w))
             r.wa[0:half, cut] = grad.astype(BF)
 
         to_mate = (s, 2 * mate + y)
         for k in range(2):
             send(outer_att, shard(far_base + k, cut), r.r_in.at[2 + k, :, cut], to_mate, k_in[j] + 2)
-        send(is_att, shard(mate, cut), r.r_in.at[0, :, cut], to_mate, k_in[j])
+        send(outer_att, shard(mate, cut), r.r_in.at[0, :, cut], to_mate, k_in[j])
+
+    to_inner = (s, 2 * (nz - 1 - z) + y)
+
+    def add(zz, part, cut):
+        rows = pl.ds(pl.multiple_of(zz * p.in_rows, p.in_rows), p.in_rows)
+        r.wa[rows, cut] = (r.wa[rows, cut].astype(F32) + part.astype(F32)).astype(BF)
 
     def attention_sum(j):
         cut = tile_cut(j)
@@ -1237,10 +1306,19 @@
         @on(inner)
         def _():
             arrived(r.r_in.at[2:4, :, cut], k_in[j] + 2)
-            for k in range(2):
-                rows = pl.ds(pl.multiple_of((far_base + k) * p.in_rows, p.in_rows), p.in_rows)
-                r.wa[rows, cut] = (r.wa[rows, cut].astype(F32) + r.r_in[2 + k, :, cut].astype(F32)).astype(BF)
-                send(inner, shard(far_base + k, cut), r.r_in.at[1, :, cut], (s, 2 * (far_base + k) + y), k_in[j] + 1)
+            for zz in (nz - 1 - z, nz - 1 - mate):
+                add(zz, r.r_in[jnp.where(zz == far_base, 2, 3), :, cut], cut)
+            send(inner, shard(nz - 1 - z, cut), r.r_in.at[1, :, cut], to_inner, k_in[j] + 1)
+            send(inner, shard(nz - 1 - mate, cut), r.r_in.at[4, :, cut], to_inner, k_in[j] + 3)
+
+    def attention_last(j):
+        cut = tile_cut(j)
+
+        @on(inner)
+        def _():
+            arrived(r.r_in.at[4, :, cut], k_in[j] + 3)
+            add(mate, r.r_in[4, :, cut], cut)
+            send(inner, shard(mate, cut), r.r_in.at[1, :, cut], (s, 2 * mate + y), k_in[j] + 1)
 
     def unit_grads(yy, i):
         def four(buf):
@@ -1250,7 +1328,7 @@
         hidden = mm(rows_x, r.w1[:, mine_in]) + r.par_f[0:1, mine_in]
         below = 0.5 + 0.5 * lax.erf(hidden * (0.5**0.5))
         slope = below + hidden * (0.3989422804014327 * jnp.exp(-0.5 * hidden * hidden))
-        dhidden = (mm_nt(up, r.w2[mine_in, :]) * slope).astype(BF)
+        dhidden = (mm(up, r.w2t[:, mine_in]) * slope).astype(BF)
         r.u_out[...] += mm_tn((hidden * below).astype(BF), up)
         r.w_col[...] += mm_tn(rows_x, dhidden)
 
@@ -1311,6 +1389,7 @@
 
     attention_tile(1)
     attention_sum(0)
+    attention_last(3)
 
     def row_0(i):
         @on(on_1)
@@ -1323,8 +1402,10 @@
     row_0(ydp)
     pair_step(de, k_row, 1, on_1, k_pass)
     attention_sum(1)
+    attention_last(0)
 
     attention_tile(2)
+    attention_last(1)
     pair_step(de, k_row, 2, on_1, k_pass)
 
     gathered(k_sm, to_sm)
@@ -1335,6 +1416,7 @@
         send(always, r.sm_tot, r.r_sm.at[z], (s, 2 * zz + y), k_smz)
 
     attention_sum(2)
+    attention_last(2)
 
     @on(is_ff)
     def _():
@@ -1350,24 +1432,28 @@
 
         send(cond, r.de_all.at[x], r.de_all.at[x], (core, dp), k_dex + x)
 
+    def column_block(k):
+        at = k * p.out_rows
+        return r.slope.at[0 : p.in_rows, pl.ds(at if isinstance(k, int) else pl.multiple_of(at, p.out_rows), p.out_rows)]
+
     @on(is_ff)
     def _():
         units_over_y(mate_half)
-        o_wout[0] = r.u_out[...].astype(BF)
+        o_wout[...] = r.u_out[...].astype(BF)
         emit(4, o_wout)
         for k in range(n_dp):
-            r.w_send[k] = r.w_col[k * p.in_rows : (k + 1) * p.in_rows, :].astype(BF)
-        r.r_col[dp] = r.w_send[dp]
+            column_block(k)[...] = r.w_col[k * p.in_rows : (k + 1) * p.in_rows, :].astype(BF)
+        r.r_col[dp] = column_block(dp)[...]
 
     for k in (4, 5, 3, 2, 6, 1, 7) if n_dp == 8 else range(1, n_dp):
         to = lax.rem(dp + k, n_dp)
-        send(is_ff, r.w_send.at[to], r.r_col.at[dp], (s, to), k_col)
-    passed_row(is_ff)
-
+        send(is_ff, column_block(to), r.r_col.at[dp], (s, to), k_col)
     @on(at_x1)
     def _():
         arrived(r.ch_all.at[c], k_cha)
         send(at_x1, r.ch_all.at[c], r.ch_all.at[c], (core, dp), k_chx)
+
+    passed_row(is_ff)
 
 
     head_part()
@@ -1391,10 +1477,14 @@
         mine = pl.ds(pl.multiple_of(z * p.in_rows, p.in_rows), p.in_rows)
         for j in (3, 0, 1, 2):
             cut = tile_cut(j)
-            arrived(r.r_in.at[0, :, cut], k_in[j])
+
+            @on(inner)
+            def _():
+                arrived(r.r_in.at[0, :, cut], k_in[j])
+                add(z, r.r_in[0, :, cut], cut)
+
             arrived(r.r_in.at[1, :, cut], k_in[j] + 1)
-            near_sum = r.wa[mine, cut].astype(F32) + r.r_in[0, :, cut].astype(F32)
-            o_win[0, :, cut] = (near_sum + r.r_in[1, :, cut].astype(F32)).astype(BF)
+            o_win[0, :, cut] = (r.wa[mine, cut].astype(F32) + r.r_in[1, :, cut].astype(F32)).astype(BF)
             pltpu.make_async_copy(o_win.at[:, :, cut], outs[3].at[:, :, cut], os.at[3]).start()
 
     @on(is_ff)
@@ -1408,7 +1498,7 @@
     r.sm_all[...] = r.r_sm[0] + r.r_sm[1] + r.r_sm[2] + r.r_sm[3]
     emit(5, o_vec)
     for i, src in enumerate((o_log, o_tab, o_pos, o_win, o_wout, o_vec)):
-        pltpu.make_async_copy(src, outs[i], os.at[i]).wait()
+        pltpu.make_async_copy(src, outs[i].at[0] if i == 4 else outs[i], os.at[i]).wait()
 
     drain(1)
     assert sends.n <= SENDS and recvs.n <= RECVS, (sends.n, recvs.n)

time: 104 us -> 103 us (level); the launches traced: 102 us -> 102 us
  no operation moved by 1% of the time
where the time goes in v6:
time: 103 us; the launch traced here: 102 us
  Pallas kernels  102 us (99%)
    pallas_call x1, Pallas kernels, whole(): pl.pallas_call(functools.partial(fused, p, list(scratch)), out_shape=part...  98 us
    pallas_call x1, Pallas kernels, whole(): pl.pallas_call(functools.partial(finish, p), out_shape=[jax.ShapeDtypeStr...  3.55 us

profile of v6, /device:TPU:1, one launch (start us, length us, event | category | flops | bytes accessed | tf_op | source)
XLA Modules:
  0.0 102.4 jit_solution(2029101124913253367)
XLA Ops:
  0.6 98.0 %shard_map.187 = (bf16[2,1,40,3648]{3,2,1,0:T(8,128)(2,1)}, f32[456,768]{1,0:T(8,128)}, f32[16,768]{1,0:T(8,128)}, bf16[1,96,3072]{2,1,0:T(8,128)(2,1)}, bf16[1,384,768]{2,1,0:T(8,128)(2,1)}, /*index=5*/f32[8,768]{1,0:T(8,128)}) custom-call(s32[2,1,128]{2,1,0:T(1,128)} %refs_0_.1, s32[2,1,128]{2,1,0:T(1,128)} %refs_1_.1, s32[2,1,40]{2,1,0:T(1,128)} %refs_2_.1, ...), custom_call_target="tpu_custom_call" | custom-call | tf_op jit(solution)/shard_map/pallas_call | solution.py:1585
  98.7 3.5 %shard_map.188 = (f32[2,1,40,3648]{3,2,1,0:T(8,128)}, f32[456,768]{1,0:T(8,128)}, f32[16,768]{1,0:T(8,128)}, f32[1,96,3072]{2,1,0:T(8,128)}, f32[1,384,768]{2,1,...) custom-call(bf16[2,1,40,3648]{3,2,1,0:T(8,128)(2,1)} %get-tuple-element.15.refs_0_, ...), custom_call_target="tpu_custom_call" | custom-call | tf_op jit(solution)/shard_map/pallas_call | solution.py:1626

commit v7 on v6

--- a/solution.py
+++ b/solution.py
@@ -385,8 +385,8 @@
     )
 
 
-SENDS = 95
-RECVS = 88
+SENDS = 86
+RECVS = 83
 VMEM_LIMIT = 64 * 2**20
 BF = jnp.bfloat16
 F32 = jnp.float32
@@ -495,7 +495,6 @@
         dpk=((ln, 3 * w), BF),
         dctx=((ln, w), BF),
         dx=((ln, w), BF),
-        dx_pair=((ln, w), BF),
         bsum=((1, ff), F32),
         vecs=((8, w), F32),
         sm_a=((8, w), F32),
@@ -507,9 +506,11 @@
         sm_all=((8, w), F32),
         r_sm=((p.nz, 8, w), F32),
         r_in=((5, p.in_rows, ff), BF),
-        x_all=((2, p.nz, 2, ln, w), BF),
-        db_all=((2, p.nz, 2, ln, w), BF),
-        w_col=((w, p.out_rows), F32),
+        x_all=((2, p.nz, ln, w), BF),
+        db_all=((2, p.nz, ln, w), BF),
+        spare_a=((4, ln, w), BF),
+        spare_b=((4, ln, w), BF),
+        w_col=((w, 2 * p.out_rows), F32),
         r_col=((p.n_dp, p.in_rows, p.out_rows), BF),
         ch_own=((mp, w), BF),
         ch_two=((mp, w), BF),
@@ -517,7 +518,7 @@
         ch_far=((mp, w), BF),
         ch_all=((2, p.n_dp, mp, w), BF),
         de_all=((2, p.n_dp, ln, w), BF),
-        u_out=((p.out_rows, w), F32),
+        u_out=((2 * p.out_rows, w), F32),
         o_tab=((p.share, w), F32),
         o_pos=((ln // p.n_dp, w), F32),
     )
@@ -694,7 +695,26 @@
     pl.semaphore_wait(barrier, len(peers))
     send(always, r.psend, r.prow.at[0], (core, dp), k_p)
 
-
+    arrived(r.prow.at[0], k_p)
+    acc[0:ln, :] = acc[pl.ds(pl.multiple_of(ln * c, ln), ln), :] + r.prow[0].astype(F32)
+    r.psum[...] = acc[0:ln, :].astype(BF)
+    send(at_x1, r.psum, r.prow.at[1], (across, dp), k_p + 1)
+
+    def weights(cond, part):
+        if part == 0:
+            send(is_att | cond, r.par_a, r.par_a, (core, dp), k_pa)
+            send(is_ff | cond, r.par_f, r.par_f, (core, dp), k_pf)
+        cuts = [slice(j * w, (j + 1) * w) for j in range(tiles)]
+        for_core_1 = [(is_att, w_in_h.at[0, :, cut], r.wa.at[:, cut], k_wa + j, 3) for j, cut in enumerate(cuts)]
+        left = [(is_ff, w_in_h.at[0, :, cut], r.w1.at[:, cut], k_w1 + j, 4) for j, cut in enumerate(cuts)]
+        right = [(is_ff, w_out_h.at[0, cut, :], r.w2.at[cut, :], k_w2 + j, 5) for j, cut in enumerate(cuts)]
+        for_core_0 = right + left if cond == at_x1 else [one for pair in zip(left, right) for one in pair]
+        for order in (for_core_1, for_core_0):
+            for whose, src, dst, recv, tag in order[:2] if part == 0 else order[2:]:
+                send(whose | cond, src, dst, (core, dp), recv, tag=tag)
+
+    weights(at_x0, 0)
+    weights(at_x1, 0)
     pltpu.make_async_copy(lg_h, lg, ls.at[l_w + 2]).wait()
     pltpu.make_async_copy(pos_h, pos, ls.at[l_w + 3]).wait()
     r.lgp[...] = jnp.zeros(r.lgp.shape, BF)
@@ -715,28 +735,6 @@
         to = lax.rem(dp + k, n_dp)
         send(always, r.lgs.at[to], r.lgr.at[dp], (s, to), k_lg, r.lgs.at[0 : n_dp - 1], 1)
         send(always, r.ids_own, r.ids_all.at[dp], (s, to), k_id, r.ids_all.at[0 : n_dp - 1], 2)
-    arrived(r.prow.at[0], k_p)
-    own_rows = acc[pl.ds(pl.multiple_of(ln * c, ln), ln), :]
-    acc[0:ln, :] = own_rows + r.prow[0].astype(F32)
-    r.psum[...] = acc[0:ln, :].astype(BF)
-    send(at_x1, r.psum, r.prow.at[1], (across, dp), k_p + 1)
-
-    def weights(cond):
-        send(is_att | cond, r.par_a, r.par_a, (core, dp), k_pa)
-        send(is_ff | cond, r.par_f, r.par_f, (core, dp), k_pf)
-        cuts = [slice(j * w, (j + 1) * w) for j in range(tiles)]
-        first = [(is_att, w_in_h.at[0, :, cut], r.wa.at[:, cut], k_wa + j, 3) for j, cut in enumerate(cuts)]
-        left = [(is_ff, w_in_h.at[0, :, cut], r.w1.at[:, cut], k_w1 + j, 4) for j, cut in enumerate(cuts)]
-        right = [(is_ff, w_out_h.at[0, cut, :], r.w2.at[cut, :], k_w2 + j, 5) for j, cut in enumerate(cuts)]
-        if cond == at_x1:
-            order = first + right + left
-        else:
-            order = first + [one for pair in zip(left, right) for one in pair]
-        for whose, src, dst, recv, tag in order:
-            send(whose | cond, src, dst, (core, dp), recv, tag=tag)
-
-    weights(at_x0)
-    weights(at_x1)
 
     for i, (at, size) in enumerate(p.chunks):
         part = mm(r.lgp[:, at : at + size], r.emb[at : at + size, :])
@@ -745,13 +743,16 @@
         else:
             r.g[...] += part
     send(always, r.g.at[pl.ds(pl.multiple_of(mp * other, mp), p.masks)], r.grow.at[0], (core, dp), k_g)
+    weights(at_x0, 1)
+    weights(at_x1, 1)
 
     def masked_gradient():
         arrived(r.grow.at[0], k_g)
         r.gwide[...] = jnp.zeros(r.gwide.shape, F32)
         r.gwide[0 : p.masks, :] = r.g[pl.ds(pl.multiple_of(mp * c, mp), p.masks), :] + r.grow[0]
 
-    on(at_x1)(masked_gradient)
+    masked_gradient()
+    send(at_x0, r.gwide.at[0 : p.masks], r.grow.at[1], (across, dp), k_g + 1)
 
     k_x = recvs.take()
 
@@ -771,6 +772,9 @@
         pltpu.make_async_copy(w_in_h.at[0], r.w1, ls.at[l_w]).wait()
         pltpu.make_async_copy(w_out_h.at[0], r.w2, ls.at[l_w + 1]).wait()
         arrived(r.par_a, k_pa)
+
+    def masked_places():
+        return jnp.where(iota((ln, ln), 0) == r.mrow[0:1, :], 1.0, 0.0).astype(BF)
 
     def turn_second():
         def step(i, carry):
@@ -812,6 +816,14 @@
         turn_second()
         first_here()
         turn_first()
+        r.mrow[...] = jnp.full(r.mrow.shape, -1, jnp.int32)
+        r.mrow[0:1, 0 : p.masks] = picks[c]
+        arrived(r.grow.at[1], k_g + 1)
+        r.gwide[0 : p.masks, :] += r.grow[1]
+        coarse = r.gwide[...].astype(BF)
+        fine = (r.gwide[...] - coarse.astype(F32)).astype(BF)
+        places = masked_places()
+        r.dyf[...] = mm(places, coarse) + mm(places, fine)
         arrived(r.x_a, k_x)
 
     low = jnp.where(iota((ln, 128), 1) < 64, 1.0, 0.0).astype(BF)
@@ -859,61 +871,30 @@
         r.ctx[:, at : at + 128] = mm(chance.astype(BF), value).astype(BF)
     wa_tile(3)
     resid = rows_x.astype(F32) + mm(r.ctx[...], r.wa[:, 3 * w : 4 * w]) + r.par_a[1:2, 0:w]
-    r.x_all[c, z, y], r.n_a[...], r.inv_a[...] = norm_forward(resid, r.par_a)
+    r.x_all[c, z], r.n_a[...], r.inv_a[...] = norm_forward(resid, r.par_a)
 
     class Gather:
         def __init__(self, buf):
             self.buf = buf
-            self.near, self.far, self.own, self.core0 = recvs.take(nz), recvs.take(2), recvs.take(), recvs.take(4)
-
-        def at(self, zz, yy):
-            return self.buf.at[c, zz, yy]
-
-        def pair(self, m, half_z, yy):
-            return self.buf.at[m, pl.ds(2 * half_z, 2), yy]
+            self.near, self.core0 = recvs.take(nz), recvs.take(nz)
+
+        def at(self, zz):
+            return self.buf.at[c, zz]
 
         def start(self):
-            own = self.at(z, y)
+            own = self.at(z)
             send(not_last, own, own, (s, dp + 2), self.near + z)
             send(not_first, own, own, (s, dp - 2), self.near + z)
-            send(is_att, own, own, (core, dp), self.own)
-            self.to_y(z, always)
-
-        def to_y(self, zz, cond):
-            recv = jnp.where(c == 0, self.core0 + 2, self.far) + zz // 2
-            send(cond, self.at(zz, y), self.at(zz, y), (jnp.where(c == 0, core, s), ydp), recv)
+            send(is_att, own, own, (core, dp), self.core0 + z)
 
         def step(self, t, cond=always):
             for sign in (-1, 1):
                 here, zz = at_distance(t, sign, cond)
-                piece = self.at(zz, y)
+                piece = self.at(zz)
                 on(here)(lambda piece=piece, zz=zz: arrived(piece, self.near + zz))
                 if t < nz - 1:
                     send(onward(here, sign), piece, piece, (s, dp - 2 * sign), self.near + zz)
-                send(here | is_att, piece, piece, (core, dp), self.core0 + zz // 2)
-
-        def cross(self, t, cond=always):
-            for sign in (-1, 1):
-                here, zz = at_distance(t, sign, cond)
-                self.to_y(zz, here)
-
-        def from_core0(self, half_z, own_side):
-            if own_side:
-                mine = (z // 2) == half_z
-
-                @pl.when(mine)
-                def _():
-                    arrived(self.buf.at[0, z + 1 - 2 * lax.rem(z, 2), y], self.core0 + half_z)
-
-                @pl.when(jnp.logical_not(mine))
-                def _():
-                    arrived(self.pair(0, half_z, y), self.core0 + half_z)
-
-            else:
-                arrived(self.pair(0, half_z, 1 - y), self.core0 + 2 + half_z)
-
-        def from_y(self, half_z):
-            arrived(self.pair(1, half_z, 1 - y), self.far + half_z)
+                send(here | is_att, piece, piece, (core, dp), self.core0 + zz)
 
     def at_distance(t, sign, cond):
         here = cond | (at_least(t) if sign < 0 else at_most(nz - 1 - t))
@@ -921,22 +902,6 @@
 
     def onward(here, sign):
         return here | (not_last if sign < 0 else not_first)
-
-    def pair_line(buf, base, cond, i):
-        piece = buf(i)
-        send(cond | not_last, piece, piece, (s, dp + 2), base + i)
-        send(cond | not_first, piece, piece, (s, dp - 2), base + i)
-
-    def pair_step(buf, base, t, cond, on_x):
-        for sign in (-1, 1):
-            for side in (0, 1):
-                here, zz = at_distance(t, sign, cond)
-                from_dp = 2 * zz + (1 - y if side else y)
-                piece = buf(from_dp)
-                on(here)(lambda piece=piece, from_dp=from_dp: arrived(piece, base + from_dp))
-                if t < nz - 1:
-                    send(onward(here, sign), piece, piece, (s, dp - 2 * sign), base + from_dp)
-                send(here, piece, piece, (across, dp), on_x)
 
     def ch(i):
         return r.ch_all.at[c, i]
@@ -977,28 +942,20 @@
         else:
             r.psum[...] = result
 
-    on(on_0)(lambda: feed(r.x_all[c, z, y]))
-    on(at_x1)(lambda: feed(r.x_all[c, z, y], turning=True))
+    on(on_0)(lambda: feed(r.x_all[c, z]))
+    on(at_x1)(lambda: feed(r.x_all[c, z], turning=True))
     send(at_x0 | is_ff, r.y_f, r.x_a, (across, dp), k_x)
 
     @on(at_x0 | is_ff)
     def _():
-        arrived(r.x_all.at[0, z, y], xs.own)
-        feed(r.x_all[0, z, y], False)
+        arrived(r.x_all.at[0, z], xs.core0 + z)
+        feed(r.x_all[0, z], False)
 
     send(at_x0 | is_ff, r.psum, r.x_a, (3 - s, dp), k_x)
 
     @on(at_x1)
     def _():
-        r.mrow[...] = jnp.full(r.mrow.shape, -1, jnp.int32)
-        r.mrow[0:1, 0 : p.masks] = picks[c]
-        places = jnp.where(iota((ln, ln), 0) == r.mrow[0:1, :], 1.0, 0.0).astype(BF)
-        r.ch_own[...] = mm_tn(places, r.y_f[...])[0:mp].astype(BF)
-        arrived(r.grow.at[1], k_g + 1)
-        r.gwide[0 : p.masks, :] += r.grow[1]
-        coarse = r.gwide[...].astype(BF)
-        fine = (r.gwide[...] - coarse.astype(F32)).astype(BF)
-        r.dyf[...] = mm(places, coarse) + mm(places, fine)
+        r.ch_own[...] = mm_tn(masked_places(), r.y_f[...])[0:mp].astype(BF)
 
     send(at_x1, r.ch_own, r.ch_own, (across, dp), k_cho)
     send(at_x1, r.ch_own, r.ch_two, (core, dp), k_chc)
@@ -1030,13 +987,13 @@
     k_ctx, k_xt, k_dba, k_sm = (recvs.take() for _ in range(4))
     to_x = lambda slot: r.b_x.at[:, :, lanes(slot)]
     to_ctx = lambda slot: r.b_ctx.at[:, :, lanes(slot)]
-    spare = [r.x_all.at[1, 0:2], r.x_all.at[1, 2:4], r.db_all.at[1, 0:2], r.db_all.at[1, 2:4]]
+    spare = [r.x_all.at[1], r.db_all.at[1], r.spare_a, r.spare_b]
 
     def in_spare(i):
         def at(slot):
             if isinstance(slot, slice):
                 return r.de_all.at[0, slot]
-            return spare[i].at[slot // 2, lax.rem(slot, 2)]
+            return spare[i].at[slot]
 
         return at
 
@@ -1070,24 +1027,20 @@
 
     @on(at_x0)
     def _():
-        masked_gradient()
-        send(at_x0, r.gwide.at[0 : p.masks], r.grow.at[1], (across, dp), k_g + 1)
         turn()
         push_rows()
         first_here()
         second_here()
-        on(is_att)(lambda: feed(r.x_all[c, z, y]))
-        xs.step(1)
-        xs.cross(1)
+        on(is_att)(lambda: feed(r.x_all[c, z]))
         turn_second()
         turn_first()
+        xs.step(1)
         for j in range(tiles):
             turn_attention(j)
-        xs.step(2)
-        xs.cross(2)
         arrived(r.ch_own, k_cho)
         r.ch_all[c, dp] = r.ch_own[...]
         send(at_x0, r.ch_own, r.ch_two, (core, dp), k_chc)
+        xs.step(2)
         for k in range(1, nz):
             send(at_x0, r.ch_own, ch(dp), (s, lax.rem(dp + 2 * k, n_dp)), k_ch)
         logits()
@@ -1121,9 +1074,9 @@
 
     dres, gain_part, shift_part = norm_backward(r.par_f, r.n_f, r.inv_f)
     r.dres[...] = dres
-    r.db_all[c, z, y] = dres.astype(BF)
+    r.db_all[c, z] = dres.astype(BF)
     db.start()
-    branch = r.db_all[c, z, y]
+    branch = r.db_all[c, z]
 
     total = r.dres[...]
     for j in range(tiles):
@@ -1137,7 +1090,6 @@
     @on(on_1)
     def _():
         xs.step(1)
-        xs.cross(1)
 
     dres, gain_part, shift_part = norm_backward(r.par_a, r.n_a, r.inv_a)
     r.dres[...] = dres
@@ -1172,19 +1124,38 @@
 
     away = jnp.where(c == 1, across, 3 - s)
 
-    def hand_on(src, i):
-        send(at_x0, src, row(c, i), (away, dp), jnp.where(c == 1, k_pass, k_row + i))
-        send(at_x0 | is_att, src, row(0, i), (core, dp), k_pass)
-
-        @on(on_0)
+    def row_line(cond, i):
+        piece = de(i)
+        send(cond | not_last, piece, piece, (s, dp + 2), k_row + i)
+        send(cond | not_first, piece, piece, (s, dp - 2), k_row + i)
+        send(cond, piece, piece, (s, ydp), k_row + i)
+
+    def row_step(t, cond):
+        for sign in (-1, 1):
+            here, zz = at_distance(t, sign, cond)
+            i = 2 * zz + y
+            on(here)(lambda i=i: arrived(de(i), k_row + i))
+            if t < nz - 1:
+                send(onward(here, sign), de(i), de(i), (s, dp - 2 * sign), k_row + i)
+            send(here, de(i), de(i), (s, ydp), k_row + i)
+            send(here, de(i), de(i), (across, dp), k_pass)
+
+    def row_cross(t, cond):
+        for sign in (-1, 1) if t else (1,):
+            here, zz = at_distance(t, sign, cond)
+            i = 2 * zz + 1 - y
+            on(here)(lambda i=i: arrived(de(i), k_row + i))
+            send(here, de(i), de(i), (across, dp), k_pass)
+
+    @on(at_x0)
+    def _():
+        send(at_x0, r.dx, row(c, dp), (away, dp), jnp.where(c == 1, k_pass, k_row + dp))
+        send(is_att, r.dx, row(0, dp), (core, dp), k_pass)
+
+        @on(is_ff)
         def _():
-            r.de_all[1, i] = src[...]
-            pair_line(de, k_row, on_0, i)
-
-    @on(at_x0)
-    def _():
-        send(at_x0, r.dx, r.dx_pair, (s, ydp), k_dp)
-        hand_on(r.dx, dp)
+            r.de_all[1, dp] = r.dx[...]
+            row_line(on_0, dp)
 
     @on(is_att)
     def _():
@@ -1198,7 +1169,7 @@
 
     push(0, k_dba, lambda i: r.dbr_a, to_dbr)
     push_dh(0)
-    small(r.sm_f, jnp.sum(r.db_all[c, z, y].astype(F32), 0, keepdims=True), r.vecs[0:1], r.vecs[1:2])
+    small(r.sm_f, jnp.sum(r.db_all[c, z].astype(F32), 0, keepdims=True), r.vecs[0:1], r.vecs[1:2])
     push(1, k_sm, lambda i: r.sm_f, to_sm)
     r.bsum[...] = jnp.zeros(r.bsum.shape, F32)
     for j in (0, 2):
@@ -1212,7 +1183,6 @@
     @on(at_x1)
     def _():
         xs.step(1, is_att)
-        xs.cross(1, is_att)
         arrived(r.ch_pair, k_chp)
         send(at_x1, r.ch_pair, r.ch_far, (across, dp), k_chq)
         xs.step(2)
@@ -1221,25 +1191,14 @@
 
     @on(at_x0)
     def _():
-        arrived(r.dx_pair, k_dp)
-        hand_on(r.dx_pair, ydp)
-
-    on(at_x1)(lambda: xs.cross(2))
-
-    @on(at_x0)
-    def _():
         xs.step(3)
-        xs.cross(3)
-
-    db.cross(1)
+
 
     @on(at_x1)
     def _():
         xs.step(3)
-        xs.cross(3)
 
     db.step(2)
-    db.cross(2)
 
     @on(at_x0)
     def _():
@@ -1253,14 +1212,13 @@
     def head_part():
         arrived(r.ch_all.at[other], k_chx)
         arrived(r.lgr.at[0 : n_dp - 1], k_lg)
-        arrived(r.ids_all.at[0 : n_dp - 1], k_id)
         lines = 2 * p.masks
         for i in range(n_dp):
             for m in range(2):
                 at = lines * i + p.masks * m
                 r.w1t[at : at + p.masks, :] = r.ch_all[m, i, 0 : p.masks]
         grad = mm_tn(r.lgr[...].reshape(n_dp * lines, p.share_pad), r.w1t[0 : n_dp * lines, :])
-        o_tab[...] = grad[0 : p.share]
+        o_tab[...] += grad[0 : p.share]
 
     k_in = [recvs.take(4) for _ in range(tiles)]
     half = nz * p.in_rows
@@ -1320,28 +1278,61 @@
             add(mate, r.r_in[4, :, cut], cut)
             send(inner, shard(mate, cut), r.r_in.at[1, :, cut], (s, 2 * mate + y), k_in[j] + 1)
 
-    def unit_grads(yy, i):
-        def four(buf):
-            return jnp.concatenate([buf[m, 2 * i + k, yy] for m in range(2) for k in range(2)], 0)
-
-        rows_x, up = four(r.x_all), four(r.db_all)
-        hidden = mm(rows_x, r.w1[:, mine_in]) + r.par_f[0:1, mine_in]
-        below = 0.5 + 0.5 * lax.erf(hidden * (0.5**0.5))
-        slope = below + hidden * (0.3989422804014327 * jnp.exp(-0.5 * hidden * hidden))
-        dhidden = (mm(up, r.w2t[:, mine_in]) * slope).astype(BF)
-        r.u_out[...] += mm_tn((hidden * below).astype(BF), up)
-        r.w_col[...] += mm_tn(rows_x, dhidden)
-
-    def units_here(t):
-        for one in (xs, db):
-            one.from_core0(t, True)
-        unit_grads(y, t)
-
-    def units_over_y(t):
-        for one in (xs, db):
-            one.from_core0(t, False)
-            one.from_y(t)
-        unit_grads(1 - y, t)
+    units_wide = pl.ds(pl.multiple_of(2 * z * p.out_rows, 2 * p.out_rows), 2 * p.out_rows)
+    units_mine = pl.ds(pl.multiple_of(y * p.out_rows, p.out_rows), p.out_rows)
+    units_other = pl.ds(pl.multiple_of((1 - y) * p.out_rows, p.out_rows), p.out_rows)
+
+    def units(k):
+        @on(is_ff)
+        def _():
+            near, far = jnp.where(z < nz // 2, z + k, z - k), jnp.where(z < nz // 2, k, nz - 1 - k)
+            edge = (z == 0) | (z == nz - 1)
+            zz = jnp.where(edge, near, far) if k > 1 else jnp.where(edge | (k == 0), near, jnp.where(z < nz // 2, z - 1, z + 1))
+            if k == 0:
+                on(at_x1)(lambda: arrived(r.x_all.at[0, zz], xs.core0 + zz))
+            else:
+                arrived(r.x_all.at[0, zz], xs.core0 + zz)
+            arrived(r.db_all.at[0, zz], db.core0 + zz)
+            rows_x = jnp.concatenate([r.x_all[m, zz] for m in range(2)], 0)
+            up = jnp.concatenate([r.db_all[m, zz] for m in range(2)], 0)
+            hidden = mm(rows_x, r.w1[:, units_wide]) + r.par_f[0:1, units_wide]
+            below = 0.5 + 0.5 * lax.erf(hidden * (0.5**0.5))
+            slope = below + hidden * (0.3989422804014327 * jnp.exp(-0.5 * hidden * hidden))
+            dhidden = (mm(up, r.w2t[:, units_wide]) * slope).astype(BF)
+            out_part, col_part = mm_tn((hidden * below).astype(BF), up), mm_tn(rows_x, dhidden)
+            if k == 0:
+                r.u_out[...], r.w_col[...] = out_part, col_part
+            else:
+                r.u_out[...] += out_part
+                r.w_col[...] += col_part
+
+    def out_piece(i):
+        return r.r_in.at[i, :, 0:w]
+
+    def col_piece(i):
+        return r.r_in.at[i % 4, :, w + p.out_rows * (i // 4) : w + p.out_rows * (i // 4 + 1)]
+
+    def stage_out(i):
+        return r.w1t.at[1408 + i * p.in_rows : 1408 + (i + 1) * p.in_rows, :]
+
+    def stage_col(i):
+        return r.w1t.at[1792 + i * p.in_rows : 1792 + (i + 1) * p.in_rows, 0 : p.out_rows]
+
+    def exchange_out(cond):
+        @on(is_ff | cond)
+        def _():
+            theirs = r.u_out[units_other, :].astype(BF)
+            for i in range(p.out_rows // p.in_rows):
+                stage_out(i)[...] = theirs[i * p.in_rows : (i + 1) * p.in_rows]
+                send(is_ff, stage_out(i), out_piece(i), (s, ydp), k_pair, tag=6)
+
+    def exchange_col(cond):
+        @on(is_ff | cond)
+        def _():
+            theirs = r.w_col[:, units_other].astype(BF)
+            for i in range(n_dp):
+                stage_col(i)[...] = theirs[i * p.in_rows : (i + 1) * p.in_rows]
+                send(is_ff, stage_col(i), col_piece(i), (s, ydp), k_pair, tag=6)
 
     entry = iota((p.share_rows, ln), 0) + (s * p.quarter + dp * p.share)
 
@@ -1357,56 +1348,56 @@
         lax.fori_loop(0, n_dp // 2, step, 0)
 
     k_col, k_smz = recvs.take(), recvs.take()
-    mine_in = pl.ds(pl.multiple_of(dp * p.out_rows, p.out_rows), p.out_rows)
-    mate_half = 1 - z // 2
+    k_pair = recvs.take()
 
     def gathered_row(cond):
         send(cond, r.de_all.at[1 - x], r.de_all.at[1 - x], (core, dp), k_dex + (1 - x))
 
+    units(0)
+    o_tab[...] = jnp.zeros(o_tab.shape, F32)
     attention_tile(3)
-    pair_step(de, k_row, 1, on_0, k_pass)
+    row_step(1, on_0)
     attention_tile(0)
+    units(1)
     db.step(3)
-    db.cross(3)
+    units(2)
+    units(3)
+    exchange_out(always)
+    exchange_col(at_x1)
+    row_step(2, on_0)
+    row_step(3, on_0)
+    exchange_col(at_x0)
     attention_sum(3)
-    pair_step(de, k_row, 2, on_0, k_pass)
+    row_cross(0, on_0)
+    row_cross(1, on_0)
 
     @on(at_x0)
     def _():
         arrived(r.ch_all.at[c, 0 : n_dp - 2], k_ch)
-        send(at_x0, r.ch_all.at[c], r.ch_all.at[c], (across, dp), k_cha)
+        send(is_att, r.ch_all.at[c], r.ch_all.at[c], (across, dp), k_cha)
         send(at_x0, r.ch_all.at[c], r.ch_all.at[c], (core, dp), k_chx)
 
-
-    @on(is_ff)
-    def _():
-        r.u_out[...] = jnp.zeros(r.u_out.shape, F32)
-        r.w_col[...] = jnp.zeros(r.w_col.shape, F32)
-        on(at_x1)(lambda: arrived(r.x_all.at[0, z, y], xs.own))
-        arrived(r.db_all.at[0, z, y], db.own)
-        units_here(z // 2)
-        units_here(mate_half)
 
     attention_tile(1)
     attention_sum(0)
     attention_last(3)
 
-    def row_0(i):
-        @on(on_1)
-        def _():
-            arrived(row(0, i), k_row + i)
-            pair_line(de, k_row, on_1, i)
-
-    row_0(dp)
+    @on(on_1)
+    def _():
+        arrived(de(dp), k_row + dp)
+        row_line(on_1, dp)
+
     on(at_x1)(logits)
-    row_0(ydp)
-    pair_step(de, k_row, 1, on_1, k_pass)
+    row_step(1, on_1)
+    row_step(2, on_1)
     attention_sum(1)
     attention_last(0)
 
     attention_tile(2)
+    attention_sum(2)
     attention_last(1)
-    pair_step(de, k_row, 2, on_1, k_pass)
+    row_cross(0, on_1)
+    row_cross(1, on_1)
 
     gathered(k_sm, to_sm)
     r.sm_tot[...] = r.b_sm[0] + r.b_sm[1] + r.b_sm[2] + r.b_sm[3]
@@ -1415,22 +1406,20 @@
         zz = lax.rem(z + k, nz)
         send(always, r.sm_tot, r.r_sm.at[z], (s, 2 * zz + y), k_smz)
 
-    attention_sum(2)
+
+    row_step(3, on_1)
+    row_cross(2, is_ff)
+    row_cross(3, is_ff)
+    gathered_row(is_ff)
+    send(on_0, r.ch_all.at[c], r.ch_all.at[c], (across, dp), k_cha)
+
+
+    def passed_row():
+        on(is_ff)(lambda: arrived(r.de_all.at[x], k_pass))
+        send(is_ff, r.de_all.at[x], r.de_all.at[x], (core, dp), k_dex + x)
+        on(is_att)(lambda: arrived(r.de_all.at[x], k_dex + x))
+
     attention_last(2)
-
-    @on(is_ff)
-    def _():
-        units_over_y(z // 2)
-
-    pair_step(de, k_row, 3, is_ff, k_pass)
-    gathered_row(is_ff)
-
-    def passed_row(cond):
-        @on(cond)
-        def _():
-            arrived(r.de_all.at[x], k_pass)
-
-        send(cond, r.de_all.at[x], r.de_all.at[x], (core, dp), k_dex + x)
 
     def column_block(k):
         at = k * p.out_rows
@@ -1438,30 +1427,34 @@
 
     @on(is_ff)
     def _():
-        units_over_y(mate_half)
-        o_wout[...] = r.u_out[...].astype(BF)
+        arrived(r.r_in.at[0:2], k_pair)
+        for i in range(p.out_rows // p.in_rows):
+            own = r.u_out[pl.ds(pl.multiple_of(y * p.out_rows + i * p.in_rows, p.in_rows), p.in_rows), :]
+            o_wout[i * p.in_rows : (i + 1) * p.in_rows, :] = (own + out_piece(i)[...].astype(F32)).astype(BF)
         emit(4, o_wout)
-        for k in range(n_dp):
-            column_block(k)[...] = r.w_col[k * p.in_rows : (k + 1) * p.in_rows, :].astype(BF)
+        for i in range(n_dp):
+            own = r.w_col[i * p.in_rows : (i + 1) * p.in_rows, units_mine]
+            column_block(i)[...] = (own + col_piece(i)[...].astype(F32)).astype(BF)
         r.r_col[dp] = column_block(dp)[...]
 
     for k in (4, 5, 3, 2, 6, 1, 7) if n_dp == 8 else range(1, n_dp):
         to = lax.rem(dp + k, n_dp)
         send(is_ff, column_block(to), r.r_col.at[dp], (s, to), k_col)
+
+    on(at_x0)(head_part)
+    on(is_att)(lambda: arrived(r.de_all.at[1 - x], k_dex + 1 - x))
+    arrived(r.ids_all.at[0 : n_dp - 1], k_id)
+    scatter(1 - x)
+
+    passed_row()
+    scatter(x)
+
     @on(at_x1)
     def _():
         arrived(r.ch_all.at[c], k_cha)
         send(at_x1, r.ch_all.at[c], r.ch_all.at[c], (core, dp), k_chx)
-
-    passed_row(is_ff)
-
-
-    head_part()
-
-    on(is_att)(lambda: arrived(r.de_all.at[1 - x], k_dex + 1 - x))
-    scatter(1 - x)
-    on(is_att)(lambda: arrived(r.de_all.at[x], k_dex + x))
-    scatter(x)
+        head_part()
+
     n_pos = ln // n_dp
     here = pl.ds(pl.multiple_of(dp * n_pos, n_pos), n_pos)
     total = jnp.zeros((n_pos, w), F32)

time: 103 us -> 101 us (0.981)
  Pallas kernels: 102 us -> 100 us
    pallas_call x1, Pallas kernels: 98 us -> 96.4 us  [whole(): pl.pallas_call(functools.partial(fused, p, list(scratch)), out_shape=part...]
where the time goes in v7:
time: 101 us
  Pallas kernels  100 us (99%)
    pallas_call x1, Pallas kernels, whole(): pl.pallas_call(functools.partial(fused, p, list(scratch)), out_shape=part...  96.4 us
    pallas_call x1, Pallas kernels, whole(): pl.pallas_call(functools.partial(finish, p), out_shape=[jax.ShapeDtypeStr...  3.55 us

profile of v7, /device:TPU:1, one launch (start us, length us, event | category | flops | bytes accessed | tf_op | source)
XLA Modules:
  0.0 100.8 jit_solution(3720044905389144404)
XLA Ops:
  0.6 96.4 %shard_map.187 = (bf16[2,1,40,3648]{3,2,1,0:T(8,128)(2,1)}, f32[456,768]{1,0:T(8,128)}, f32[16,768]{1,0:T(8,128)}, bf16[1,96,3072]{2,1,0:T(8,128)(2,1)}, bf16[1,384,768]{2,1,0:T(8,128)(2,1)}, /*index=5*/f32[8,768]{1,0:T(8,128)}) custom-call(s32[2,1,128]{2,1,0:T(1,128)} %refs_0_.1, s32[2,1,128]{2,1,0:T(1,128)} %refs_1_.1, s32[2,1,40]{2,1,0:T(1,128)} %refs_2_.1, ...), custom_call_target="tpu_custom_call" | custom-call | tf_op jit(solution)/shard_map/pallas_call | solution.py:1578
  97.1 3.5 %shard_map.188 = (f32[2,1,40,3648]{3,2,1,0:T(8,128)}, f32[456,768]{1,0:T(8,128)}, f32[16,768]{1,0:T(8,128)}, f32[1,96,3072]{2,1,0:T(8,128)}, f32[1,384,768]{2,1,...) custom-call(bf16[2,1,40,3648]{3,2,1,0:T(8,128)(2,1)} %get-tuple-element.15.refs_0_, ...), custom_call_target="tpu_custom_call" | custom-call | tf_op jit(solution)/shard_map/pallas_call | solution.py:1619
